TPU v7x, 32 devices: a whole 2x2x4 slice. The times are simulated.
32 devices in a mesh: groups: 2 (over x), dom: 8 (over z, y), panel: 2 (over core).
Axes of the slice: x: 2, y: 2, z: 4, core: 2. Of those that a mesh axis runs over, the one named last changes fastest.
Arguments:
- panels: float32 [8, 8192], P(None, ('groups', 'panel')), parts along dimension 1, may hold values from -1 to 1
- particles: float32 [6, 131072], P(None, ('groups', 'dom', 'panel')), parts along dimension 1, may hold values from -1 to 1
- counts: int32 [1024], P(('groups', 'dom', 'panel')), parts along dimension 0, may hold values from 1 to 128, as said below
- near: int32 [64, 512], P(('groups', 'panel'), 'dom'), parts along dimension 0, may hold values from 0 to 1, as said below
Outputs:
- normal_velocity: float32 [8192], P(('groups', 'panel')), parts along dimension 0
- particle_velocity: float32 [3, 131072], P(None, ('groups', 'dom', 'panel')), parts along dimension 1
There are 2 independent parts, one for each index of `groups`. A program takes and returns all parts, laid end to end along the dimension named above; each array names one. Nothing has to cross between parts.
Inputs may be any that keep to these rules, and one draw needn't show every extreme that they name: `counts`: at least one block is full in every draw. Every particle block has one to three near panel blocks, adjacent to one another; there is no bound on how many particle blocks one panel block pairs with.
All inputs are finite; a program needn't handle non-finite values.
Results may differ from a plain program's by a relative error of at most 0.0003.
Values sent between devices are 32-bit elements; how exact they have to be, the bound alone decides.
No kernel may reach another device: no remote copies, remote signals or barrier semaphores. Data moves between devices by JAX's collectives and lax.ppermute only.
A program may use at most 64 MiB of HBM per device.

v0:
```python
import jax
import jax.numpy as jnp
from jax import lax
from jax.sharding import PartitionSpec as P

core_sq = 0.04
inv_four_pi = 0.07957747154594767


def tile_terms(panels, pos, alpha, cols, valid, blk):
    npan = panels.shape[1]
    width = pos.shape[1]
    nb = npan // blk
    grp = width // blk
    r0 = panels[0][:, None] - pos[0][None, :]
    r1 = panels[1][:, None] - pos[1][None, :]
    r2 = panels[2][:, None] - pos[2][None, :]
    nx0 = panels[3][:, None]
    nx1 = panels[4][:, None]
    nx2 = panels[5][:, None]
    source = panels[6][:, None]
    doublet = panels[7][:, None]
    inv = lax.rsqrt(r0 * r0 + r1 * r1 + r2 * r2 + core_sq)
    inv3 = inv * inv * inv
    inv5 = inv3 * inv * inv
    masked = alpha * valid[None, :]
    a0 = masked[0][None, :]
    a1 = masked[1][None, :]
    a2 = masked[2][None, :]
    ndot = nx0 * (r1 * a2 - r2 * a1) + nx1 * (r2 * a0 - r0 * a2) + nx2 * (r0 * a1 - r1 * a0)
    block_sums = jnp.sum((ndot * inv3).reshape(npan, grp, blk), axis=2)
    row_weight = jnp.repeat(cols, blk, axis=0)
    panel_part = -inv_four_pi * jnp.sum(block_sums * row_weight, axis=1)
    nr = nx0 * r0 + nx1 * r1 + nx2 * r2
    coef_r = -source * inv3 + 3.0 * doublet * nr * inv5
    coef_n = -doublet * inv3
    weight3 = cols[:, :, None]

    def component(rk, nk):
        term = (coef_r * rk + nk * coef_n).reshape(nb, blk, width)
        summed = jnp.sum(term, axis=1).reshape(nb, grp, blk)
        return jnp.sum(summed * weight3, axis=0).reshape(width)

    vel = inv_four_pi * jnp.stack([component(r0, nx0), component(r1, nx1), component(r2, nx2)])
    return (panel_part, vel)


def local_pairs(panels, particles, counts, near_local):
    blk = 128
    npan = panels.shape[1]
    nblk = counts.shape[0]
    group = 1
    for option in (4, 2):
        if group == 1 and nblk % option == 0 and (npan * option * blk <= 1048576):
            group = option
    steps_count = nblk // group
    width = group * blk
    slabs = particles.reshape(6, steps_count, width).transpose(1, 0, 2)
    count_rows = counts.reshape(steps_count, group)
    near_cols = near_local.T.reshape(steps_count, group, near_local.shape[0])

    def step(total, item):
        slab, count_row, cols = item
        slot = jnp.arange(width, dtype=jnp.int32) % blk
        valid = (slot < jnp.repeat(count_row, blk)).astype(jnp.float32)
        part, vel = tile_terms(panels, slab[0:3], slab[3:6], cols.T.astype(jnp.float32), valid, blk)
        return (total + part, vel)

    total, vels = lax.scan(step, jnp.zeros((npan,), jnp.float32), (slabs, count_rows, near_cols))
    return (total, vels.transpose(1, 0, 2).reshape(3, nblk * blk))


def on_device(panels, particles, counts, near):
    whole, all_counts = (
        lax.all_gather(particles, "panel", axis=1, tiled=True),
        lax.all_gather(counts, "panel", axis=0, tiled=True),
    )
    partial_value, vel = local_pairs(panels, whole, all_counts, near)
    normal_velocity = lax.psum(partial_value, "dom")
    particle_velocity = lax.psum_scatter(vel, "panel", scatter_dimension=1, tiled=True)
    return (normal_velocity, particle_velocity)


def solution(mesh):
    return jax.shard_map(
        on_device,
        mesh=mesh,
        in_specs=(
            P(None, ("groups", "panel")),
            P(None, ("groups", "dom", "panel")),
            P(("groups", "dom", "panel")),
            P(("groups", "panel"), "dom"),
        ),
        out_specs=(P(("groups", "panel")), P(None, ("groups", "dom", "panel"))),
        check_vma=False,
    )
```

profile of v0, /device:TPU:0, one launch (start us, length us, event | category | flops | bytes accessed | tf_op | source)
XLA Modules:
  0.0 255.9 jit_solution(2539459897433163309)
XLA Ops:
  7.2 1.2 dynamic-slice
  10.0 1.9 all-reduce
  13.7 2.2 all_gather.6
  15.9 203.8 %while.15 = (s32[]{:T(128)}, f32[2048]{0:T(1024)S(1)}, f32[16,3,512]{2,1,0:T(4,128)S(1)}, f32[8,2048]{1,0:T(8,128)}, f32[16,6,512]{2,1,0:T(8,128)S(1)}, /*index=...) while((s32[]{:T(128)}, f32[2048]{0:T(1024)S(1)}, ...), condition=%wide.region_9.10_spmd.clone, body=%wide.region_0.9_spmd.clone.sunk | while | flops 65059396 | bytes 679179 | solution.py:69
  17.4 5.0 %fusion.66 = f32[2048,4]{0,1:T(4,128)S(1)} fusion(f32[2048]{0:T(1024)S(1)} %bitcast.163, f32[4,128]{1,0:T(4,128)S(1)} %bitcast.184, f32[2048]{0:T(1024)S(1)} %bitcast.165, f32[4,128]{1,0:T(4,128)S(1)} %bitcast.187, f32[2048]{0:T(1024)S(1)} %bitcast.167, f32[4,128]{1,0:T(4,128)S(1)} %bitcast.188, f32[4,128]{1,0:T(4,128)S(1)} %bitcast.182, ...), kind=kLoop, calls=%fused_computation.25.clone.1 | loop fusion | flops 28303360 | bytes 94208 | tf_op jit(solution)/shard_map/while/body/eval_jaxpr/reduce_sum | solution.py:31
  22.4 6.1 %fusion.68 = (f32[16,512]{1,0:T(8,128)S(1)}, f32[16,512]{1,0:T(8,128)S(1)}, f32[16,512]{1,0:T(8,128)S(1)}) fusion(f32[16,128]{1,0:T(8,128)S(1)} %bitcast.174, f32[512]{0:T(512)S(1)} %bitcast.185, f32[16,128]{1,0:T(8,128)S(1)} %bitcast.166, f32[512]{0:T(512)S(1)} %bitcast.183, f32[16,128]{1,0:T(8,128)S(1)} %bitcast.170, f32[512]{0:T(512)S(1)} %bitcast.181, ...), kind=kLoop, calls=%fused_computation.47.clone.1 | loop fusion | flops 36675584 | bytes 178176 | tf_op jit(solution)/shard_map/while/body/eval_jaxpr/reduce_sum | solution.py:41
  30.1 5.0 %fusion.66 = f32[2048,4]{0,1:T(4,128)S(1)} fusion(f32[2048]{0:T(1024)S(1)} %bitcast.163, f32[4,128]{1,0:T(4,128)S(1)} %bitcast.184, f32[2048]{0:T(1024)S(1)} %bitcast.165, f32[4,128]{1,0:T(4,128)S(1)} %bitcast.187, f32[2048]{0:T(1024)S(1)} %bitcast.167, f32[4,128]{1,0:T(4,128)S(1)} %bitcast.188, f32[4,128]{1,0:T(4,128)S(1)} %bitcast.182, ...), kind=kLoop, calls=%fused_computation.25.clone.1 | loop fusion | flops 28303360 | bytes 94208 | tf_op jit(solution)/shard_map/while/body/eval_jaxpr/reduce_sum | solution.py:31
  35.1 6.1 %fusion.68 = (f32[16,512]{1,0:T(8,128)S(1)}, f32[16,512]{1,0:T(8,128)S(1)}, f32[16,512]{1,0:T(8,128)S(1)}) fusion(f32[16,128]{1,0:T(8,128)S(1)} %bitcast.174, f32[512]{0:T(512)S(1)} %bitcast.185, f32[16,128]{1,0:T(8,128)S(1)} %bitcast.166, f32[512]{0:T(512)S(1)} %bitcast.183, f32[16,128]{1,0:T(8,128)S(1)} %bitcast.170, f32[512]{0:T(512)S(1)} %bitcast.181, ...), kind=kLoop, calls=%fused_computation.47.clone.1 | loop fusion | flops 36675584 | bytes 178176 | tf_op jit(solution)/shard_map/while/body/eval_jaxpr/reduce_sum | solution.py:41
  41.6 1.2 slice_multiply_fusion.2
  42.8 5.0 %fusion.66 = f32[2048,4]{0,1:T(4,128)S(1)} fusion(f32[2048]{0:T(1024)S(1)} %bitcast.163, f32[4,128]{1,0:T(4,128)S(1)} %bitcast.184, f32[2048]{0:T(1024)S(1)} %bitcast.165, f32[4,128]{1,0:T(4,128)S(1)} %bitcast.187, f32[2048]{0:T(1024)S(1)} %bitcast.167, f32[4,128]{1,0:T(4,128)S(1)} %bitcast.188, f32[4,128]{1,0:T(4,128)S(1)} %bitcast.182, ...), kind=kLoop, calls=%fused_computation.25.clone.1 | loop fusion | flops 28303360 | bytes 94208 | tf_op jit(solution)/shard_map/while/body/eval_jaxpr/reduce_sum | solution.py:31
  47.9 6.1 %fusion.68 = (f32[16,512]{1,0:T(8,128)S(1)}, f32[16,512]{1,0:T(8,128)S(1)}, f32[16,512]{1,0:T(8,128)S(1)}) fusion(f32[16,128]{1,0:T(8,128)S(1)} %bitcast.174, f32[512]{0:T(512)S(1)} %bitcast.185, f32[16,128]{1,0:T(8,128)S(1)} %bitcast.166, f32[512]{0:T(512)S(1)} %bitcast.183, f32[16,128]{1,0:T(8,128)S(1)} %bitcast.170, f32[512]{0:T(512)S(1)} %bitcast.181, ...), kind=kLoop, calls=%fused_computation.47.clone.1 | loop fusion | flops 36675584 | bytes 178176 | tf_op jit(solution)/shard_map/while/body/eval_jaxpr/reduce_sum | solution.py:41
  54.4 1.2 slice_multiply_fusion.2
  55.6 5.0 %fusion.66 = f32[2048,4]{0,1:T(4,128)S(1)} fusion(f32[2048]{0:T(1024)S(1)} %bitcast.163, f32[4,128]{1,0:T(4,128)S(1)} %bitcast.184, f32[2048]{0:T(1024)S(1)} %bitcast.165, f32[4,128]{1,0:T(4,128)S(1)} %bitcast.187, f32[2048]{0:T(1024)S(1)} %bitcast.167, f32[4,128]{1,0:T(4,128)S(1)} %bitcast.188, f32[4,128]{1,0:T(4,128)S(1)} %bitcast.182, ...), kind=kLoop, calls=%fused_computation.25.clone.1 | loop fusion | flops 28303360 | bytes 94208 | tf_op jit(solution)/shard_map/while/body/eval_jaxpr/reduce_sum | solution.py:31
  60.6 6.1 %fusion.68 = (f32[16,512]{1,0:T(8,128)S(1)}, f32[16,512]{1,0:T(8,128)S(1)}, f32[16,512]{1,0:T(8,128)S(1)}) fusion(f32[16,128]{1,0:T(8,128)S(1)} %bitcast.174, f32[512]{0:T(512)S(1)} %bitcast.185, f32[16,128]{1,0:T(8,128)S(1)} %bitcast.166, f32[512]{0:T(512)S(1)} %bitcast.183, f32[16,128]{1,0:T(8,128)S(1)} %bitcast.170, f32[512]{0:T(512)S(1)} %bitcast.181, ...), kind=kLoop, calls=%fused_computation.47.clone.1 | loop fusion | flops 36675584 | bytes 178176 | tf_op jit(solution)/shard_map/while/body/eval_jaxpr/reduce_sum | solution.py:41
  67.1 1.2 slice_multiply_fusion.2
  68.3 5.0 %fusion.66 = f32[2048,4]{0,1:T(4,128)S(1)} fusion(f32[2048]{0:T(1024)S(1)} %bitcast.163, f32[4,128]{1,0:T(4,128)S(1)} %bitcast.184, f32[2048]{0:T(1024)S(1)} %bitcast.165, f32[4,128]{1,0:T(4,128)S(1)} %bitcast.187, f32[2048]{0:T(1024)S(1)} %bitcast.167, f32[4,128]{1,0:T(4,128)S(1)} %bitcast.188, f32[4,128]{1,0:T(4,128)S(1)} %bitcast.182, ...), kind=kLoop, calls=%fused_computation.25.clone.1 | loop fusion | flops 28303360 | bytes 94208 | tf_op jit(solution)/shard_map/while/body/eval_jaxpr/reduce_sum | solution.py:31
  73.3 6.1 %fusion.68 = (f32[16,512]{1,0:T(8,128)S(1)}, f32[16,512]{1,0:T(8,128)S(1)}, f32[16,512]{1,0:T(8,128)S(1)}) fusion(f32[16,128]{1,0:T(8,128)S(1)} %bitcast.174, f32[512]{0:T(512)S(1)} %bitcast.185, f32[16,128]{1,0:T(8,128)S(1)} %bitcast.166, f32[512]{0:T(512)S(1)} %bitcast.183, f32[16,128]{1,0:T(8,128)S(1)} %bitcast.170, f32[512]{0:T(512)S(1)} %bitcast.181, ...), kind=kLoop, calls=%fused_computation.47.clone.1 | loop fusion | flops 36675584 | bytes 178176 | tf_op jit(solution)/shard_map/while/body/eval_jaxpr/reduce_sum | solution.py:41
  79.8 1.2 slice_multiply_fusion.2
  81.0 5.0 %fusion.66 = f32[2048,4]{0,1:T(4,128)S(1)} fusion(f32[2048]{0:T(1024)S(1)} %bitcast.163, f32[4,128]{1,0:T(4,128)S(1)} %bitcast.184, f32[2048]{0:T(1024)S(1)} %bitcast.165, f32[4,128]{1,0:T(4,128)S(1)} %bitcast.187, f32[2048]{0:T(1024)S(1)} %bitcast.167, f32[4,128]{1,0:T(4,128)S(1)} %bitcast.188, f32[4,128]{1,0:T(4,128)S(1)} %bitcast.182, ...), kind=kLoop, calls=%fused_computation.25.clone.1 | loop fusion | flops 28303360 | bytes 94208 | tf_op jit(solution)/shard_map/while/body/eval_jaxpr/reduce_sum | solution.py:31
  86.1 6.1 %fusion.68 = (f32[16,512]{1,0:T(8,128)S(1)}, f32[16,512]{1,0:T(8,128)S(1)}, f32[16,512]{1,0:T(8,128)S(1)}) fusion(f32[16,128]{1,0:T(8,128)S(1)} %bitcast.174, f32[512]{0:T(512)S(1)} %bitcast.185, f32[16,128]{1,0:T(8,128)S(1)} %bitcast.166, f32[512]{0:T(512)S(1)} %bitcast.183, f32[16,128]{1,0:T(8,128)S(1)} %bitcast.170, f32[512]{0:T(512)S(1)} %bitcast.181, ...), kind=kLoop, calls=%fused_computation.47.clone.1 | loop fusion | flops 36675584 | bytes 178176 | tf_op jit(solution)/shard_map/while/body/eval_jaxpr/reduce_sum | solution.py:41
  92.6 1.2 slice_multiply_fusion.2
  93.8 5.0 %fusion.66 = f32[2048,4]{0,1:T(4,128)S(1)} fusion(f32[2048]{0:T(1024)S(1)} %bitcast.163, f32[4,128]{1,0:T(4,128)S(1)} %bitcast.184, f32[2048]{0:T(1024)S(1)} %bitcast.165, f32[4,128]{1,0:T(4,128)S(1)} %bitcast.187, f32[2048]{0:T(1024)S(1)} %bitcast.167, f32[4,128]{1,0:T(4,128)S(1)} %bitcast.188, f32[4,128]{1,0:T(4,128)S(1)} %bitcast.182, ...), kind=kLoop, calls=%fused_computation.25.clone.1 | loop fusion | flops 28303360 | bytes 94208 | tf_op jit(solution)/shard_map/while/body/eval_jaxpr/reduce_sum | solution.py:31
  98.8 6.1 %fusion.68 = (f32[16,512]{1,0:T(8,128)S(1)}, f32[16,512]{1,0:T(8,128)S(1)}, f32[16,512]{1,0:T(8,128)S(1)}) fusion(f32[16,128]{1,0:T(8,128)S(1)} %bitcast.174, f32[512]{0:T(512)S(1)} %bitcast.185, f32[16,128]{1,0:T(8,128)S(1)} %bitcast.166, f32[512]{0:T(512)S(1)} %bitcast.183, f32[16,128]{1,0:T(8,128)S(1)} %bitcast.170, f32[512]{0:T(512)S(1)} %bitcast.181, ...), kind=kLoop, calls=%fused_computation.47.clone.1 | loop fusion | flops 36675584 | bytes 178176 | tf_op jit(solution)/shard_map/while/body/eval_jaxpr/reduce_sum | solution.py:41
  105.3 1.2 slice_multiply_fusion.2
  106.5 5.0 %fusion.66 = f32[2048,4]{0,1:T(4,128)S(1)} fusion(f32[2048]{0:T(1024)S(1)} %bitcast.163, f32[4,128]{1,0:T(4,128)S(1)} %bitcast.184, f32[2048]{0:T(1024)S(1)} %bitcast.165, f32[4,128]{1,0:T(4,128)S(1)} %bitcast.187, f32[2048]{0:T(1024)S(1)} %bitcast.167, f32[4,128]{1,0:T(4,128)S(1)} %bitcast.188, f32[4,128]{1,0:T(4,128)S(1)} %bitcast.182, ...), kind=kLoop, calls=%fused_computation.25.clone.1 | loop fusion | flops 28303360 | bytes 94208 | tf_op jit(solution)/shard_map/while/body/eval_jaxpr/reduce_sum | solution.py:31
  111.5 6.1 %fusion.68 = (f32[16,512]{1,0:T(8,128)S(1)}, f32[16,512]{1,0:T(8,128)S(1)}, f32[16,512]{1,0:T(8,128)S(1)}) fusion(f32[16,128]{1,0:T(8,128)S(1)} %bitcast.174, f32[512]{0:T(512)S(1)} %bitcast.185, f32[16,128]{1,0:T(8,128)S(1)} %bitcast.166, f32[512]{0:T(512)S(1)} %bitcast.183, f32[16,128]{1,0:T(8,128)S(1)} %bitcast.170, f32[512]{0:T(512)S(1)} %bitcast.181, ...), kind=kLoop, calls=%fused_computation.47.clone.1 | loop fusion | flops 36675584 | bytes 178176 | tf_op jit(solution)/shard_map/while/body/eval_jaxpr/reduce_sum | solution.py:41
  118.0 1.2 slice_multiply_fusion.2
  119.2 5.0 %fusion.66 = f32[2048,4]{0,1:T(4,128)S(1)} fusion(f32[2048]{0:T(1024)S(1)} %bitcast.163, f32[4,128]{1,0:T(4,128)S(1)} %bitcast.184, f32[2048]{0:T(1024)S(1)} %bitcast.165, f32[4,128]{1,0:T(4,128)S(1)} %bitcast.187, f32[2048]{0:T(1024)S(1)} %bitcast.167, f32[4,128]{1,0:T(4,128)S(1)} %bitcast.188, f32[4,128]{1,0:T(4,128)S(1)} %bitcast.182, ...), kind=kLoop, calls=%fused_computation.25.clone.1 | loop fusion | flops 28303360 | bytes 94208 | tf_op jit(solution)/shard_map/while/body/eval_jaxpr/reduce_sum | solution.py:31
  124.3 6.1 %fusion.68 = (f32[16,512]{1,0:T(8,128)S(1)}, f32[16,512]{1,0:T(8,128)S(1)}, f32[16,512]{1,0:T(8,128)S(1)}) fusion(f32[16,128]{1,0:T(8,128)S(1)} %bitcast.174, f32[512]{0:T(512)S(1)} %bitcast.185, f32[16,128]{1,0:T(8,128)S(1)} %bitcast.166, f32[512]{0:T(512)S(1)} %bitcast.183, f32[16,128]{1,0:T(8,128)S(1)} %bitcast.170, f32[512]{0:T(512)S(1)} %bitcast.181, ...), kind=kLoop, calls=%fused_computation.47.clone.1 | loop fusion | flops 36675584 | bytes 178176 | tf_op jit(solution)/shard_map/while/body/eval_jaxpr/reduce_sum | solution.py:41
  132.0 5.0 %fusion.66 = f32[2048,4]{0,1:T(4,128)S(1)} fusion(f32[2048]{0:T(1024)S(1)} %bitcast.163, f32[4,128]{1,0:T(4,128)S(1)} %bitcast.184, f32[2048]{0:T(1024)S(1)} %bitcast.165, f32[4,128]{1,0:T(4,128)S(1)} %bitcast.187, f32[2048]{0:T(1024)S(1)} %bitcast.167, f32[4,128]{1,0:T(4,128)S(1)} %bitcast.188, f32[4,128]{1,0:T(4,128)S(1)} %bitcast.182, ...), kind=kLoop, calls=%fused_computation.25.clone.1 | loop fusion | flops 28303360 | bytes 94208 | tf_op jit(solution)/shard_map/while/body/eval_jaxpr/reduce_sum | solution.py:31
  137.0 6.1 %fusion.68 = (f32[16,512]{1,0:T(8,128)S(1)}, f32[16,512]{1,0:T(8,128)S(1)}, f32[16,512]{1,0:T(8,128)S(1)}) fusion(f32[16,128]{1,0:T(8,128)S(1)} %bitcast.174, f32[512]{0:T(512)S(1)} %bitcast.185, f32[16,128]{1,0:T(8,128)S(1)} %bitcast.166, f32[512]{0:T(512)S(1)} %bitcast.183, f32[16,128]{1,0:T(8,128)S(1)} %bitcast.170, f32[512]{0:T(512)S(1)} %bitcast.181, ...), kind=kLoop, calls=%fused_computation.47.clone.1 | loop fusion | flops 36675584 | bytes 178176 | tf_op jit(solution)/shard_map/while/body/eval_jaxpr/reduce_sum | solution.py:41
  144.7 5.0 %fusion.66 = f32[2048,4]{0,1:T(4,128)S(1)} fusion(f32[2048]{0:T(1024)S(1)} %bitcast.163, f32[4,128]{1,0:T(4,128)S(1)} %bitcast.184, f32[2048]{0:T(1024)S(1)} %bitcast.165, f32[4,128]{1,0:T(4,128)S(1)} %bitcast.187, f32[2048]{0:T(1024)S(1)} %bitcast.167, f32[4,128]{1,0:T(4,128)S(1)} %bitcast.188, f32[4,128]{1,0:T(4,128)S(1)} %bitcast.182, ...), kind=kLoop, calls=%fused_computation.25.clone.1 | loop fusion | flops 28303360 | bytes 94208 | tf_op jit(solution)/shard_map/while/body/eval_jaxpr/reduce_sum | solution.py:31
  149.7 6.1 %fusion.68 = (f32[16,512]{1,0:T(8,128)S(1)}, f32[16,512]{1,0:T(8,128)S(1)}, f32[16,512]{1,0:T(8,128)S(1)}) fusion(f32[16,128]{1,0:T(8,128)S(1)} %bitcast.174, f32[512]{0:T(512)S(1)} %bitcast.185, f32[16,128]{1,0:T(8,128)S(1)} %bitcast.166, f32[512]{0:T(512)S(1)} %bitcast.183, f32[16,128]{1,0:T(8,128)S(1)} %bitcast.170, f32[512]{0:T(512)S(1)} %bitcast.181, ...), kind=kLoop, calls=%fused_computation.47.clone.1 | loop fusion | flops 36675584 | bytes 178176 | tf_op jit(solution)/shard_map/while/body/eval_jaxpr/reduce_sum | solution.py:41
  156.2 1.2 slice_multiply_fusion.2
  157.5 5.0 %fusion.66 = f32[2048,4]{0,1:T(4,128)S(1)} fusion(f32[2048]{0:T(1024)S(1)} %bitcast.163, f32[4,128]{1,0:T(4,128)S(1)} %bitcast.184, f32[2048]{0:T(1024)S(1)} %bitcast.165, f32[4,128]{1,0:T(4,128)S(1)} %bitcast.187, f32[2048]{0:T(1024)S(1)} %bitcast.167, f32[4,128]{1,0:T(4,128)S(1)} %bitcast.188, f32[4,128]{1,0:T(4,128)S(1)} %bitcast.182, ...), kind=kLoop, calls=%fused_computation.25.clone.1 | loop fusion | flops 28303360 | bytes 94208 | tf_op jit(solution)/shard_map/while/body/eval_jaxpr/reduce_sum | solution.py:31
  162.5 6.1 %fusion.68 = (f32[16,512]{1,0:T(8,128)S(1)}, f32[16,512]{1,0:T(8,128)S(1)}, f32[16,512]{1,0:T(8,128)S(1)}) fusion(f32[16,128]{1,0:T(8,128)S(1)} %bitcast.174, f32[512]{0:T(512)S(1)} %bitcast.185, f32[16,128]{1,0:T(8,128)S(1)} %bitcast.166, f32[512]{0:T(512)S(1)} %bitcast.183, f32[16,128]{1,0:T(8,128)S(1)} %bitcast.170, f32[512]{0:T(512)S(1)} %bitcast.181, ...), kind=kLoop, calls=%fused_computation.47.clone.1 | loop fusion | flops 36675584 | bytes 178176 | tf_op jit(solution)/shard_map/while/body/eval_jaxpr/reduce_sum | solution.py:41
  169.0 1.2 slice_multiply_fusion.2
  170.2 5.0 %fusion.66 = f32[2048,4]{0,1:T(4,128)S(1)} fusion(f32[2048]{0:T(1024)S(1)} %bitcast.163, f32[4,128]{1,0:T(4,128)S(1)} %bitcast.184, f32[2048]{0:T(1024)S(1)} %bitcast.165, f32[4,128]{1,0:T(4,128)S(1)} %bitcast.187, f32[2048]{0:T(1024)S(1)} %bitcast.167, f32[4,128]{1,0:T(4,128)S(1)} %bitcast.188, f32[4,128]{1,0:T(4,128)S(1)} %bitcast.182, ...), kind=kLoop, calls=%fused_computation.25.clone.1 | loop fusion | flops 28303360 | bytes 94208 | tf_op jit(solution)/shard_map/while/body/eval_jaxpr/reduce_sum | solution.py:31
  175.2 6.1 %fusion.68 = (f32[16,512]{1,0:T(8,128)S(1)}, f32[16,512]{1,0:T(8,128)S(1)}, f32[16,512]{1,0:T(8,128)S(1)}) fusion(f32[16,128]{1,0:T(8,128)S(1)} %bitcast.174, f32[512]{0:T(512)S(1)} %bitcast.185, f32[16,128]{1,0:T(8,128)S(1)} %bitcast.166, f32[512]{0:T(512)S(1)} %bitcast.183, f32[16,128]{1,0:T(8,128)S(1)} %bitcast.170, f32[512]{0:T(512)S(1)} %bitcast.181, ...), kind=kLoop, calls=%fused_computation.47.clone.1 | loop fusion | flops 36675584 | bytes 178176 | tf_op jit(solution)/shard_map/while/body/eval_jaxpr/reduce_sum | solution.py:41
  182.9 5.0 %fusion.66 = f32[2048,4]{0,1:T(4,128)S(1)} fusion(f32[2048]{0:T(1024)S(1)} %bitcast.163, f32[4,128]{1,0:T(4,128)S(1)} %bitcast.184, f32[2048]{0:T(1024)S(1)} %bitcast.165, f32[4,128]{1,0:T(4,128)S(1)} %bitcast.187, f32[2048]{0:T(1024)S(1)} %bitcast.167, f32[4,128]{1,0:T(4,128)S(1)} %bitcast.188, f32[4,128]{1,0:T(4,128)S(1)} %bitcast.182, ...), kind=kLoop, calls=%fused_computation.25.clone.1 | loop fusion | flops 28303360 | bytes 94208 | tf_op jit(solution)/shard_map/while/body/eval_jaxpr/reduce_sum | solution.py:31
  188.0 6.1 %fusion.68 = (f32[16,512]{1,0:T(8,128)S(1)}, f32[16,512]{1,0:T(8,128)S(1)}, f32[16,512]{1,0:T(8,128)S(1)}) fusion(f32[16,128]{1,0:T(8,128)S(1)} %bitcast.174, f32[512]{0:T(512)S(1)} %bitcast.185, f32[16,128]{1,0:T(8,128)S(1)} %bitcast.166, f32[512]{0:T(512)S(1)} %bitcast.183, f32[16,128]{1,0:T(8,128)S(1)} %bitcast.170, f32[512]{0:T(512)S(1)} %bitcast.181, ...), kind=kLoop, calls=%fused_computation.47.clone.1 | loop fusion | flops 36675584 | bytes 178176 | tf_op jit(solution)/shard_map/while/body/eval_jaxpr/reduce_sum | solution.py:41
  195.7 5.0 %fusion.66 = f32[2048,4]{0,1:T(4,128)S(1)} fusion(f32[2048]{0:T(1024)S(1)} %bitcast.163, f32[4,128]{1,0:T(4,128)S(1)} %bitcast.184, f32[2048]{0:T(1024)S(1)} %bitcast.165, f32[4,128]{1,0:T(4,128)S(1)} %bitcast.187, f32[2048]{0:T(1024)S(1)} %bitcast.167, f32[4,128]{1,0:T(4,128)S(1)} %bitcast.188, f32[4,128]{1,0:T(4,128)S(1)} %bitcast.182, ...), kind=kLoop, calls=%fused_computation.25.clone.1 | loop fusion | flops 28303360 | bytes 94208 | tf_op jit(solution)/shard_map/while/body/eval_jaxpr/reduce_sum | solution.py:31
  200.7 6.1 %fusion.68 = (f32[16,512]{1,0:T(8,128)S(1)}, f32[16,512]{1,0:T(8,128)S(1)}, f32[16,512]{1,0:T(8,128)S(1)}) fusion(f32[16,128]{1,0:T(8,128)S(1)} %bitcast.174, f32[512]{0:T(512)S(1)} %bitcast.185, f32[16,128]{1,0:T(8,128)S(1)} %bitcast.166, f32[512]{0:T(512)S(1)} %bitcast.183, f32[16,128]{1,0:T(8,128)S(1)} %bitcast.170, f32[512]{0:T(512)S(1)} %bitcast.181, ...), kind=kLoop, calls=%fused_computation.47.clone.1 | loop fusion | flops 36675584 | bytes 178176 | tf_op jit(solution)/shard_map/while/body/eval_jaxpr/reduce_sum | solution.py:41
  208.4 5.0 %fusion.66 = f32[2048,4]{0,1:T(4,128)S(1)} fusion(f32[2048]{0:T(1024)S(1)} %bitcast.163, f32[4,128]{1,0:T(4,128)S(1)} %bitcast.184, f32[2048]{0:T(1024)S(1)} %bitcast.165, f32[4,128]{1,0:T(4,128)S(1)} %bitcast.187, f32[2048]{0:T(1024)S(1)} %bitcast.167, f32[4,128]{1,0:T(4,128)S(1)} %bitcast.188, f32[4,128]{1,0:T(4,128)S(1)} %bitcast.182, ...), kind=kLoop, calls=%fused_computation.25.clone.1 | loop fusion | flops 28303360 | bytes 94208 | tf_op jit(solution)/shard_map/while/body/eval_jaxpr/reduce_sum | solution.py:31
  213.4 6.1 %fusion.68 = (f32[16,512]{1,0:T(8,128)S(1)}, f32[16,512]{1,0:T(8,128)S(1)}, f32[16,512]{1,0:T(8,128)S(1)}) fusion(f32[16,128]{1,0:T(8,128)S(1)} %bitcast.174, f32[512]{0:T(512)S(1)} %bitcast.185, f32[16,128]{1,0:T(8,128)S(1)} %bitcast.166, f32[512]{0:T(512)S(1)} %bitcast.183, f32[16,128]{1,0:T(8,128)S(1)} %bitcast.170, f32[512]{0:T(512)S(1)} %bitcast.181, ...), kind=kLoop, calls=%fused_computation.47.clone.1 | loop fusion | flops 36675584 | bytes 178176 | tf_op jit(solution)/shard_map/while/body/eval_jaxpr/reduce_sum | solution.py:41
  219.7 2.6 %copy.23 = f32[3,8192]{0,1:T(8,128)} copy(f32[3,8192]{1,0:T(4,128)S(1)} %bitcast.178) | data formatting | bytes 196608
  222.4 23.8 %psum.7 = f32[2048]{0:T(1024)} all-reduce(f32[2048]{0:T(1024)S(1)} %get-tuple-element.104), channel_id=1, replica_groups=mesh['groups'=2,'dom'=8,'panel'=2] {'dom'}, use_global_device_ids=true, to_apply=%region_10.11 | all-reduce | flops 2048 | bytes 16384 | tf_op jit(solution)/shard_map/psum | solution.py:79
  246.2 2.8 %copy.24 = f32[3,4096]{1,0:T(4,128)} copy(f32[3,4096]{0,1:T(8,128)} %bitcast.160) | data formatting | bytes 98304
  (193 shorter events, 16.8 us)
Async XLA Ops:
  7.2 239.0 %reduce-scatter.4.cloned.1.call-start = ((), (), s32[]{:S(2)}) async-start(), calls=%async_computation.1 | async-start | bytes 6291456
Sparse Core Ops, SparseCore 0:
  222.5 14.6 reduce-scatter.3
where the time goes:
time: 257 us; the launch traced here: 256 us
  other arithmetic  202 us (79%)
  blocking collectives  28 us (11%)
  between operations  14.7 us (6%)
  local copies, waits for them, and re-layouts  10 us (4%)
    reduce_sum x16, other arithmetic, component(): summed = jnp.sum(term, axis=1).reshape(nb, grp, blk)  98.1 us
    reduce_sum x16, other arithmetic, tile_terms(): block_sums = jnp.sum((ndot * inv3).reshape(npan, grp, blk), axis=2)  79.5 us
    psum x1, blocking collectives, on_device(): normal_velocity = lax.psum(partial_value, 'dom')  23.8 us
    mul x16, other arithmetic, tile_terms(): coef_r = -source * inv3 + 3.0 * doublet * nr * inv5  19.3 us
    unnamed x5, local copies, waits for them, and re-layouts  7.56 us
  transfers between devices with their start and end apart: 1, of which 0 were waited for; matrix products, arithmetic and copies ran while one was open for 0% of the time, Pallas kernels for 0%

commit v1 on v0

v1 whole, which is shorter than its diff:
```python
import functools

import jax
import jax.numpy as jnp
from jax import lax
from jax.experimental import pallas as pl
from jax.experimental.pallas import tpu as pltpu
from jax.sharding import PartitionSpec as P

core_sq = 0.04
inv_four_pi = 0.07957747154594767
BLK = 128
WIN = 3
bf16 = jnp.bfloat16
f32 = jnp.float32


def split2(v):
    hi = v.astype(bf16)
    lo = (v - hi.astype(f32)).astype(bf16)
    return hi, lo


def split3(v):
    a = v.astype(bf16).astype(f32)
    rest = v - a
    b = rest.astype(bf16).astype(f32)
    return a, b, rest - b


def up(v, k):
    return pltpu.roll(v, (8 - k) % 8, 0)


def rows8(width):
    return lax.broadcasted_iota(jnp.int32, (8, width), 0)


def particle_features(particles, counts, ut, fe, org, tile):
    nblk = particles.shape[1] // BLK
    row = rows8(BLK)
    lane = lax.broadcasted_iota(jnp.int32, (8, BLK), 1)

    def one(q, carry):
        at = pl.ds(pl.multiple_of(q * BLK, BLK), BLK)
        t = tile.at[q % 2]
        t[0:6, :] = particles[:, at]
        p = jnp.where(row < 6, t[...], 0.0)
        x = jnp.where(row < 3, p, 0.0)
        a = jnp.where(row < 3, up(p, 3), 0.0)
        xx = jnp.sum(x * x, axis=0, keepdims=True) + core_sq
        feat = jnp.where(row < 3, x, jnp.where(row < 6, 1.0, jnp.where(row == 6, xx, 0.0)))
        x1, x2, x3 = split3(feat)
        u = jnp.concatenate([x1, x1, x2, x2, x1, x3], axis=0)
        ut[pl.ds(pl.multiple_of(q * BLK, BLK), BLK), :] = u.T.astype(bf16)
        o = jnp.broadcast_to(x[:, 0:1], (8, BLK))
        d = x - o

        def rot1(v):
            return jnp.where(row < 2, up(v, 1), jnp.where(row == 2, up(v, 6), 0.0))

        def rot2(v):
            return jnp.where(row < 1, up(v, 2), jnp.where(row < 3, up(v, 7), 0.0))

        cross = rot1(d) * rot2(a) - rot2(d) * rot1(a)
        f = jnp.where(row < 3, a, up(cross, 5))
        f = jnp.where((row < 6) & (lane < counts[q]), f, 0.0)
        f1 = f.astype(bf16).astype(f32)
        f16 = jnp.concatenate([f1, f - f1], axis=0).astype(bf16)
        fe[pl.ds(pl.multiple_of(q * 16, 16), 16), :] = jnp.concatenate([f16, f16], axis=1)
        org[pl.ds(pl.multiple_of(q * 24, 8), 8), :] = o
        org[pl.ds(pl.multiple_of(q * 24 + 8, 8), 8), :] = rot1(o)
        org[pl.ds(pl.multiple_of(q * 24 + 16, 8), 8), :] = rot2(o)
        return carry

    lax.fori_loop(0, nblk, one, 0, unroll=4)


def spans(mine, other, me, box, table, sem):
    half, cols = mine.shape
    row = lax.broadcasted_iota(jnp.int32, (half, cols), 0)
    big = jnp.int32(2 * half)
    a, b = mine[...], other[...]
    first = jnp.minimum(
        jnp.min(jnp.where(a > 0, row + me * half, big), axis=0, keepdims=True),
        jnp.min(jnp.where(b > 0, row + (1 - me) * half, big), axis=0, keepdims=True),
    )
    number = jnp.sum(a, axis=0, keepdims=True) + jnp.sum(b, axis=0, keepdims=True)
    pad = jnp.zeros((1, BLK - cols), jnp.int32) if cols < BLK else None
    if pad is not None:
        first = jnp.concatenate([first, pad], axis=1)
        number = jnp.concatenate([number, pad], axis=1)
    wide = first.shape[1]
    rowb = rows8(wide)
    box[...] = jnp.where(rowb == 0, first, jnp.where(rowb == 1, number, 0))
    return pltpu.make_async_copy(box, table, sem)


def stack6(v, c1, c2, c3, at):
    pair = jnp.concatenate([c1, c2], axis=0).astype(bf16)
    v[0:16, at] = pair
    v[16:32, at] = pair
    v[32:48, at] = jnp.concatenate([c3, c1], axis=0).astype(bf16)


def distance_rows(p, row):
    c = jnp.where(row < 3, p, 0.0)
    return jnp.where(row < 3, -2.0 * c, jnp.where(row < 6, up(c * c, 5), jnp.where(row == 6, 1.0, 0.0)))


def each_panel_chunk(panels, others, me, chunk, body):
    half = panels.shape[1]

    def run(ref, start):
        def one(k, carry):
            src = pl.ds(pl.multiple_of(k * chunk, chunk), chunk)
            dst = pl.ds(pl.multiple_of(start + k * chunk, chunk), chunk)
            body(ref[:, src], dst)
            return carry

        lax.fori_loop(0, half // chunk, one, 0, unroll=2)

    run(panels, me * half)
    run(others, (1 - me) * half)
    body(jnp.zeros((8, chunk), f32), pl.ds(2 * half, chunk))


def panel_sums(panels, others, near, near_o, ut, fe, org, out, v, n1, n2, c1, c2, tot, box, table, sem):
    me = lax.axis_index("panel")
    nblk = ut.shape[0] // BLK
    npan = 2 * panels.shape[1]
    copy = spans(near, near_o, me, box, table, sem)
    copy.start()
    chunk = 2 * BLK
    row = rows8(chunk)

    def build(p, at):
        stack6(v, *split3(distance_rows(p, row)), at)
        n1[:, at] = jnp.where(row < 2, up(p, 4), jnp.where(row == 2, up(p, 1), jnp.where(row < 6, -p, 0.0)))
        n2[:, at] = jnp.where(row < 1, up(p, 5), jnp.where(row < 3, up(p, 2), 0.0))
        c1[:, at] = jnp.where(row < 2, up(p, 1), jnp.where(row == 2, up(p, 6), 0.0))
        c2[:, at] = jnp.where(row < 1, up(p, 2), jnp.where(row < 3, up(p, 7), 1.0))
        tot[:, at] = jnp.zeros((8, chunk), f32)

    each_panel_chunk(panels, others, me, chunk, build)
    copy.wait()

    def one(q, carry):
        first = table[0, me * nblk + q]
        number = table[1, me * nblk + q]
        base = pl.multiple_of(first * BLK, BLK)
        at = pl.ds(base, WIN * BLK)
        r2 = jnp.dot(ut[pl.ds(pl.multiple_of(q * BLK, BLK), BLK), :], v[:, at], preferred_element_type=f32)
        inv = lax.rsqrt(r2)
        hi, lo = split2(inv * inv * inv)
        g = jnp.dot(
            fe[pl.ds(pl.multiple_of(q * 16, 16), 16), :],
            jnp.concatenate([hi, lo], axis=0),
            preferred_element_type=f32,
        )
        g = g[0:8] + g[8:16]
        o1 = org[pl.ds(pl.multiple_of(q * 24 + 8, 8), 8), :]
        o2 = org[pl.ds(pl.multiple_of(q * 24 + 16, 8), 8), :]
        for k in range(WIN):
            here = pl.ds(pl.multiple_of(base + k * BLK, BLK), BLK)
            m = n1[:, here] * (c2[:, here] - o2) - n2[:, here] * (c1[:, here] - o1)
            add = g[:, k * BLK : (k + 1) * BLK] * m
            tot[:, here] += jnp.where(k < number, add, 0.0)
        return carry

    lax.fori_loop(0, nblk, one, 0, unroll=4)
    out[...] = -inv_four_pi * jnp.sum(tot[:, 0:npan], axis=0, keepdims=True)


def particle_sums(particles, panels, others, near, near_o, ut, org, out, v, vn, d0, sb, mn, tile, box, table, sem):
    me = lax.axis_index("panel")
    nblk = ut.shape[0] // BLK
    copy = spans(near, near_o, me, box, table, sem)
    copy.start()
    chunk = 2 * BLK
    row = rows8(chunk)

    def build(p, at):
        stack6(v, *split3(distance_rows(p, row)), at)
        n = up(p, 3)
        m = jnp.broadcast_to(p[7:8, :], p.shape)
        mn3 = jnp.where(row < 3, n * m, 0.0)
        c = jnp.where(row < 3, p, 0.0)
        stack6(vn, *split3(jnp.where(row < 3, -3.0 * mn3, up(3.0 * mn3 * c, 5))), at)
        d0[:, at] = jnp.where(row < 3, p, jnp.where(row == 3, 1.0, 0.0))
        sb[:, at] = jnp.broadcast_to(p[6:7, :], p.shape)
        mn[:, at] = mn3

    each_panel_chunk(panels, others, me, chunk, build)
    copy.wait()
    dims = (((1,), (1,)), ((), ()))

    def one(q, carry):
        first = table[0, me * nblk + q]
        number = table[1, me * nblk + q]
        at = pl.ds(pl.multiple_of(first * BLK, BLK), WIN * BLK)
        mine = pl.ds(pl.multiple_of(q * BLK, BLK), BLK)
        u = ut[mine, :]
        r2 = jnp.dot(u, v[:, at], preferred_element_type=f32)
        nr = jnp.dot(u, vn[:, at], preferred_element_type=f32)
        inv = lax.rsqrt(r2)
        inv2 = inv * inv
        inv3 = inv2 * inv
        term = inv3 * (inv2 * nr)
        o = org[pl.ds(pl.multiple_of(q * 24, 8), 8), :]
        wide = jnp.concatenate([o] * WIN, axis=1)
        lane = lax.broadcasted_iota(jnp.int32, (8, WIN * BLK), 1)
        live = lane < number * BLK
        d = jnp.where(live, d0[:, at] - wide, 0.0)
        e = jnp.where(live, -sb[:, at] * d - mn[:, at], 0.0)

        def rows16(w):
            w1 = w.astype(bf16).astype(f32)
            return jnp.concatenate([w1, w - w1], axis=0).astype(bf16)

        d16, e16 = rows16(d), rows16(e)
        t1, t2 = split2(term)
        i1, i2 = split2(inv3)
        h = (
            lax.dot_general(d16, t1, dims, preferred_element_type=f32)
            + lax.dot_general(d16, t2, dims, preferred_element_type=f32)
            + lax.dot_general(e16, i1, dims, preferred_element_type=f32)
            + lax.dot_general(e16, i2, dims, preferred_element_type=f32)
        )
        h = h[0:8] + h[8:16]
        x = particles[0:3, mine] - o[0:3]
        out[:, mine] = inv_four_pi * (h[0:3] - x * h[3:4])
        return carry

    lax.fori_loop(0, nblk, one, 0, unroll=2)


def vmem():
    return pl.BlockSpec(memory_space=pltpu.VMEM)


def smem():
    return pl.BlockSpec(memory_space=pltpu.SMEM)


def params():
    return pltpu.CompilerParams(vmem_limit_bytes=24 * 1024 * 1024)


def prepare(particles, counts):
    width = particles.shape[1]
    nblk = width // BLK
    return pl.pallas_call(
        particle_features,
        out_shape=(
            jax.ShapeDtypeStruct((width, 48), bf16),
            jax.ShapeDtypeStruct((nblk * 16, 2 * BLK), bf16),
            jax.ShapeDtypeStruct((nblk * 24, BLK), f32),
        ),
        in_specs=[vmem(), smem()],
        out_specs=(vmem(), vmem(), vmem()),
        scratch_shapes=[pltpu.VMEM((2, 8, BLK), f32)],
        compiler_params=params(),
        name="prepare",
    )(particles, counts)


def table_scratch(cols):
    wide = max(cols, BLK)
    return [pltpu.VMEM((8, wide), jnp.int32), pltpu.SMEM((8, wide), jnp.int32), pltpu.SemaphoreType.DMA]


def panel_side(panels, others, near, near_o, ut, fe, org):
    npan = 2 * panels.shape[1]
    full = npan + 2 * BLK
    return pl.pallas_call(
        panel_sums,
        out_shape=jax.ShapeDtypeStruct((1, npan), f32),
        in_specs=[vmem()] * 7,
        out_specs=vmem(),
        scratch_shapes=[pltpu.VMEM((48, full), bf16)]
        + [pltpu.VMEM((8, full), f32)] * 5
        + table_scratch(near.shape[1]),
        compiler_params=params(),
        name="panel_side",
    )(panels, others, near, near_o, ut, fe, org)


def particle_side(particles, panels, others, near, near_o, ut, org):
    npan = 2 * panels.shape[1]
    full = npan + 2 * BLK
    return pl.pallas_call(
        particle_sums,
        out_shape=jax.ShapeDtypeStruct((3, particles.shape[1]), f32),
        in_specs=[vmem()] * 7,
        out_specs=vmem(),
        scratch_shapes=[pltpu.VMEM((48, full), bf16)] * 2
        + [pltpu.VMEM((8, full), f32)] * 3
        + [pltpu.VMEM((8, BLK), f32)]
        + table_scratch(near.shape[1]),
        compiler_params=params(),
        name="particle_side",
    )(particles, panels, others, near, near_o, ut, org)


def on_device(dom, panels, particles, counts, near):
    swap = [(0, 1), (1, 0)]
    others = lax.ppermute(panels, "panel", swap)
    near_o = lax.ppermute(near, "panel", swap)
    ut, fe, org = prepare(particles, counts)
    total = panel_side(panels, others, near, near_o, ut, fe, org)
    velocity = particle_side(particles, panels, others, near, near_o, ut, org)
    total = total.reshape(total.shape[1])
    step = 1
    while step < dom:
        pairs = [(2 * i + c, 2 * (i ^ step) + 1 - c) for i in range(dom) for c in range(2)]
        total = total + lax.ppermute(total, ("dom", "panel"), pairs)
        step *= 2
    half = total.shape[0] // 2
    me = lax.axis_index("panel")
    keep = lax.dynamic_slice(total, (me * half,), (half,))
    give = lax.dynamic_slice(total, ((1 - me) * half,), (half,))
    return keep + lax.ppermute(give, "panel", swap), velocity


def solution(mesh):
    return jax.shard_map(
        functools.partial(on_device, mesh.shape["dom"]),
        mesh=mesh,
        in_specs=(
            P(None, ("groups", "panel")),
            P(None, ("groups", "dom", "panel")),
            P(("groups", "dom", "panel")),
            P(("groups", "panel"), "dom"),
        ),
        out_specs=(P(("groups", "panel")), P(None, ("groups", "dom", "panel"))),
        check_vma=False,
    )
```

time: 257 us -> 41.2 us (0.16)
  other arithmetic: 202 us -> 0.62 us
  blocking collectives: 28 us -> 0 us
  Pallas kernels: 0 us -> 25.6 us
  between operations: 14.7 us -> 0.71 us
  local copies, waits for them, and re-layouts: 10 us -> 1.58 us
  starting transfers between devices: 0.04 us -> 8.23 us
  waiting for transfers between devices: 0.02 us -> 4.34 us
    reduce_sum x64 -> x0, other arithmetic: 180 us -> none  [the longest x16 98.1 us: component(): summed = jnp.sum(term, axis=1).reshape(nb, grp, blk)]
    pallas_call x0 -> x3, Pallas kernels: none -> 25.6 us  [the longest x1 16.5 us: particle_side(): pl.pallas_call(particle_sums, out_shape=jax.ShapeDtypeStruct((3, particle...]
    psum x1 -> x0, blocking collectives: 23.8 us -> none  [on_device(): normal_velocity = lax.psum(partial_value, 'dom')]
    mul x32 -> x0, other arithmetic: 19.5 us -> none  [the longest x16 19.3 us: tile_terms(): coef_r = -source * inv3 + 3.0 * doublet * nr * inv5]
    ppermute x0 -> x6, starting transfers between devices: none -> 8.23 us  [the longest x3 7.26 us: on_device(): total = total + lax.ppermute(total, ('dom', 'panel'), pairs)]
    unnamed x5 -> x10, local copies, waits for them, and re-layouts: 7.56 us -> 1.57 us
    ppermute x0 -> x6, waiting for transfers between devices: none -> 4.34 us  [the longest x3 4.33 us: on_device(): total = total + lax.ppermute(total, ('dom', 'panel'), pairs)]
  transfers between devices with their start and end apart: 1 -> 6, of which waited for: 0 -> 3; matrix products, arithmetic and copies ran while one was open for 0% -> 0% of each run, Pallas kernels for 0% -> 45%
where the time goes in v1:
time: 41.2 us; the launch traced here: 41.1 us
  Pallas kernels  25.6 us (62%)
  starting transfers between devices  8.23 us (20%)
  waiting for transfers between devices  4.34 us (11%)
  local copies, waits for them, and re-layouts  1.58 us (4%)
  between operations  0.71 us (2%)
  other arithmetic  0.62 us (2%)
    pallas_call x1, Pallas kernels, particle_side(): pl.pallas_call(particle_sums, out_shape=jax.ShapeDtypeStruct((3, particle...  16.5 us
    ppermute x3, starting transfers between devices, on_device(): total = total + lax.ppermute(total, ('dom', 'panel'), pairs)  7.26 us
    pallas_call x1, Pallas kernels, panel_side(): pl.pallas_call(panel_sums, out_shape=jax.ShapeDtypeStruct((1, npan), f32)...  7.16 us
    ppermute x3, waiting for transfers between devices, on_device(): total = total + lax.ppermute(total, ('dom', 'panel'), pairs)  4.33 us
    pallas_call x1, Pallas kernels, prepare(): pl.pallas_call(particle_features, out_shape=(jax.ShapeDtypeStruct((width,...  1.92 us
    unnamed x10, local copies, waits for them, and re-layouts  1.57 us
  transfers between devices with their start and end apart: 6, of which 3 were waited for; matrix products, arithmetic and copies ran while one was open for 0% of the time, Pallas kernels for 45%

profile of v1, /device:TPU:0, one launch (start us, length us, event | category | flops | bytes accessed | tf_op | source)
XLA Modules:
  0.0 41.1 jit_solution(15136257577651364923)
XLA Ops:
  0.6 0.5 %collective-permute-start = (f32[8,2048]{1,0:T(8,128)}, f32[8,2048]{1,0:T(8,128)S(1)}, u32[]{:S(2)}, u32[]{:S(2)}) collective-permute-start(f32[8,2048]{1,0:T(8,128)} %panels.3), channel_id=1, source_target_pairs={{0,1},{1,0},{2,3},{3,2},{4,5},{5,4},{6,7},{7,6},{8,9},{9,8},{10,11... | collective-permute-start | bytes 196616 | tf_op jit(solution)/shard_map/ppermute | solution.py:308
  1.1 0.1 collective-permute-start.1
  1.2 0.0 copy-start
  1.2 0.9 %copy-done = f32[6,4096]{1,0:T(8,128)S(1)} copy-done((f32[6,4096]{1,0:T(8,128)S(1)}, f32[6,4096]{1,0:T(8,128)}, u32[]{:S(2)}) %copy-start) | copy-done | bytes 98328
  2.1 0.0 copy-start.4
  2.1 0.7 %copy-done.4 = s32[32]{0:T(128)S(1)} copy-done((s32[32]{0:T(128)S(1)}, s32[32]{0:T(128)}, u32[]{:S(2)}) %copy-start.4) | copy-done | bytes 152
  2.8 0.0 copy-start.2
  2.8 0.0 copy-start.3
  2.8 1.9 %prepare.1 = (bf16[4096,48]{1,0:T(8,128)(2,1)S(1)}, bf16[512,256]{1,0:T(8,128)(2,1)S(1)}, f32[768,128]{1,0:T(8,128)S(1)}) custom-call(f32[6,4096]{1,0:T(8,128)S(1)} %copy-done, s32[32]{0:T(128)S(1)} %copy-done.4), custom_call_target="tpu_custom_call" | custom-call | tf_op jit(solution)/shard_map/prepare/pallas_call | solution.py:253
  4.7 0.0 collective-permute-done.1.near_o
  4.7 0.0 collective-permute-done.others
  4.7 0.0 copy-done.2
  4.7 0.0 copy-done.3
  4.8 7.2 %panel_side.1 = f32[1,4096]{1,0:T(1,128)S(1)} custom-call(f32[8,2048]{1,0:T(8,128)S(1)} %copy-done.2, f32[8,2048]{1,0:T(8,128)S(1)} %collective-permute-done.others, s32[16,64]{1,0:T(8,128)S(1)} %copy-done.3, s32[16,64]{1,0:T(8,128)S(1)} %collective-permute-done.1.near_o, bf16[4096,48]{1,0:T(8,128)(2,1)S(1)} %get-tuple-element.5.ut, ...), custom_call_target="tpu_custom_call" | custom-call | tf_op jit(solution)/shard_map/panel_side/pallas_call | solution.py:276
  11.9 0.0 copy-start.1
  11.9 2.7 %collective-permute-start.2 = (f32[4096]{0:T(1024)S(1)}, f32[4096]{0:T(1024)S(1)}, u32[]{:S(2)}, u32[]{:S(2)}) collective-permute-start(f32[4096]{0:T(1024)S(1)} %bitcast.1), channel_id=1, source_target_pairs={{0,3},{1,2},{2,1},{3,0},{4,7},{5,6},{6,5},{7,4},{8,11},{9,10},{10,... | collective-permute-start | bytes 49160 | tf_op jit(solution)/shard_map/ppermute | solution.py:317
  14.6 1.4 %collective-permute-done.2 = f32[4096]{0:T(1024)S(1)} collective-permute-done((f32[4096]{0:T(1024)S(1)}, f32[4096]{0:T(1024)S(1)}, u32[]{:S(2)}, u32[]{:S(2)}) %collective-permute-start.2) | collective-permute-done | bytes 16416 | tf_op jit(solution)/shard_map/ppermute | solution.py:317
  16.1 1.8 %collective-permute-start.3 = (f32[4096]{0:T(1024)S(1)}, f32[4096]{0:T(1024)S(1)}, u32[]{:S(2)}, u32[]{:S(2)}) collective-permute-start(f32[4096]{0:T(1024)S(1)} %add.18), channel_id=1, source_target_pairs={{0,5},{1,4},{2,7},{3,6},{4,1},{5,0},{6,3},{7,2},{8,13},{9,12},{10,... | collective-permute-start | bytes 49160 | tf_op jit(solution)/shard_map/ppermute | solution.py:317
  17.9 1.4 %collective-permute-done.3 = f32[4096]{0:T(1024)S(1)} collective-permute-done((f32[4096]{0:T(1024)S(1)}, f32[4096]{0:T(1024)S(1)}, u32[]{:S(2)}, u32[]{:S(2)}) %collective-permute-start.3) | collective-permute-done | bytes 16416 | tf_op jit(solution)/shard_map/ppermute | solution.py:317
  19.4 2.7 %collective-permute-start.4 = (f32[4096]{0:T(1024)S(1)}, f32[4096]{0:T(1024)S(1)}, u32[]{:S(2)}, u32[]{:S(2)}) collective-permute-start(f32[4096]{0:T(1024)S(1)} %add.19), channel_id=1, source_target_pairs={{0,9},{1,8},{2,11},{3,10},{4,13},{5,12},{6,15},{7,14},{8,1},{9,0},... | collective-permute-start | bytes 49160 | tf_op jit(solution)/shard_map/ppermute | solution.py:317
  22.1 1.4 %collective-permute-done.4 = f32[4096]{0:T(1024)S(1)} collective-permute-done((f32[4096]{0:T(1024)S(1)}, f32[4096]{0:T(1024)S(1)}, u32[]{:S(2)}, u32[]{:S(2)}) %collective-permute-start.4) | collective-permute-done | bytes 16416 | tf_op jit(solution)/shard_map/ppermute | solution.py:317
  23.6 0.4 collective-permute-start.5
  23.9 0.0 copy-done.1
  23.9 16.5 %particle_side.1 = f32[3,4096]{1,0:T(4,128)} custom-call(f32[6,4096]{1,0:T(8,128)S(1)} %copy-done.1, f32[8,2048]{1,0:T(8,128)S(1)} %copy-done.2, f32[8,2048]{1,0:T(8,128)S(1)} %collective-permute-done.others, s32[16,64]{1,0:T(8,128)S(1)} %copy-done.3, s32[16,64]{1,0:T(8,128)S(1)} %collective-permute-done.1.near_o, bf16[4096,48]{1,0:T(8,128)(2,1)S(1)} %get-tuple-element.5.ut, ...), custom_call_target="tpu_custom_call" | custom-call | tf_op jit(solution)/shard_map/particle_side/pallas_call | solution.py:292
  40.4 0.0 collective-permute-done.5
  40.5 0.6 %dynamic-slice_add_fusion = f32[2048]{0:T(1024)} fusion(f32[2048]{0:T(1024)S(1)} %collective-permute-done.5, f32[4096]{0:T(1024)S(1)} %add.20, s32[]{:T(128)S(6)} %select_n.6), kind=kLoop, calls=%fused_computation | loop fusion | flops 2048 | bytes 24580 | tf_op jit(solution)/shard_map/add | solution.py:323
  (4 shorter events, 0.0 us)
Async XLA Ops:
  0.6 4.1 %collective-permute-start = (f32[8,2048]{1,0:T(8,128)}, f32[8,2048]{1,0:T(8,128)S(1)}, u32[]{:S(2)}, u32[]{:S(2)}) collective-permute-start(f32[8,2048]{1,0:T(8,128)} %panels.3), channel_id=1, source_target_pairs={{0,1},{1,0},{2,3},{3,2},{4,5},{5,4},{6,7},{7,6},{8,9},{9,8},{10,11... | collective-permute-start | bytes 196616 | tf_op jit(solution)/shard_map/ppermute | solution.py:308
  1.1 3.6 %collective-permute-start.1 = (s32[16,64]{1,0:T(8,128)}, s32[16,64]{1,0:T(8,128)S(1)}, u32[]{:S(2)}, u32[]{:S(2)}) collective-permute-start(s32[16,64]{1,0:T(8,128)} %near.3), channel_id=1, source_target_pairs={{0,1},{1,0},{2,3},{3,2},{4,5},{5,4},{6,7},{7,6},{8,9},{9,8},{10,11... | collective-permute-start | bytes 12296 | tf_op jit(solution)/shard_map/ppermute | solution.py:309
  1.2 0.9 %copy-start = (f32[6,4096]{1,0:T(8,128)S(1)}, f32[6,4096]{1,0:T(8,128)}, u32[]{:S(2)}) copy-start(f32[6,4096]{1,0:T(8,128)} %particles.3) | copy-start | bytes 294916
  2.1 0.7 %copy-start.4 = (s32[32]{0:T(128)S(1)}, s32[32]{0:T(128)}, u32[]{:S(2)}) copy-start(s32[32]{0:T(128)} %counts.1) | copy-start | bytes 388
  2.8 2.0 %copy-start.2 = (f32[8,2048]{1,0:T(8,128)S(1)}, f32[8,2048]{1,0:T(8,128)}, u32[]{:S(2)}) copy-start(f32[8,2048]{1,0:T(8,128)} %panels.3) | copy-start | bytes 196612
  2.8 2.0 %copy-start.3 = (s32[16,64]{1,0:T(8,128)S(1)}, s32[16,64]{1,0:T(8,128)}, u32[]{:S(2)}) copy-start(s32[16,64]{1,0:T(8,128)} %near.3) | copy-start | bytes 12292
  11.9 12.0 %copy-start.1 = (f32[6,4096]{1,0:T(8,128)S(1)}, f32[6,4096]{1,0:T(8,128)}, u32[]{:S(2)}) copy-start(f32[6,4096]{1,0:T(8,128)} %particles.3) | copy-start | bytes 294916
  11.9 4.2 %collective-permute-start.2 = (f32[4096]{0:T(1024)S(1)}, f32[4096]{0:T(1024)S(1)}, u32[]{:S(2)}, u32[]{:S(2)}) collective-permute-start(f32[4096]{0:T(1024)S(1)} %bitcast.1), channel_id=1, source_target_pairs={{0,3},{1,2},{2,1},{3,0},{4,7},{5,6},{6,5},{7,4},{8,11},{9,10},{10,... | collective-permute-start | bytes 49160 | tf_op jit(solution)/shard_map/ppermute | solution.py:317
  16.1 3.3 %collective-permute-start.3 = (f32[4096]{0:T(1024)S(1)}, f32[4096]{0:T(1024)S(1)}, u32[]{:S(2)}, u32[]{:S(2)}) collective-permute-start(f32[4096]{0:T(1024)S(1)} %add.18), channel_id=1, source_target_pairs={{0,5},{1,4},{2,7},{3,6},{4,1},{5,0},{6,3},{7,2},{8,13},{9,12},{10,... | collective-permute-start | bytes 49160 | tf_op jit(solution)/shard_map/ppermute | solution.py:317
  19.4 4.2 %collective-permute-start.4 = (f32[4096]{0:T(1024)S(1)}, f32[4096]{0:T(1024)S(1)}, u32[]{:S(2)}, u32[]{:S(2)}) collective-permute-start(f32[4096]{0:T(1024)S(1)} %add.19), channel_id=1, source_target_pairs={{0,9},{1,8},{2,11},{3,10},{4,13},{5,12},{6,15},{7,14},{8,1},{9,0},... | collective-permute-start | bytes 49160 | tf_op jit(solution)/shard_map/ppermute | solution.py:317
  23.6 16.9 %collective-permute-start.5 = (f32[2048]{0:T(1024)S(1)}, f32[2048]{0:T(1024)S(1)}, u32[]{:S(2)}, u32[]{:S(2)}) collective-permute-start(f32[2048]{0:T(1024)S(1)} %dynamic_slice.7), channel_id=1, source_target_pairs={{0,1},{1,0},{2,3},{3,2},{4,5},{5,4},{6,7},{7,6},{8,9},{9,8},{10,11... | collective-permute-start | bytes 24584 | tf_op jit(solution)/shard_map/ppermute | solution.py:323

commit v2 on v1

v2 whole, which is shorter than its diff:
```python
import functools

import jax
import jax.numpy as jnp
from jax import lax
from jax.experimental import pallas as pl
from jax.experimental.pallas import tpu as pltpu
from jax.sharding import PartitionSpec as P

core_sq = 0.04
inv_four_pi = 0.07957747154594767
BLK = 128
WIN = 3
EACH1 = 16
EACH = 8
bf16 = jnp.bfloat16
f32 = jnp.float32


def split2(v):
    hi = v.astype(bf16)
    lo = (v - hi.astype(f32)).astype(bf16)
    return hi, lo


def split3(v):
    a = v.astype(bf16).astype(f32)
    rest = v - a
    b = rest.astype(bf16).astype(f32)
    return a, b, rest - b


def rows16(w):
    w1 = w.astype(bf16).astype(f32)
    return jnp.concatenate([w1, w - w1], axis=0).astype(bf16)


def up(v, k):
    return pltpu.roll(v, (8 - k) % 8, 0)


def rows8(width):
    return lax.broadcasted_iota(jnp.int32, (8, width), 0)


def block(q, size):
    return pl.ds(pl.multiple_of(q * size, size), size)


def particle_features(particles, u_t, u_n, fe, org, parts):
    nblk = particles.shape[1] // BLK
    parts[0:6, :] = particles[...]
    row = rows8(BLK)

    def one(q, carry):
        p = parts[:, block(q, BLK)]
        x = jnp.where(row < 3, p, 0.0)
        a = jnp.where(row < 3, up(p, 3), 0.0)
        xx = jnp.sum(x * x, axis=0, keepdims=True) + core_sq
        feat = jnp.where(row < 3, x, jnp.where(row < 6, 1.0, jnp.where(row == 6, xx, 0.0)))
        x1, x2, x3 = split3(feat)
        u = jnp.concatenate([x1, x1, x2, x2, x1, x3], axis=0)
        u_t[block(q, BLK), :] = u.T.astype(bf16)
        u_n[:, block(q, BLK)] = u.astype(bf16)
        o = jnp.broadcast_to(x[:, 0:1], (8, BLK))
        d = x - o

        def rot1(v):
            return jnp.where(row < 2, up(v, 1), jnp.where(row == 2, up(v, 6), 0.0))

        def rot2(v):
            return jnp.where(row < 1, up(v, 2), jnp.where(row < 3, up(v, 7), 0.0))

        cross = rot1(d) * rot2(a) - rot2(d) * rot1(a)
        f = jnp.where(row < 3, a, up(cross, 5))
        f = jnp.where(row < 6, f, 0.0)
        f16 = rows16(f)
        fe[block(q, 16), :] = jnp.concatenate([f16, f16], axis=1)
        for i, v in enumerate((o, rot1(o), rot2(o), d)):
            org[pl.ds(pl.multiple_of(q * 32 + 8 * i, 8), 8), :] = v
        return carry

    lax.fori_loop(0, nblk, one, 0, unroll=4)


def spans(mine, other, me, box):
    half, cols = mine.shape
    row = lax.broadcasted_iota(jnp.int32, (half, cols), 0)
    big = jnp.int32(2 * half)
    a, b = mine[...], other[...]
    first = jnp.minimum(
        jnp.min(jnp.where(a > 0, row + me * half, big), axis=0, keepdims=True),
        jnp.min(jnp.where(b > 0, row + (1 - me) * half, big), axis=0, keepdims=True),
    )
    number = jnp.sum(a, axis=0, keepdims=True) + jnp.sum(b, axis=0, keepdims=True)
    if cols < BLK:
        pad = jnp.zeros((1, BLK - cols), jnp.int32)
        first = jnp.concatenate([first, pad], axis=1)
        number = jnp.concatenate([number, pad], axis=1)
    rowb = rows8(first.shape[1])
    box[...] = jnp.where(rowb == 0, first, jnp.where(rowb == 1, number, 0))


def each_panel_chunk(panels, others, me, chunk, body):
    half = panels.shape[1]

    def run(ref, start):
        def one(k, carry):
            src = pl.ds(pl.multiple_of(k * chunk, chunk), chunk)
            dst = pl.ds(pl.multiple_of(start + k * chunk, chunk), chunk)
            body(ref[:, src], dst)
            return carry

        lax.fori_loop(0, half // chunk, one, 0, unroll=2)

    run(panels, me * half)
    run(others, (1 - me) * half)
    body(jnp.zeros((8, chunk), f32), pl.ds(2 * half, chunk))


def stack6(v, c1, c2, c3, at):
    pair = jnp.concatenate([c1, c2], axis=0).astype(bf16)
    v[0:16, at] = pair
    v[16:32, at] = pair
    v[32:48, at] = jnp.concatenate([c3, c1], axis=0).astype(bf16)


def list_items(table, offset, count, items):
    filled = jnp.int32(0)
    for i in range(count):
        first = table[0, offset + i]
        number = table[1, offset + i]
        for k in range(WIN):
            items[0, filled] = i
            items[1, filled] = first + k
            filled = filled + jnp.where(k < number, 1, 0)
    return filled


def panel_sums(counts, panels, others, near, near_o, ut, fe, org, out, pan, box, v, n1, n2, c1, c2, tot, table, items, sem):
    me = lax.axis_index("panel")
    nblk = ut.shape[0] // BLK
    npan = 2 * panels.shape[1]
    spans(near, near_o, me, box)
    copy = pltpu.make_async_copy(box, table, sem)
    copy.start()
    chunk = 2 * BLK
    row = rows8(chunk)

    def build(p, at):
        pan[:, at] = p
        c = jnp.where(row < 3, p, 0.0)
        dist = jnp.where(row < 3, -2.0 * c, jnp.where(row < 6, up(c * c, 5), jnp.where(row == 6, 1.0, 0.0)))
        stack6(v, *split3(dist), at)
        n1[:, at] = jnp.where(row < 2, up(p, 4), jnp.where(row == 2, up(p, 1), jnp.where(row < 6, -p, 0.0)))
        n2[:, at] = jnp.where(row < 1, up(p, 5), jnp.where(row < 3, up(p, 2), 0.0))
        c1[:, at] = jnp.where(row < 2, up(p, 1), jnp.where(row == 2, up(p, 6), 0.0))
        c2[:, at] = jnp.where(row < 1, up(p, 2), jnp.where(row < 3, up(p, 7), 1.0))
        tot[:, at] = jnp.zeros((8, chunk), f32)

    each_panel_chunk(panels, others, me, chunk, build)
    copy.wait()

    filled = list_items(table, me * nblk, nblk, items)
    lane = lax.broadcasted_iota(jnp.int32, (16, 2 * BLK), 1) % BLK

    def moments(n):
        q, at = items[0, n], block(items[1, n], BLK)
        r2 = jnp.dot(ut[block(q, BLK), :], v[:, at], preferred_element_type=f32)
        inv = lax.rsqrt(r2)
        hi, lo = split2(inv * inv * inv)
        weight = jnp.where(lane < counts[q], 1.0, 0.0).astype(bf16)
        return fe[block(q, 16), :] * weight, jnp.concatenate([hi, lo], axis=0)

    def finish(n, g, keep):
        q, at = items[0, n], block(items[1, n], BLK)
        o1 = org[pl.ds(pl.multiple_of(q * 32 + 8, 8), 8), :]
        o2 = org[pl.ds(pl.multiple_of(q * 32 + 16, 8), 8), :]
        m = n1[:, at] * (c2[:, at] - o2) - n2[:, at] * (c1[:, at] - o1)
        tot[:, at] += (g[0:8] + g[8:16]) * (m * keep)

    def some(i, carry):
        ns = [jnp.minimum(i * EACH1 + e, filled - 1) for e in range(EACH1)]
        keeps = [jnp.where(i * EACH1 + e < filled, 1.0, 0.0) for e in range(EACH1)]
        parts = [moments(n) for n in ns]
        for e in range(0, EACH1, 2):
            (fa, ka), (fb, kb) = parts[e], parts[e + 1]
            g = jnp.dot(
                jnp.concatenate([fa, fb], axis=0), jnp.concatenate([ka, kb], axis=1), preferred_element_type=f32
            )
            finish(ns[e], g[0:16, 0:BLK], keeps[e])
            finish(ns[e + 1], g[16:32, BLK:], keeps[e + 1])
        return carry

    lax.fori_loop(0, (filled + EACH1 - 1) // EACH1, some, 0)
    out[...] = -inv_four_pi * jnp.sum(tot[:, 0:npan], axis=0, keepdims=True)


def particle_sums(start, count, nblk, build, pan, table, un, v, org, *rest):
    items = rest[-1]
    row8 = rows8(BLK)
    if build:
        out, vn = rest[:2]
        earlier = []
        chunk = 2 * BLK
        row = rows8(chunk)

        def one_chunk(k, carry):
            at = block(k, chunk)
            p = pan[:, at]
            mn3 = jnp.where(row < 3, up(p, 3) * p[7:8, :], 0.0) * 3.0
            c = jnp.where(row < 3, p, 0.0)
            stack6(vn, *split3(jnp.where(row < 3, -mn3, up(mn3 * c, 5))), at)
            return carry

        lax.fori_loop(0, pan.shape[1] // chunk, one_chunk, 0)
    else:
        vn = rest[0]
        earlier, out = rest[1:-2], rest[-2]
    me = lax.axis_index("panel")
    offset = 0
    for e in earlier:
        out[:, offset : offset + e.shape[1]] = e[...]
        offset += e.shape[1]
    out[:, offset : offset + count * BLK] = jnp.zeros((3, count * BLK), f32)
    filled = list_items(table, me * nblk + start, count, items)
    turn = (((0,), (0,)), ((), ()))

    def factors(n):
        i, at = items[0, n], block(items[1, n], BLK)
        q = start + i
        p = pan[:, at]
        d = jnp.where(row8 < 3, p - org[pl.ds(pl.multiple_of(q * 32, 8), 8), :], jnp.where(row8 == 3, 1.0, 0.0))
        mn = jnp.where(row8 < 3, up(p, 3) * p[7:8], 0.0)
        d16, e16 = rows16(d), rows16(-p[6:7] * d - mn)
        u = un[:, block(q, BLK)]
        r2 = lax.dot_general(v[:, at], u, turn, preferred_element_type=f32)
        nr = lax.dot_general(vn[:, at], u, turn, preferred_element_type=f32)
        inv = lax.rsqrt(r2)
        inv2 = inv * inv
        inv3 = inv2 * inv
        t1, t2 = split2(inv3 * (inv2 * nr))
        i1, i2 = split2(inv3)
        return jnp.concatenate([d16, d16, e16, e16], axis=1), jnp.concatenate([t1, t2, i1, i2], axis=0)

    def finish(n, h, keep):
        i = items[0, n]
        x = org[pl.ds(pl.multiple_of((start + i) * 32 + 24, 8), 8), :]
        h = (h[0:8] + h[8:16]) * keep
        out[:, pl.ds(pl.multiple_of(offset + i * BLK, BLK), BLK)] += h[0:3] - x[0:3] * h[3:4]

    def some(i, carry):
        ns = [jnp.minimum(i * EACH + e, filled - 1) for e in range(EACH)]
        keeps = [jnp.where(i * EACH + e < filled, inv_four_pi, 0.0) for e in range(EACH)]
        parts = [factors(n) for n in ns]
        for e in range(0, EACH, 2):
            (fa, ka), (fb, kb) = parts[e], parts[e + 1]
            h = jnp.dot(
                jnp.concatenate([fa, fb], axis=0), jnp.concatenate([ka, kb], axis=1), preferred_element_type=f32
            )
            finish(ns[e], h[0:16, 0:BLK], keeps[e])
            finish(ns[e + 1], h[16:32, BLK:], keeps[e + 1])
        return carry

    lax.fori_loop(0, (filled + EACH - 1) // EACH, some, 0)


def vmem():
    return pl.BlockSpec(memory_space=pltpu.VMEM)


def smem():
    return pl.BlockSpec(memory_space=pltpu.SMEM)


def params(mib=24):
    return pltpu.CompilerParams(vmem_limit_bytes=mib * 1024 * 1024)


def prepare(particles):
    width = particles.shape[1]
    nblk = width // BLK
    return pl.pallas_call(
        particle_features,
        out_shape=(
            jax.ShapeDtypeStruct((width, 48), bf16),
            jax.ShapeDtypeStruct((48, width), bf16),
            jax.ShapeDtypeStruct((nblk * 16, 2 * BLK), bf16),
            jax.ShapeDtypeStruct((nblk * 32, BLK), f32),
        ),
        in_specs=[vmem()],
        out_specs=(vmem(),) * 4,
        scratch_shapes=[pltpu.VMEM((8, width), f32)],
        compiler_params=params(),
        name="prepare",
    )(particles)


def panel_side(counts, panels, others, near, near_o, ut, fe, org):
    npan = 2 * panels.shape[1]
    full = npan + 2 * BLK
    wide = max(near.shape[1], BLK)
    return pl.pallas_call(
        panel_sums,
        out_shape=(
            jax.ShapeDtypeStruct((1, npan), f32),
            jax.ShapeDtypeStruct((8, full), f32),
            jax.ShapeDtypeStruct((8, wide), jnp.int32),
            jax.ShapeDtypeStruct((48, full), bf16),
        ),
        in_specs=[smem()] + [vmem()] * 7,
        out_specs=(vmem(),) * 4,
        scratch_shapes=[pltpu.VMEM((8, full), f32)] * 5
        + [
            pltpu.SMEM((8, wide), jnp.int32),
            pltpu.SMEM((2, WIN * counts.shape[0] + 1), jnp.int32),
            pltpu.SemaphoreType.DMA,
        ],
        compiler_params=params(),
        name="panel_side",
    )(counts, panels, others, near, near_o, ut, fe, org)


def particle_side(start, count, nblk, pan, box, un, v, org, vn, earlier):
    done = sum(e.shape[1] for e in earlier)
    build = vn is None
    shape = jax.ShapeDtypeStruct((3, done + count * BLK), f32)
    args = [pan, box, un, v, org] + ([] if build else [vn]) + list(earlier)
    return pl.pallas_call(
        functools.partial(particle_sums, start, count, nblk, build),
        out_shape=(shape, jax.ShapeDtypeStruct(v.shape, bf16)) if build else shape,
        in_specs=[vmem(), smem()] + [vmem()] * (len(args) - 2),
        out_specs=(vmem(), vmem()) if build else vmem(),
        scratch_shapes=[pltpu.SMEM((2, WIN * count + 1), jnp.int32)],
        compiler_params=params(),
        cost_estimate=pl.CostEstimate(flops=count * 3 * BLK * BLK * 32, bytes_accessed=count * 1000, transcendentals=0),
        name="particle_side",
    )(*args)


def on_device(dom, panels, particles, counts, near):
    swap = [(0, 1), (1, 0)]
    others = lax.ppermute(panels, "panel", swap)
    near_o = lax.ppermute(near, "panel", swap)
    ut, un, fe, org = prepare(particles)
    total, pan, box, v = panel_side(counts, panels, others, near, near_o, ut, fe, org)
    total = total.reshape(total.shape[1])
    nblk = counts.shape[0]
    steps = [1 << b for b in range((dom - 1).bit_length())]
    edges = [nblk * i // (len(steps) + 1) for i in range(len(steps) + 2)]
    chunks, factors = [], None

    for number, step in enumerate(steps):
        pairs = [(2 * i + c, 2 * (i ^ step) + 1 - c) for i in range(dom) for c in range(2)]
        total, at = lax.optimization_barrier((total, box))
        got = particle_side(edges[number], edges[number + 1] - edges[number], nblk, pan, at, un, v, org, factors, [])
        if factors is None:
            got, factors = got
        arrived, got = lax.optimization_barrier((lax.ppermute(total, ("dom", "panel"), pairs), got))
        chunks.append(got)
        total = total + arrived
    half = total.shape[0] // 2
    me = lax.axis_index("panel")
    total, at = lax.optimization_barrier((total, box))
    velocity = particle_side(edges[-2], edges[-1] - edges[-2], nblk, pan, at, un, v, org, factors, chunks)
    keep = lax.dynamic_slice(total, (me * half,), (half,))
    give = lax.dynamic_slice(total, ((1 - me) * half,), (half,))
    return keep + lax.ppermute(give, "panel", swap), velocity


def solution(mesh):
    return jax.shard_map(
        functools.partial(on_device, mesh.shape["dom"]),
        mesh=mesh,
        in_specs=(
            P(None, ("groups", "panel")),
            P(None, ("groups", "dom", "panel")),
            P(("groups", "dom", "panel")),
            P(("groups", "panel"), "dom"),
        ),
        out_specs=(P(("groups", "panel")), P(None, ("groups", "dom", "panel"))),
        check_vma=False,
    )
```

time: 41.2 us -> 25.4 us (0.62); the launches traced: 41.1 us -> 25.7 us
  Pallas kernels: 25.6 us -> 14.9 us
  waiting for transfers between devices: 4.34 us -> 0.52 us
  starting transfers between devices: 8.23 us -> 7.34 us
    pallas_call x2 -> x5, Pallas kernels: 23.7 us -> 13.6 us  [the longest x4 9.42 us: particle_side(): pl.pallas_call(functools.partial(particle_sums, start, count, nblk, build...]
    ppermute x3, waiting for transfers between devices: 4.33 us -> 0.51 us  [on_device(): lax.ppermute(total, ('dom', 'panel'), pairs)]
    ppermute x3, starting transfers between devices: 7.26 us -> 6.15 us  [on_device(): lax.ppermute(total, ('dom', 'panel'), pairs)]
    pallas_call x1, Pallas kernels: 1.92 us -> 1.3 us  [prepare(): pl.pallas_call(particle_features, out_shape=(jax.ShapeDtypeStruct((width,...]
    unnamed x10 -> x8, local copies, waits for them, and re-layouts: 1.57 us -> 1.54 us
  transfers between devices with their start and end apart: 6 -> 6, of which waited for: 3 -> 1; matrix products, arithmetic and copies ran while one was open for 0% -> 0% of each run, Pallas kernels for 45% -> 42%
where the time goes in v2:
time: 25.4 us; the launch traced here: 25.7 us
  Pallas kernels  14.9 us (59%)
  starting transfers between devices  7.34 us (29%)
  local copies, waits for them, and re-layouts  1.55 us (6%)
  between operations  0.75 us (3%)
  other arithmetic  0.62 us (2%)
  waiting for transfers between devices  0.52 us (2%)
    pallas_call x4, Pallas kernels, particle_side(): pl.pallas_call(functools.partial(particle_sums, start, count, nblk, build...  9.42 us
    ppermute x3, starting transfers between devices, on_device(): lax.ppermute(total, ('dom', 'panel'), pairs)  6.15 us
    pallas_call x1, Pallas kernels, panel_side(): pl.pallas_call(panel_sums, out_shape=(jax.ShapeDtypeStruct((1, npan), f32...  4.21 us
    unnamed x8, local copies, waits for them, and re-layouts  1.54 us
    pallas_call x1, Pallas kernels, prepare(): pl.pallas_call(particle_features, out_shape=(jax.ShapeDtypeStruct((width,...  1.3 us
    add x1, other arithmetic, on_device(): return (keep + lax.ppermute(give, 'panel', swap), velocity)  0.6 us
    ppermute x1, starting transfers between devices, on_device(): return (keep + lax.ppermute(give, 'panel', swap), velocity)  0.59 us
    ppermute x1, starting transfers between devices, on_device(): others = lax.ppermute(panels, 'panel', swap)  0.52 us
  transfers between devices with their start and end apart: 6, of which 1 were waited for; matrix products, arithmetic and copies ran while one was open for 0% of the time, Pallas kernels for 42%

profile of v2, /device:TPU:0, one launch (start us, length us, event | category | flops | bytes accessed | tf_op | source)
XLA Modules:
  0.0 25.7 jit_solution(16734079823835537023)
XLA Ops:
  0.6 0.5 %collective-permute-start = (f32[8,2048]{1,0:T(8,128)}, f32[8,2048]{1,0:T(8,128)S(1)}, u32[]{:S(2)}, u32[]{:S(2)}) collective-permute-start(f32[8,2048]{1,0:T(8,128)} %panels.1), channel_id=1, source_target_pairs={{0,1},{1,0},{2,3},{3,2},{4,5},{5,4},{6,7},{7,6},{8,9},{9,8},{10,11... | collective-permute-start | bytes 196616 | tf_op jit(solution)/shard_map/ppermute | solution.py:343
  1.1 0.1 collective-permute-start.1
  1.2 0.0 copy-start
  1.2 0.9 %copy-done = f32[6,4096]{1,0:T(8,128)S(1)} copy-done((f32[6,4096]{1,0:T(8,128)S(1)}, f32[6,4096]{1,0:T(8,128)}, u32[]{:S(2)}) %copy-start) | copy-done | bytes 98328
  2.1 0.0 copy-start.1
  2.1 0.0 copy-start.2
  2.1 1.3 %prepare.1 = (bf16[4096,48]{1,0:T(8,128)(2,1)S(1)}, bf16[48,4096]{1,0:T(8,128)(2,1)S(1)}, bf16[512,256]{1,0:T(8,128)(2,1)S(1)}, f32[1024,128]{1,0:T(8,128)S(1)}) custom-call(f32[6,4096]{1,0:T(8,128)S(1)} %copy-done), custom_call_target="tpu_custom_call" | custom-call | tf_op jit(solution)/shard_map/prepare/pallas_call | solution.py:283
  3.4 0.0 collective-permute-done.1.near_o
  3.5 0.0 collective-permute-done.others
  3.5 0.0 copy-start.3
  3.5 0.0 copy-done.1
  3.5 0.0 copy-done.2
  3.5 0.6 %copy-done.3 = s32[32]{0:T(128)S(1)} copy-done((s32[32]{0:T(128)S(1)}, s32[32]{0:T(128)}, u32[]{:S(2)}) %copy-start.3) | copy-done | bytes 152
  4.1 4.2 %panel_side.1 = (f32[1,4096]{1,0:T(1,128)S(1)}, f32[8,4352]{1,0:T(8,128)S(1)}, s32[8,128]{1,0:T(8,128)S(1)}, bf16[48,4352]{1,0:T(8,128)(2,1)S(1)}) custom-call(s32[32]{0:T(128)S(1)} %copy-done.3, f32[8,2048]{1,0:T(8,128)S(1)} %copy-done.1, f32[8,2048]{1,0:T(8,128)S(1)} %collective-permute-done.others, s32[16,64]{1,0:T(8,128)S(1)} %copy-done.2, ...), custom_call_target="tpu_custom_call" | custom-call | tf_op jit(solution)/shard_map/panel_side/pallas_call | solution.py:303
  8.3 2.7 %collective-permute-start.2 = (f32[4096]{0:T(1024)S(1)}, f32[4096]{0:T(1024)S(1)}, u32[]{:S(2)}, u32[]{:S(2)}) collective-permute-start(f32[4096]{0:T(1024)S(1)} %bitcast.1), channel_id=1, source_target_pairs={{0,3},{1,2},{2,1},{3,0},{4,7},{5,6},{6,5},{7,4},{8,11},{9,10},{10,... | collective-permute-start | bytes 49160 | tf_op jit(solution)/shard_map/ppermute | solution.py:359
  11.0 2.7 %particle_side.4 = (f32[3,1024]{1,0:T(4,128)S(1)}, bf16[48,4352]{1,0:T(8,128)(2,1)S(1)}) custom-call(f32[8,4352]{1,0:T(8,128)S(1)} %get-tuple-element.32.pan, s32[8,128]{1,0:T(8,128)S(1)} %get-tuple-element.46.table, bf16[48,4096]{1,0:T(8,128)(2,1)S(1)} %get-tuple-element.34.un, bf16[48,4352]{1,0:T(8,128)(2,1)S(1)} %get-tuple-element.35.v, ...), custom_call_target="tpu_custom_call" | custom-call | flops 12582912 | bytes 8000 | tf_op jit(solution)/shard_map/particle_side/pallas_call | solution.py:329
  13.7 0.0 collective-permute-done.2
  13.7 1.7 %collective-permute-start.3 = (f32[4096]{0:T(1024)S(1)}, f32[4096]{0:T(1024)S(1)}, u32[]{:S(2)}, u32[]{:S(2)}) collective-permute-start(f32[4096]{0:T(1024)S(1)} %add.18), channel_id=1, source_target_pairs={{0,5},{1,4},{2,7},{3,6},{4,1},{5,0},{6,3},{7,2},{8,13},{9,12},{10,... | collective-permute-start | bytes 49160 | tf_op jit(solution)/shard_map/ppermute | solution.py:359
  15.4 1.8 %particle_side.5.rest_2_ = f32[3,1024]{1,0:T(4,128)S(1)} custom-call(f32[8,4352]{1,0:T(8,128)S(1)} %get-tuple-element.32.pan, s32[8,128]{1,0:T(8,128)S(1)} %get-tuple-element.46.table, bf16[48,4096]{1,0:T(8,128)(2,1)S(1)} %get-tuple-element.34.un, bf16[48,4352]{1,0:T(8,128)(2,1)S(1)} %get-tuple-element.35.v, f32[1024,128]{1,0:T(8,128)S(1)} %get-tuple-element.28.org, ...), custom_call_target="tpu_custom_call" | custom-call | flops 12582912 | bytes 8000 | tf_op jit(solution)/shard_map/particle_side/pallas_call | solution.py:329
  17.3 0.0 collective-permute-done.3
  17.3 1.8 %collective-permute-start.4 = (f32[4096]{0:T(1024)S(1)}, f32[4096]{0:T(1024)S(1)}, u32[]{:S(2)}, u32[]{:S(2)}) collective-permute-start(f32[4096]{0:T(1024)S(1)} %add.19), channel_id=1, source_target_pairs={{0,9},{1,8},{2,11},{3,10},{4,13},{5,12},{6,15},{7,14},{8,1},{9,0},... | collective-permute-start | bytes 49160 | tf_op jit(solution)/shard_map/ppermute | solution.py:359
  19.1 1.8 %particle_side.6.rest_3_ = f32[3,1024]{1,0:T(4,128)S(1)} custom-call(f32[8,4352]{1,0:T(8,128)S(1)} %get-tuple-element.32.pan, s32[8,128]{1,0:T(8,128)S(1)} %get-tuple-element.46.table, bf16[48,4096]{1,0:T(8,128)(2,1)S(1)} %get-tuple-element.34.un, bf16[48,4352]{1,0:T(8,128)(2,1)S(1)} %get-tuple-element.35.v, f32[1024,128]{1,0:T(8,128)S(1)} %get-tuple-element.28.org, ...), custom_call_target="tpu_custom_call" | custom-call | flops 12582912 | bytes 8000 | tf_op jit(solution)/shard_map/particle_side/pallas_call | solution.py:329
  20.9 0.5 %collective-permute-done.4 = f32[4096]{0:T(1024)S(1)} collective-permute-done((f32[4096]{0:T(1024)S(1)}, f32[4096]{0:T(1024)S(1)}, u32[]{:S(2)}, u32[]{:S(2)}) %collective-permute-start.4) | collective-permute-done | bytes 16416 | tf_op jit(solution)/shard_map/ppermute | solution.py:359
  21.4 0.6 %collective-permute-start.5 = (f32[2048]{0:T(1024)S(1)}, f32[2048]{0:T(1024)S(1)}, u32[]{:S(2)}, u32[]{:S(2)}) collective-permute-start(f32[2048]{0:T(1024)S(1)} %dynamic_slice.7), channel_id=1, source_target_pairs={{0,1},{1,0},{2,3},{3,2},{4,5},{5,4},{6,7},{7,6},{8,9},{9,8},{10,11... | collective-permute-start | bytes 24584 | tf_op jit(solution)/shard_map/ppermute | solution.py:368
  22.0 3.1 %particle_side.7 = f32[3,4096]{1,0:T(4,128)} custom-call(f32[8,4352]{1,0:T(8,128)S(1)} %get-tuple-element.32.pan, s32[8,128]{1,0:T(8,128)S(1)} %get-tuple-element.46.table, bf16[48,4096]{1,0:T(8,128)(2,1)S(1)} %get-tuple-element.34.un, bf16[48,4352]{1,0:T(8,128)(2,1)S(1)} %get-tuple-element.35.v, f32[1024,128]{1,0:T(8,128)S(1)} %get-tuple-element.28.org, ...), custom_call_target="tpu_custom_call" | custom-call | flops 12582912 | bytes 8000 | tf_op jit(solution)/shard_map/particle_side/pallas_call | solution.py:329
  25.1 0.0 collective-permute-done.5
  25.1 0.6 %dynamic-slice_add_fusion = f32[2048]{0:T(1024)} fusion(f32[2048]{0:T(1024)S(1)} %collective-permute-done.5, f32[4096]{0:T(1024)S(1)} %add.20, s32[]{:T(128)S(6)} %select_n.6), kind=kLoop, calls=%fused_computation | loop fusion | flops 2048 | bytes 24580 | tf_op jit(solution)/shard_map/add | solution.py:368
  (4 shorter events, 0.0 us)
Async XLA Ops:
  0.6 2.8 %collective-permute-start = (f32[8,2048]{1,0:T(8,128)}, f32[8,2048]{1,0:T(8,128)S(1)}, u32[]{:S(2)}, u32[]{:S(2)}) collective-permute-start(f32[8,2048]{1,0:T(8,128)} %panels.1), channel_id=1, source_target_pairs={{0,1},{1,0},{2,3},{3,2},{4,5},{5,4},{6,7},{7,6},{8,9},{9,8},{10,11... | collective-permute-start | bytes 196616 | tf_op jit(solution)/shard_map/ppermute | solution.py:343
  1.1 2.3 %collective-permute-start.1 = (s32[16,64]{1,0:T(8,128)}, s32[16,64]{1,0:T(8,128)S(1)}, u32[]{:S(2)}, u32[]{:S(2)}) collective-permute-start(s32[16,64]{1,0:T(8,128)} %near.1), channel_id=1, source_target_pairs={{0,1},{1,0},{2,3},{3,2},{4,5},{5,4},{6,7},{7,6},{8,9},{9,8},{10,11... | collective-permute-start | bytes 12296 | tf_op jit(solution)/shard_map/ppermute | solution.py:344
  1.2 0.9 %copy-start = (f32[6,4096]{1,0:T(8,128)S(1)}, f32[6,4096]{1,0:T(8,128)}, u32[]{:S(2)}) copy-start(f32[6,4096]{1,0:T(8,128)} %particles.1) | copy-start | bytes 294916
  2.1 1.4 %copy-start.1 = (f32[8,2048]{1,0:T(8,128)S(1)}, f32[8,2048]{1,0:T(8,128)}, u32[]{:S(2)}) copy-start(f32[8,2048]{1,0:T(8,128)} %panels.1) | copy-start | bytes 196612
  2.1 1.4 %copy-start.2 = (s32[16,64]{1,0:T(8,128)S(1)}, s32[16,64]{1,0:T(8,128)}, u32[]{:S(2)}) copy-start(s32[16,64]{1,0:T(8,128)} %near.1) | copy-start | bytes 12292
  3.5 0.7 %copy-start.3 = (s32[32]{0:T(128)S(1)}, s32[32]{0:T(128)}, u32[]{:S(2)}) copy-start(s32[32]{0:T(128)} %counts.1) | copy-start | bytes 388
  8.3 5.4 %collective-permute-start.2 = (f32[4096]{0:T(1024)S(1)}, f32[4096]{0:T(1024)S(1)}, u32[]{:S(2)}, u32[]{:S(2)}) collective-permute-start(f32[4096]{0:T(1024)S(1)} %bitcast.1), channel_id=1, source_target_pairs={{0,3},{1,2},{2,1},{3,0},{4,7},{5,6},{6,5},{7,4},{8,11},{9,10},{10,... | collective-permute-start | bytes 49160 | tf_op jit(solution)/shard_map/ppermute | solution.py:359
  13.7 3.5 %collective-permute-start.3 = (f32[4096]{0:T(1024)S(1)}, f32[4096]{0:T(1024)S(1)}, u32[]{:S(2)}, u32[]{:S(2)}) collective-permute-start(f32[4096]{0:T(1024)S(1)} %add.18), channel_id=1, source_target_pairs={{0,5},{1,4},{2,7},{3,6},{4,1},{5,0},{6,3},{7,2},{8,13},{9,12},{10,... | collective-permute-start | bytes 49160 | tf_op jit(solution)/shard_map/ppermute | solution.py:359
  17.3 4.1 %collective-permute-start.4 = (f32[4096]{0:T(1024)S(1)}, f32[4096]{0:T(1024)S(1)}, u32[]{:S(2)}, u32[]{:S(2)}) collective-permute-start(f32[4096]{0:T(1024)S(1)} %add.19), channel_id=1, source_target_pairs={{0,9},{1,8},{2,11},{3,10},{4,13},{5,12},{6,15},{7,14},{8,1},{9,0},... | collective-permute-start | bytes 49160 | tf_op jit(solution)/shard_map/ppermute | solution.py:359
  21.4 3.7 %collective-permute-start.5 = (f32[2048]{0:T(1024)S(1)}, f32[2048]{0:T(1024)S(1)}, u32[]{:S(2)}, u32[]{:S(2)}) collective-permute-start(f32[2048]{0:T(1024)S(1)} %dynamic_slice.7), channel_id=1, source_target_pairs={{0,1},{1,0},{2,3},{3,2},{4,5},{5,4},{6,7},{7,6},{8,9},{9,8},{10,11... | collective-permute-start | bytes 24584 | tf_op jit(solution)/shard_map/ppermute | solution.py:368

commit v3 on v2

v3 whole, which is shorter than its diff:
```python
import functools

import jax
import jax.numpy as jnp
from jax import lax
from jax.experimental import pallas as pl
from jax.experimental.pallas import tpu as pltpu
from jax.sharding import PartitionSpec as P

core_sq = 0.04
inv_four_pi = 0.07957747154594767
BLK = 128
WIN = 3
EACH1 = 16
EACH = 8
bf16 = jnp.bfloat16
f32 = jnp.float32


def split2(v):
    hi = v.astype(bf16)
    lo = (v - hi.astype(f32)).astype(bf16)
    return hi, lo


def split3(v):
    a = v.astype(bf16).astype(f32)
    rest = v - a
    b = rest.astype(bf16).astype(f32)
    return a, b, rest - b


def rows16(w):
    w1 = w.astype(bf16).astype(f32)
    return jnp.concatenate([w1, w - w1], axis=0).astype(bf16)


def up(v, k):
    return pltpu.roll(v, (8 - k) % 8, 0)


def rows8(width):
    return lax.broadcasted_iota(jnp.int32, (8, width), 0)


def block(q, size):
    return pl.ds(pl.multiple_of(q * size, size), size)


def particle_features(particles, un, fe, org, parts):
    nblk = particles.shape[1] // BLK
    parts[0:6, :] = particles[...]
    row = rows8(BLK)

    def one(q, carry):
        p = parts[:, block(q, BLK)]
        x = jnp.where(row < 3, p, 0.0)
        a = jnp.where(row < 3, up(p, 3), 0.0)
        xx = jnp.sum(x * x, axis=0, keepdims=True) + core_sq
        feat = jnp.where(row < 3, x, jnp.where(row < 6, 1.0, jnp.where(row == 6, xx, 0.0)))
        x1, x2, x3 = split3(feat)
        u = jnp.concatenate([x1, x1, x2, x2, x1, x3], axis=0)
        un[q] = u.astype(bf16)
        o = jnp.broadcast_to(x[:, 0:1], (8, BLK))
        d = x - o

        def rot1(v):
            return jnp.where(row < 2, up(v, 1), jnp.where(row == 2, up(v, 6), 0.0))

        def rot2(v):
            return jnp.where(row < 1, up(v, 2), jnp.where(row < 3, up(v, 7), 0.0))

        cross = rot1(d) * rot2(a) - rot2(d) * rot1(a)
        f = jnp.where(row < 3, a, up(cross, 5))
        f = jnp.where(row < 6, f, 0.0)
        f16 = rows16(f)
        fe[q] = jnp.concatenate([f16, f16], axis=1)
        for i, v in enumerate((o, rot1(o), rot2(o), d)):
            org[q, 8 * i : 8 * i + 8, :] = v
        return carry

    lax.fori_loop(0, nblk, one, 0, unroll=4)


def list_pairs(mine, other, counts, me, nblk, column, box):
    half, cols = mine.shape
    row = lax.broadcasted_iota(jnp.int32, (half, cols), 0)
    big = jnp.int32(2 * half)
    a, b = mine[...], other[...]
    first = jnp.minimum(
        jnp.min(jnp.where(a > 0, row + me * half, big), axis=0, keepdims=True),
        jnp.min(jnp.where(b > 0, row + (1 - me) * half, big), axis=0, keepdims=True),
    )
    number = jnp.sum(a, axis=0, keepdims=True) + jnp.sum(b, axis=0, keepdims=True)
    row8 = rows8(cols)
    alive = counts[...]
    if nblk < cols:
        alive = jnp.concatenate([alive, jnp.zeros((1, cols - nblk), jnp.int32)], axis=1)
    column[...] = jnp.where(row8 == 0, first, jnp.where(row8 == 1, number, alive)).astype(f32).T
    own = column[pl.ds(pl.multiple_of(me * nblk, 8), nblk), :]
    wide = box.shape[1]
    first = jnp.broadcast_to(own[:, 0:1], (nblk, wide))
    number = jnp.broadcast_to(own[:, 1:2], (nblk, wide))
    alive = jnp.broadcast_to(column[0:nblk, 2:3], (nblk, wide))
    before = lax.broadcasted_iota(jnp.int32, (nblk, nblk), 0) > lax.broadcasted_iota(jnp.int32, (nblk, nblk), 1)
    start = jnp.dot(before.astype(f32).astype(bf16), number.astype(bf16), preferred_element_type=f32)
    lane = lax.broadcasted_iota(jnp.int32, (nblk, wide), 1).astype(f32)
    block_of = lax.broadcasted_iota(jnp.int32, (nblk, wide), 0).astype(f32)
    here = (lane >= start) & (lane < start + number)
    particle = jnp.sum(jnp.where(here, block_of, 0.0), axis=0, keepdims=True)
    empty = 2.0 * half
    panel = empty + jnp.sum(jnp.where(here, first + lane - start - empty, 0.0), axis=0, keepdims=True)
    alive = jnp.sum(jnp.where(here, alive, 0.0), axis=0, keepdims=True)
    total = jnp.sum(number, axis=0, keepdims=True)
    row8 = rows8(wide)
    box[...] = jnp.where(row8 == 0, particle, jnp.where(row8 == 1, panel, jnp.where(row8 == 2, alive, total))).astype(jnp.int32)


def each_panel_block(panels, others, me, body):
    many = panels.shape[1] // BLK

    def run(ref, start):
        def one(k, carry):
            body(ref[:, block(k, BLK)], start + k)
            return carry

        lax.fori_loop(0, many, one, 0, unroll=4)

    run(panels, me * many)
    run(others, (1 - me) * many)
    for extra in range(WIN - 1):
        body(jnp.zeros((8, BLK), f32), 2 * many + extra)


def stack6(c1, c2, c3):
    pair = jnp.concatenate([c1, c2], axis=0).astype(bf16)
    return jnp.concatenate([pair, pair, jnp.concatenate([c3, c1], axis=0).astype(bf16)], axis=0)


def apart(a, b):
    none = jnp.zeros(a.shape, a.dtype)
    return jnp.concatenate([jnp.concatenate([a, none], axis=1), jnp.concatenate([none, b], axis=1)], axis=0)


TURN = (((0,), (0,)), ((), ()))


def panel_sums(counts, panels, others, near, near_o, un, fe, org, out, pan, box, v, geo, tot, column, items, sem):
    me = lax.axis_index("panel")
    nblk = un.shape[0]
    list_pairs(near, near_o, counts, me, nblk, column, box)
    copy = pltpu.make_async_copy(box, items, sem)
    copy.start()
    row = rows8(BLK)

    def build(p, at):
        pan[at] = p
        c = jnp.where(row < 3, p, 0.0)
        dist = jnp.where(row < 3, -2.0 * c, jnp.where(row < 6, up(c * c, 5), jnp.where(row == 6, 1.0, 0.0)))
        v[at] = stack6(*split3(dist))
        geo[at, 0:8, :] = jnp.where(row < 2, up(p, 4), jnp.where(row == 2, up(p, 1), jnp.where(row < 6, -p, 0.0)))
        geo[at, 8:16, :] = jnp.where(row < 1, up(p, 5), jnp.where(row < 3, up(p, 2), 0.0))
        geo[at, 16:24, :] = jnp.where(row < 2, up(p, 1), jnp.where(row == 2, up(p, 6), 0.0))
        geo[at, 24:32, :] = jnp.where(row < 1, up(p, 2), jnp.where(row < 3, up(p, 7), 1.0))
        tot[at] = jnp.zeros((8, BLK), f32)

    each_panel_block(panels, others, me, build)
    copy.wait()
    filled = items[3, 0]
    lane = lax.broadcasted_iota(jnp.int32, (16, 2 * BLK), 1) % BLK

    def moments(n):
        qa, qb = items[0, n], items[0, n + 1]
        u = jnp.concatenate([un[qa], un[qb]], axis=0)
        r2 = lax.dot_general(u, apart(v[items[1, n]], v[items[1, n + 1]]), TURN, preferred_element_type=f32)
        inv = lax.rsqrt(r2)
        hi, lo = split2(inv * inv * inv)
        f = [fe[q] * jnp.where(lane < items[2, n + i], 1.0, 0.0).astype(bf16) for i, q in enumerate((qa, qb))]
        return jnp.concatenate(f, axis=0), jnp.concatenate([hi, lo], axis=0)

    def finish(n, g):
        q, at = items[0, n], items[1, n]
        m = geo[at, 0:8, :] * (geo[at, 24:32, :] - org[q, 16:24, :]) - geo[at, 8:16, :] * (geo[at, 16:24, :] - org[q, 8:16, :])
        tot[at] += (g[0:8] + g[8:16]) * m

    def some(i, carry):
        ns = [i * EACH1 + e for e in range(0, EACH1, 2)]
        parts = [moments(n) for n in ns]
        for n, (f, k) in zip(ns, parts):
            g = jnp.dot(f, k, preferred_element_type=f32)
            finish(n, g[0:16, 0:BLK])
            finish(n + 1, g[16:32, BLK:])
        return carry

    lax.fori_loop(0, (filled + EACH1 - 1) // EACH1, some, 0)
    for k in range(out.shape[1] // BLK):
        out[:, k * BLK : (k + 1) * BLK] = -inv_four_pi * jnp.sum(tot[k], axis=0, keepdims=True)


def share(rounds, part, parts):
    return jnp.minimum(rounds, (2 * part * rounds + 2 * parts - 2) // (2 * parts - 1))


def particle_sums(part, parts, build, pan, items, un, v, org, *rest):
    row = rows8(BLK)
    last = part == parts - 1
    if build:
        out, vn = rest[:2]
        earlier = []

        def one_block(k, carry):
            p = pan[k]
            mn3 = jnp.where(row < 3, up(p, 3) * p[7:8, :], 0.0) * 3.0
            c = jnp.where(row < 3, p, 0.0)
            vn[k] = stack6(*split3(jnp.where(row < 3, -mn3, up(mn3 * c, 5))))
            return carry

        lax.fori_loop(0, pan.shape[0], one_block, 0, unroll=2)
    else:
        vn = rest[0]
        earlier, out = (rest[1:-2], rest[-2]) if last else (rest[1:-1], rest[-1])
    total = rest[-1] if last else out
    total[...] = sum((e[...] for e in earlier), jnp.zeros(total.shape, f32))
    listed = items[...]
    filled = listed[3, 0]
    def rows(n):
        p = pan[n[1]]
        d = jnp.where(row < 3, p - org[n[0], 0:8, :], jnp.where(row == 3, 1.0, 0.0))
        mn = jnp.where(row < 3, up(p, 3) * p[7:8], 0.0)
        d16, e16 = rows16(d), rows16(-p[6:7] * d - mn)
        return jnp.concatenate([d16, d16, e16, e16], axis=1)

    def factors(n, m):
        both = [jnp.concatenate([v[at], vn[at]], axis=1) for at in (n[1], m[1])]
        u = apart(un[n[0]], un[m[0]])
        pair = lax.dot_general(jnp.concatenate(both, axis=0), u, TURN, preferred_element_type=f32)
        inv = lax.rsqrt(pair[0:BLK])
        inv2 = inv * inv
        inv3 = inv2 * inv
        t1, t2 = split2(inv3 * (inv2 * pair[BLK:]))
        i1, i2 = split2(inv3)
        return jnp.concatenate([rows(n), rows(m)], axis=0), jnp.concatenate([t1, t2, i1, i2], axis=0)

    def finish(n, h):
        q = n[0]
        h = (h[0:8] + h[8:16]) * inv_four_pi
        total[q] += h - org[q, 24:32, :] * h[3:4]

    def some(i, carry):
        now = pltpu.roll(listed, listed.shape[1] - i * EACH, 1)
        ns = [(now[0, e], now[1, e]) for e in range(EACH)]
        parts = [factors(ns[e], ns[e + 1]) for e in range(0, EACH, 2)]
        for e, (f, k) in zip(range(0, EACH, 2), parts):
            h = jnp.dot(f, k, preferred_element_type=f32)
            finish(ns[e], h[0:16, 0:BLK])
            finish(ns[e + 1], h[16:32, BLK:])
        return carry

    rounds = (filled + EACH - 1) // EACH
    lax.fori_loop(share(rounds, part, parts), share(rounds, part + 1, parts), some, 0)
    if last:
        for q in range(total.shape[0]):
            out[:, q * BLK : (q + 1) * BLK] = total[q, 0:3, :]


def vmem():
    return pl.BlockSpec(memory_space=pltpu.VMEM)


def smem():
    return pl.BlockSpec(memory_space=pltpu.SMEM)


def params(mib=24):
    return pltpu.CompilerParams(vmem_limit_bytes=mib * 1024 * 1024)


def prepare(particles):
    width = particles.shape[1]
    nblk = width // BLK
    return pl.pallas_call(
        particle_features,
        out_shape=(
            jax.ShapeDtypeStruct((nblk, 48, BLK), bf16),
            jax.ShapeDtypeStruct((nblk, 16, 2 * BLK), bf16),
            jax.ShapeDtypeStruct((nblk, 32, BLK), f32),
        ),
        in_specs=[vmem()],
        out_specs=(vmem(),) * 3,
        scratch_shapes=[pltpu.VMEM((8, width), f32)],
        compiler_params=params(),
        cost_estimate=pl.CostEstimate(flops=2 * 10**9, bytes_accessed=10**6, transcendentals=0),
        name="prepare",
    )(particles)


def panel_side(counts, panels, others, near, near_o, un, fe, org):
    npan = 2 * panels.shape[1]
    full = npan // BLK + WIN - 1
    wide = pl.cdiv(WIN * counts.shape[1] + EACH1, BLK) * BLK
    return pl.pallas_call(
        panel_sums,
        out_shape=(
            jax.ShapeDtypeStruct((1, npan), f32),
            jax.ShapeDtypeStruct((full, 8, BLK), f32),
            jax.ShapeDtypeStruct((8, wide), jnp.int32),
            jax.ShapeDtypeStruct((full, 48, BLK), bf16),
        ),
        in_specs=[vmem()] * 8,
        out_specs=(vmem(),) * 4,
        scratch_shapes=[
            pltpu.VMEM((full, 32, BLK), f32),
            pltpu.VMEM((full, 8, BLK), f32),
            pltpu.VMEM((near.shape[1], 8), f32),
            pltpu.SMEM((8, wide), jnp.int32),
            pltpu.SemaphoreType.DMA,
        ],
        compiler_params=params(),
        name="panel_side",
    )(counts, panels, others, near, near_o, un, fe, org)


def particle_side(part, parts, pan, box, un, v, org, vn, earlier):
    build, last = vn is None, part == parts - 1
    sums = (un.shape[0], 8, BLK)
    shape = jax.ShapeDtypeStruct((3, un.shape[0] * BLK) if last else sums, f32)
    args = [pan, box, un, v, org] + ([] if build else [vn]) + list(earlier)
    return pl.pallas_call(
        functools.partial(particle_sums, part, parts, build),
        out_shape=(shape, jax.ShapeDtypeStruct(v.shape, bf16)) if build else shape,
        in_specs=[vmem()] * len(args),
        out_specs=(vmem(), vmem()) if build else vmem(),
        scratch_shapes=[pltpu.VMEM(sums, f32)] if last else [],
        compiler_params=params(),
        cost_estimate=pl.CostEstimate(flops=10**9, bytes_accessed=10**5, transcendentals=0),
        name="particle_side",
    )(*args)


def on_device(dom, panels, particles, counts, near):
    swap = [(0, 1), (1, 0)]
    others = lax.ppermute(panels, "panel", swap)
    near_o = lax.ppermute(near, "panel", swap)
    un, fe, org = prepare(particles)
    total, pan, box, v = panel_side(counts.reshape(1, -1), panels, others, near, near_o, un, fe, org)
    total = total.reshape(total.shape[1])
    steps = [1 << b for b in range((dom - 1).bit_length())]
    parts = len(steps) + 1
    chunks, factors = [], None

    for number, step in enumerate(steps):
        pairs = [(2 * i + c, 2 * (i ^ step) + 1 - c) for i in range(dom) for c in range(2)]
        total, at = lax.optimization_barrier((total, box))
        got = particle_side(number, parts, pan, at, un, v, org, factors, [])
        if factors is None:
            got, factors = got
        arrived, got = lax.optimization_barrier((lax.ppermute(total, ("dom", "panel"), pairs), got))
        chunks.append(got)
        total = total + arrived
    half = total.shape[0] // 2
    me = lax.axis_index("panel")
    total, at = lax.optimization_barrier((total, box))
    velocity = particle_side(parts - 1, parts, pan, at, un, v, org, factors, chunks)
    keep = lax.dynamic_slice(total, (me * half,), (half,))
    give = lax.dynamic_slice(total, ((1 - me) * half,), (half,))
    return keep + lax.ppermute(give, "panel", swap), velocity


def solution(mesh):
    return jax.shard_map(
        functools.partial(on_device, mesh.shape["dom"]),
        mesh=mesh,
        in_specs=(
            P(None, ("groups", "panel")),
            P(None, ("groups", "dom", "panel")),
            P(("groups", "dom", "panel")),
            P(("groups", "panel"), "dom"),
        ),
        out_specs=(P(("groups", "panel")), P(None, ("groups", "dom", "panel"))),
        check_vma=False,
    )
```

time: 25.4 us -> 23.4 us (0.921); the launches traced: 25.7 us -> 23.1 us
  Pallas kernels: 14.9 us -> 13.2 us
  waiting for transfers between devices: 0.52 us -> 0.02 us
  starting transfers between devices: 7.34 us -> 6.88 us
    pallas_call x5, Pallas kernels: 10.7 us -> 9.36 us  [the longest x4 8.62 us: particle_side(): pl.pallas_call(functools.partial(particle_sums, part, parts, build), out_...]
    ppermute x1, starting transfers between devices: 0.59 us -> 0.07 us  [on_device(): return (keep + lax.ppermute(give, 'panel', swap), velocity)]
    ppermute x3, waiting for transfers between devices: 0.51 us -> 0.01 us  [on_device(): lax.ppermute(total, ('dom', 'panel'), pairs)]
    pallas_call x1, Pallas kernels: 4.21 us -> 3.82 us  [panel_side(): pl.pallas_call(panel_sums, out_shape=(jax.ShapeDtypeStruct((1, npan), f32...]
  transfers between devices with their start and end apart: 6 -> 6, of which waited for: 1 -> 0; matrix products, arithmetic and copies ran while one was open for 0% -> 0% of each run, Pallas kernels for 42% -> 41%
where the time goes in v3:
time: 23.4 us; the launch traced here: 23.1 us
  Pallas kernels  13.2 us (56%)
  starting transfers between devices  6.88 us (29%)
  local copies, waits for them, and re-layouts  1.59 us (7%)
  between operations  0.77 us (3%)
  other arithmetic  0.62 us (3%)
    pallas_call x4, Pallas kernels, particle_side(): pl.pallas_call(functools.partial(particle_sums, part, parts, build), out_...  8.62 us
    ppermute x3, starting transfers between devices, on_device(): lax.ppermute(total, ('dom', 'panel'), pairs)  6.22 us
    pallas_call x1, Pallas kernels, panel_side(): pl.pallas_call(panel_sums, out_shape=(jax.ShapeDtypeStruct((1, npan), f32...  3.82 us
    unnamed x8, local copies, waits for them, and re-layouts  1.58 us
    pallas_call x1, Pallas kernels, prepare(): pl.pallas_call(particle_features, out_shape=(jax.ShapeDtypeStruct((nblk,...  0.74 us
    add x1, other arithmetic, on_device(): return (keep + lax.ppermute(give, 'panel', swap), velocity)  0.6 us
    ppermute x1, starting transfers between devices, on_device(): others = lax.ppermute(panels, 'panel', swap)  0.52 us
  transfers between devices with their start and end apart: 6, of which 0 were waited for; matrix products, arithmetic and copies ran while one was open for 0% of the time, Pallas kernels for 41%

profile of v3, /device:TPU:0, one launch (start us, length us, event | category | flops | bytes accessed | tf_op | source)
XLA Modules:
  0.0 23.1 jit_solution(7508636326806716844)
XLA Ops:
  0.6 0.5 %collective-permute-start = (f32[8,2048]{1,0:T(8,128)}, f32[8,2048]{1,0:T(8,128)S(1)}, u32[]{:S(2)}, u32[]{:S(2)}) collective-permute-start(f32[8,2048]{1,0:T(8,128)} %panels.1), channel_id=1, source_target_pairs={{0,1},{1,0},{2,3},{3,2},{4,5},{5,4},{6,7},{7,6},{8,9},{9,8},{10,11... | collective-permute-start | bytes 196616 | tf_op jit(solution)/shard_map/ppermute | solution.py:342
  1.1 0.1 collective-permute-start.1
  1.2 0.0 copy-start.3
  1.2 0.9 %copy-done.3 = f32[6,4096]{1,0:T(8,128)S(1)} copy-done((f32[6,4096]{1,0:T(8,128)S(1)}, f32[6,4096]{1,0:T(8,128)}, u32[]{:S(2)}) %copy-start.3) | copy-done | bytes 98328
  2.1 0.0 copy-start
  2.1 0.7 %prepare.1 = (bf16[32,48,128]{2,1,0:T(8,128)(2,1)S(1)}, bf16[32,16,256]{2,1,0:T(8,128)(2,1)S(1)}, f32[32,32,128]{2,1,0:T(8,128)S(1)}) custom-call(f32[6,4096]{1,0:T(8,128)S(1)} %copy-done.3), custom_call_target="tpu_custom_call" | custom-call | flops 2000000000 | bytes 1000000 | tf_op jit(solution)/shard_map/prepare/pallas_call | solution.py:281
  2.9 0.0 copy-start.1
  2.9 0.0 collective-permute-done.1.near_o
  2.9 0.0 collective-permute-done.others
  2.9 0.0 copy-start.2
  2.9 0.0 copy-done
  3.0 0.6 %copy-done.1 = s32[16,64]{1,0:T(8,128)S(1)} copy-done((s32[16,64]{1,0:T(8,128)S(1)}, s32[16,64]{1,0:T(8,128)}, u32[]{:S(2)}) %copy-start.1) | copy-done | bytes 4120
  3.6 0.0 copy-done.2
  3.6 3.8 %panel_side.1 = (f32[1,4096]{1,0:T(1,128)S(1)}, f32[34,8,128]{2,1,0:T(8,128)S(1)}, s32[8,128]{1,0:T(8,128)S(1)}, bf16[34,48,128]{2,1,0:T(8,128)(2,1)S(1)}) custom-call(s32[1,32]{1,0:T(1,128)S(1)} %bitcast.4, f32[8,2048]{1,0:T(8,128)S(1)} %copy-done, f32[8,2048]{1,0:T(8,128)S(1)} %collective-permute-done.others, s32[16,64]{1,0:T(8,128)S(1)} %copy-done.1, ...), custom_call_target="tpu_custom_call" | custom-call | tf_op jit(solution)/shard_map/panel_side/pallas_call | solution.py:301
  7.4 2.7 %collective-permute-start.2 = (f32[4096]{0:T(1024)S(1)}, f32[4096]{0:T(1024)S(1)}, u32[]{:S(2)}, u32[]{:S(2)}) collective-permute-start(f32[4096]{0:T(1024)S(1)} %bitcast.2), channel_id=1, source_target_pairs={{0,3},{1,2},{2,1},{3,0},{4,7},{5,6},{6,5},{7,4},{8,11},{9,10},{10,... | collective-permute-start | bytes 49160 | tf_op jit(solution)/shard_map/ppermute | solution.py:357
  10.1 2.5 %particle_side.4 = (f32[32,8,128]{2,1,0:T(8,128)S(1)}, bf16[34,48,128]{2,1,0:T(8,128)(2,1)S(1)}) custom-call(f32[34,8,128]{2,1,0:T(8,128)S(1)} %get-tuple-element.31.pan, s32[8,128]{1,0:T(8,128)S(1)} %get-tuple-element.44.items, bf16[32,48,128]{2,1,0:T(8,128)(2,1)S(1)} %get-tuple-element.25.un, bf16[34,48,128]{2,1,0:T(8,128)(2,1)S(1)} %get-tuple-element.33.v, ...), custom_call_target="tpu_custom_call" | custom-call | flops 1000000000 | bytes 100000 | tf_op jit(solution)/shard_map/particle_side/pallas_call | solution.py:328
  12.7 0.0 collective-permute-done.2
  12.7 1.1 %collective-permute-start.3 = (f32[4096]{0:T(1024)S(1)}, f32[4096]{0:T(1024)S(1)}, u32[]{:S(2)}, u32[]{:S(2)}) collective-permute-start(f32[4096]{0:T(1024)S(1)} %add.18), channel_id=1, source_target_pairs={{0,5},{1,4},{2,7},{3,6},{4,1},{5,0},{6,3},{7,2},{8,13},{9,12},{10,... | collective-permute-start | bytes 49160 | tf_op jit(solution)/shard_map/ppermute | solution.py:357
  13.8 2.3 %particle_side.5.rest_2_ = f32[32,8,128]{2,1,0:T(8,128)S(1)} custom-call(f32[34,8,128]{2,1,0:T(8,128)S(1)} %get-tuple-element.31.pan, s32[8,128]{1,0:T(8,128)S(1)} %get-tuple-element.44.items, bf16[32,48,128]{2,1,0:T(8,128)(2,1)S(1)} %get-tuple-element.25.un, bf16[34,48,128]{2,1,0:T(8,128)(2,1)S(1)} %get-tuple-element.33.v, ...), custom_call_target="tpu_custom_call" | custom-call | flops 1000000000 | bytes 100000 | tf_op jit(solution)/shard_map/particle_side/pallas_call | solution.py:328
  16.1 0.0 collective-permute-done.3
  16.1 2.4 %collective-permute-start.4 = (f32[4096]{0:T(1024)S(1)}, f32[4096]{0:T(1024)S(1)}, u32[]{:S(2)}, u32[]{:S(2)}) collective-permute-start(f32[4096]{0:T(1024)S(1)} %add.19), channel_id=1, source_target_pairs={{0,9},{1,8},{2,11},{3,10},{4,13},{5,12},{6,15},{7,14},{8,1},{9,0},... | collective-permute-start | bytes 49160 | tf_op jit(solution)/shard_map/ppermute | solution.py:357
  18.5 2.3 %particle_side.6.rest_3_ = f32[32,8,128]{2,1,0:T(8,128)S(1)} custom-call(f32[34,8,128]{2,1,0:T(8,128)S(1)} %get-tuple-element.31.pan, s32[8,128]{1,0:T(8,128)S(1)} %get-tuple-element.44.items, bf16[32,48,128]{2,1,0:T(8,128)(2,1)S(1)} %get-tuple-element.25.un, bf16[34,48,128]{2,1,0:T(8,128)(2,1)S(1)} %get-tuple-element.33.v, ...), custom_call_target="tpu_custom_call" | custom-call | flops 1000000000 | bytes 100000 | tf_op jit(solution)/shard_map/particle_side/pallas_call | solution.py:328
  20.9 0.0 collective-permute-done.4
  20.9 0.1 collective-permute-start.5
  21.0 1.5 %particle_side.7 = f32[3,4096]{1,0:T(4,128)} custom-call(f32[34,8,128]{2,1,0:T(8,128)S(1)} %get-tuple-element.31.pan, s32[8,128]{1,0:T(8,128)S(1)} %get-tuple-element.44.items, bf16[32,48,128]{2,1,0:T(8,128)(2,1)S(1)} %get-tuple-element.25.un, bf16[34,48,128]{2,1,0:T(8,128)(2,1)S(1)} %get-tuple-element.33.v, f32[32,32,128]{2,1,0:T(8,128)S(1)} %get-tuple-element.27.org, ...), custom_call_target="tpu_custom_call" | custom-call | flops 1000000000 | bytes 100000 | tf_op jit(solution)/shard_map/particle_side/pallas_call | solution.py:328
  22.5 0.0 collective-permute-done.5
  22.5 0.6 %dynamic-slice_add_fusion = f32[2048]{0:T(1024)} fusion(f32[2048]{0:T(1024)S(1)} %collective-permute-done.5, f32[4096]{0:T(1024)S(1)} %add.20, s32[]{:T(128)S(6)} %select_n.6), kind=kLoop, calls=%fused_computation | loop fusion | flops 2048 | bytes 24580 | tf_op jit(solution)/shard_map/add | solution.py:366
  (4 shorter events, 0.0 us)
Async XLA Ops:
  0.6 2.3 %collective-permute-start = (f32[8,2048]{1,0:T(8,128)}, f32[8,2048]{1,0:T(8,128)S(1)}, u32[]{:S(2)}, u32[]{:S(2)}) collective-permute-start(f32[8,2048]{1,0:T(8,128)} %panels.1), channel_id=1, source_target_pairs={{0,1},{1,0},{2,3},{3,2},{4,5},{5,4},{6,7},{7,6},{8,9},{9,8},{10,11... | collective-permute-start | bytes 196616 | tf_op jit(solution)/shard_map/ppermute | solution.py:342
  1.1 1.7 %collective-permute-start.1 = (s32[16,64]{1,0:T(8,128)}, s32[16,64]{1,0:T(8,128)S(1)}, u32[]{:S(2)}, u32[]{:S(2)}) collective-permute-start(s32[16,64]{1,0:T(8,128)} %near.1), channel_id=1, source_target_pairs={{0,1},{1,0},{2,3},{3,2},{4,5},{5,4},{6,7},{7,6},{8,9},{9,8},{10,11... | collective-permute-start | bytes 12296 | tf_op jit(solution)/shard_map/ppermute | solution.py:343
  1.2 0.9 %copy-start.3 = (f32[6,4096]{1,0:T(8,128)S(1)}, f32[6,4096]{1,0:T(8,128)}, u32[]{:S(2)}) copy-start(f32[6,4096]{1,0:T(8,128)} %particles.1) | copy-start | bytes 294916
  2.1 0.8 %copy-start = (f32[8,2048]{1,0:T(8,128)S(1)}, f32[8,2048]{1,0:T(8,128)}, u32[]{:S(2)}) copy-start(f32[8,2048]{1,0:T(8,128)} %panels.1) | copy-start | bytes 196612
  2.9 0.7 %copy-start.1 = (s32[16,64]{1,0:T(8,128)S(1)}, s32[16,64]{1,0:T(8,128)}, u32[]{:S(2)}) copy-start(s32[16,64]{1,0:T(8,128)} %near.1) | copy-start | bytes 12292
  2.9 0.7 %copy-start.2 = (s32[32]{0:T(128)S(1)}, s32[32]{0:T(128)}, u32[]{:S(2)}) copy-start(s32[32]{0:T(128)} %param.6) | copy-start | bytes 388
  7.4 5.2 %collective-permute-start.2 = (f32[4096]{0:T(1024)S(1)}, f32[4096]{0:T(1024)S(1)}, u32[]{:S(2)}, u32[]{:S(2)}) collective-permute-start(f32[4096]{0:T(1024)S(1)} %bitcast.2), channel_id=1, source_target_pairs={{0,3},{1,2},{2,1},{3,0},{4,7},{5,6},{6,5},{7,4},{8,11},{9,10},{10,... | collective-permute-start | bytes 49160 | tf_op jit(solution)/shard_map/ppermute | solution.py:357
  12.7 3.4 %collective-permute-start.3 = (f32[4096]{0:T(1024)S(1)}, f32[4096]{0:T(1024)S(1)}, u32[]{:S(2)}, u32[]{:S(2)}) collective-permute-start(f32[4096]{0:T(1024)S(1)} %add.18), channel_id=1, source_target_pairs={{0,5},{1,4},{2,7},{3,6},{4,1},{5,0},{6,3},{7,2},{8,13},{9,12},{10,... | collective-permute-start | bytes 49160 | tf_op jit(solution)/shard_map/ppermute | solution.py:357
  16.1 4.7 %collective-permute-start.4 = (f32[4096]{0:T(1024)S(1)}, f32[4096]{0:T(1024)S(1)}, u32[]{:S(2)}, u32[]{:S(2)}) collective-permute-start(f32[4096]{0:T(1024)S(1)} %add.19), channel_id=1, source_target_pairs={{0,9},{1,8},{2,11},{3,10},{4,13},{5,12},{6,15},{7,14},{8,1},{9,0},... | collective-permute-start | bytes 49160 | tf_op jit(solution)/shard_map/ppermute | solution.py:357
  20.9 1.6 %collective-permute-start.5 = (f32[2048]{0:T(1024)S(1)}, f32[2048]{0:T(1024)S(1)}, u32[]{:S(2)}, u32[]{:S(2)}) collective-permute-start(f32[2048]{0:T(1024)S(1)} %dynamic_slice.7), channel_id=1, source_target_pairs={{0,1},{1,0},{2,3},{3,2},{4,5},{5,4},{6,7},{7,6},{8,9},{9,8},{10,11... | collective-permute-start | bytes 24584 | tf_op jit(solution)/shard_map/ppermute | solution.py:366

commit v4 on v3

--- a/solution.py
+++ b/solution.py
@@ -145,7 +145,7 @@
 TURN = (((0,), (0,)), ((), ()))
 
 
-def panel_sums(counts, panels, others, near, near_o, un, fe, org, out, pan, box, v, geo, tot, column, items, sem):
+def panel_sums(counts, panels, others, near, near_o, un, fe, org, out, pan, box, v, vn, geo, tot, column, items, sem):
     me = lax.axis_index("panel")
     nblk = un.shape[0]
     list_pairs(near, near_o, counts, me, nblk, column, box)
@@ -158,6 +158,8 @@
         c = jnp.where(row < 3, p, 0.0)
         dist = jnp.where(row < 3, -2.0 * c, jnp.where(row < 6, up(c * c, 5), jnp.where(row == 6, 1.0, 0.0)))
         v[at] = stack6(*split3(dist))
+        mn3 = jnp.where(row < 3, up(p, 3) * p[7:8, :], 0.0) * 3.0
+        vn[at] = stack6(*split3(jnp.where(row < 3, -mn3, up(mn3 * c, 5))))
         geo[at, 0:8, :] = jnp.where(row < 2, up(p, 4), jnp.where(row == 2, up(p, 1), jnp.where(row < 6, -p, 0.0)))
         geo[at, 8:16, :] = jnp.where(row < 1, up(p, 5), jnp.where(row < 3, up(p, 2), 0.0))
         geo[at, 16:24, :] = jnp.where(row < 2, up(p, 1), jnp.where(row == 2, up(p, 6), 0.0))
@@ -201,26 +203,10 @@
     return jnp.minimum(rounds, (2 * part * rounds + 2 * parts - 2) // (2 * parts - 1))
 
 
-def particle_sums(part, parts, build, pan, items, un, v, org, *rest):
+def particle_sums(part, parts, pan, items, un, v, vn, org, *rest):
     row = rows8(BLK)
-    last = part == parts - 1
-    if build:
-        out, vn = rest[:2]
-        earlier = []
-
-        def one_block(k, carry):
-            p = pan[k]
-            mn3 = jnp.where(row < 3, up(p, 3) * p[7:8, :], 0.0) * 3.0
-            c = jnp.where(row < 3, p, 0.0)
-            vn[k] = stack6(*split3(jnp.where(row < 3, -mn3, up(mn3 * c, 5))))
-            return carry
-
-        lax.fori_loop(0, pan.shape[0], one_block, 0, unroll=2)
-    else:
-        vn = rest[0]
-        earlier, out = (rest[1:-2], rest[-2]) if last else (rest[1:-1], rest[-1])
-    total = rest[-1] if last else out
-    total[...] = sum((e[...] for e in earlier), jnp.zeros(total.shape, f32))
+    total, = rest
+    total[...] = jnp.zeros(total.shape, f32)
     listed = items[...]
     filled = listed[3, 0]
     def rows(n):
@@ -258,9 +244,15 @@
 
     rounds = (filled + EACH - 1) // EACH
     lax.fori_loop(share(rounds, part, parts), share(rounds, part + 1, parts), some, 0)
-    if last:
-        for q in range(total.shape[0]):
-            out[:, q * BLK : (q + 1) * BLK] = total[q, 0:3, :]
+
+
+def last_sums(total, arrived, *rest):
+    pieces, (normal, velocity) = rest[:-2], rest[-2:]
+    half = normal.shape[1]
+    me = lax.axis_index("panel")
+    normal[...] = total[:, pl.ds(pl.multiple_of(me * half, half), half)] + arrived[...]
+    for q in range(pieces[0].shape[0]):
+        velocity[:, q * BLK : (q + 1) * BLK] = sum(p[q] for p in pieces)[0:3]
 
 
 def vmem():
@@ -305,9 +297,10 @@
             jax.ShapeDtypeStruct((full, 8, BLK), f32),
             jax.ShapeDtypeStruct((8, wide), jnp.int32),
             jax.ShapeDtypeStruct((full, 48, BLK), bf16),
+            jax.ShapeDtypeStruct((full, 48, BLK), bf16),
         ),
         in_specs=[vmem()] * 8,
-        out_specs=(vmem(),) * 4,
+        out_specs=(vmem(),) * 5,
         scratch_shapes=[
             pltpu.VMEM((full, 32, BLK), f32),
             pltpu.VMEM((full, 8, BLK), f32),
@@ -320,21 +313,32 @@
     )(counts, panels, others, near, near_o, un, fe, org)
 
 
-def particle_side(part, parts, pan, box, un, v, org, vn, earlier):
-    build, last = vn is None, part == parts - 1
-    sums = (un.shape[0], 8, BLK)
-    shape = jax.ShapeDtypeStruct((3, un.shape[0] * BLK) if last else sums, f32)
-    args = [pan, box, un, v, org] + ([] if build else [vn]) + list(earlier)
+def particle_side(part, parts, pan, box, un, v, vn, org):
     return pl.pallas_call(
-        functools.partial(particle_sums, part, parts, build),
-        out_shape=(shape, jax.ShapeDtypeStruct(v.shape, bf16)) if build else shape,
-        in_specs=[vmem()] * len(args),
-        out_specs=(vmem(), vmem()) if build else vmem(),
-        scratch_shapes=[pltpu.VMEM(sums, f32)] if last else [],
+        functools.partial(particle_sums, part, parts),
+        out_shape=jax.ShapeDtypeStruct((un.shape[0], 8, BLK), f32),
+        in_specs=[vmem()] * 6,
+        out_specs=vmem(),
         compiler_params=params(),
         cost_estimate=pl.CostEstimate(flops=10**9, bytes_accessed=10**5, transcendentals=0),
         name="particle_side",
-    )(*args)
+    )(pan, box, un, v, vn, org)
+
+
+def close(total, arrived, pieces):
+    half = arrived.shape[0]
+    normal, velocity = pl.pallas_call(
+        last_sums,
+        out_shape=(
+            jax.ShapeDtypeStruct((1, half), f32),
+            jax.ShapeDtypeStruct((3, pieces[0].shape[0] * BLK), f32),
+        ),
+        in_specs=[vmem()] * (2 + len(pieces)),
+        out_specs=(vmem(), vmem()),
+        compiler_params=params(),
+        name="close",
+    )(total.reshape(1, -1), arrived.reshape(1, -1), *pieces)
+    return normal.reshape(half), velocity
 
 
 def on_device(dom, panels, particles, counts, near):
@@ -342,28 +346,25 @@
     others = lax.ppermute(panels, "panel", swap)
     near_o = lax.ppermute(near, "panel", swap)
     un, fe, org = prepare(particles)
-    total, pan, box, v = panel_side(counts.reshape(1, -1), panels, others, near, near_o, un, fe, org)
+    total, pan, box, v, vn = panel_side(counts.reshape(1, -1), panels, others, near, near_o, un, fe, org)
     total = total.reshape(total.shape[1])
     steps = [1 << b for b in range((dom - 1).bit_length())]
     parts = len(steps) + 1
-    chunks, factors = [], None
+    chunks = []
 
     for number, step in enumerate(steps):
         pairs = [(2 * i + c, 2 * (i ^ step) + 1 - c) for i in range(dom) for c in range(2)]
         total, at = lax.optimization_barrier((total, box))
-        got = particle_side(number, parts, pan, at, un, v, org, factors, [])
-        if factors is None:
-            got, factors = got
+        got = particle_side(number, parts, pan, at, un, v, vn, org)
         arrived, got = lax.optimization_barrier((lax.ppermute(total, ("dom", "panel"), pairs), got))
         chunks.append(got)
         total = total + arrived
     half = total.shape[0] // 2
     me = lax.axis_index("panel")
     total, at = lax.optimization_barrier((total, box))
-    velocity = particle_side(parts - 1, parts, pan, at, un, v, org, factors, chunks)
-    keep = lax.dynamic_slice(total, (me * half,), (half,))
+    chunks.append(particle_side(parts - 1, parts, pan, at, un, v, vn, org))
     give = lax.dynamic_slice(total, ((1 - me) * half,), (half,))
-    return keep + lax.ppermute(give, "panel", swap), velocity
+    return close(total, lax.ppermute(give, "panel", swap), chunks)
 
 
 def solution(mesh):

time: 23.4 us -> 22.7 us (0.970)
  waiting for transfers between devices: 0.02 us -> 1.09 us
  Pallas kernels: 13.2 us -> 12.2 us
  other arithmetic: 0.62 us -> 0.02 us
    pallas_call x4 -> x5, Pallas kernels: 8.62 us -> 7.62 us  [the longest x4 6.96 us: particle_side(): pl.pallas_call(functools.partial(particle_sums, part, parts), out_shape=j...]
    ppermute x3, waiting for transfers between devices: 0.01 us -> 0.74 us  [on_device(): lax.ppermute(total, ('dom', 'panel'), pairs)]
    add x1 -> x0, other arithmetic: 0.6 us -> none  [on_device(): return (keep + lax.ppermute(give, 'panel', swap), velocity)]
    ppermute x1, waiting for transfers between devices: 0.01 us -> 0.35 us  [on_device(): return close(total, lax.ppermute(give, 'panel', swap), chunks)]
  transfers between devices with their start and end apart: 6 -> 6, of which waited for: 0 -> 2; matrix products, arithmetic and copies ran while one was open for 0% -> 0% of each run, Pallas kernels for 41% -> 34%
where the time goes in v4:
time: 22.7 us; the launch traced here: 22.4 us
  Pallas kernels  12.2 us (54%)
  starting transfers between devices  6.82 us (30%)
  local copies, waits for them, and re-layouts  1.58 us (7%)
  waiting for transfers between devices  1.09 us (5%)
  between operations  0.75 us (3%)
    pallas_call x4, Pallas kernels, particle_side(): pl.pallas_call(functools.partial(particle_sums, part, parts), out_shape=j...  6.96 us
    ppermute x3, starting transfers between devices, on_device(): lax.ppermute(total, ('dom', 'panel'), pairs)  6.23 us
    pallas_call x1, Pallas kernels, panel_side(): pl.pallas_call(panel_sums, out_shape=(jax.ShapeDtypeStruct((1, npan), f32...  3.82 us
    unnamed x8, local copies, waits for them, and re-layouts  1.58 us
    ppermute x3, waiting for transfers between devices, on_device(): lax.ppermute(total, ('dom', 'panel'), pairs)  0.74 us
    pallas_call x1, Pallas kernels, prepare(): pl.pallas_call(particle_features, out_shape=(jax.ShapeDtypeStruct((nblk,...  0.74 us
    pallas_call x1, Pallas kernels, close(): pl.pallas_call(last_sums, out_shape=(jax.ShapeDtypeStruct((1, half), f32)...  0.66 us
    ppermute x1, starting transfers between devices, on_device(): others = lax.ppermute(panels, 'panel', swap)  0.52 us
  transfers between devices with their start and end apart: 6, of which 2 were waited for; matrix products, arithmetic and copies ran while one was open for 0% of the time, Pallas kernels for 34%

profile of v4, /device:TPU:0, one launch (start us, length us, event | category | flops | bytes accessed | tf_op | source)
XLA Modules:
  0.0 22.4 jit_solution(13309948779343699242)
XLA Ops:
  0.6 0.5 %collective-permute-start = (f32[8,2048]{1,0:T(8,128)}, f32[8,2048]{1,0:T(8,128)S(1)}, u32[]{:S(2)}, u32[]{:S(2)}) collective-permute-start(f32[8,2048]{1,0:T(8,128)} %panels.1), channel_id=1, source_target_pairs={{0,1},{1,0},{2,3},{3,2},{4,5},{5,4},{6,7},{7,6},{8,9},{9,8},{10,11... | collective-permute-start | bytes 196616 | tf_op jit(solution)/shard_map/ppermute | solution.py:346
  1.1 0.1 collective-permute-start.1
  1.2 0.0 copy-start.3
  1.2 0.9 %copy-done.3 = f32[6,4096]{1,0:T(8,128)S(1)} copy-done((f32[6,4096]{1,0:T(8,128)S(1)}, f32[6,4096]{1,0:T(8,128)}, u32[]{:S(2)}) %copy-start.3) | copy-done | bytes 98328
  2.1 0.0 copy-start
  2.1 0.7 %prepare.1 = (bf16[32,48,128]{2,1,0:T(8,128)(2,1)S(1)}, bf16[32,16,256]{2,1,0:T(8,128)(2,1)S(1)}, f32[32,32,128]{2,1,0:T(8,128)S(1)}) custom-call(f32[6,4096]{1,0:T(8,128)S(1)} %copy-done.3), custom_call_target="tpu_custom_call" | custom-call | flops 2000000000 | bytes 1000000 | tf_op jit(solution)/shard_map/prepare/pallas_call | solution.py:273
  2.9 0.0 copy-start.1
  2.9 0.0 collective-permute-done.1.near_o
  2.9 0.0 collective-permute-done.others
  2.9 0.0 copy-start.2
  2.9 0.0 copy-done
  3.0 0.6 %copy-done.1 = s32[16,64]{1,0:T(8,128)S(1)} copy-done((s32[16,64]{1,0:T(8,128)S(1)}, s32[16,64]{1,0:T(8,128)}, u32[]{:S(2)}) %copy-start.1) | copy-done | bytes 4120
  3.6 0.0 copy-done.2
  3.6 3.8 %panel_side.1 = (f32[1,4096]{1,0:T(1,128)S(1)}, f32[34,8,128]{2,1,0:T(8,128)S(1)}, s32[8,128]{1,0:T(8,128)S(1)}, bf16[34,48,128]{2,1,0:T(8,128)(2,1)S(1)}, bf16[34,48,128]{2,1,0:T(8,128)(2,1)S(1)}) custom-call(s32[1,32]{1,0:T(1,128)S(1)} %bitcast.9, f32[8,2048]{1,0:T(8,128)S(1)} %copy-done, f32[8,2048]{1,0:T(8,128)S(1)} %collective-permute-done.others, ...), custom_call_target="tpu_custom_call" | custom-call | tf_op jit(solution)/shard_map/panel_side/pallas_call | solution.py:293
  7.4 2.1 %collective-permute-start.2 = (f32[4096]{0:T(1024)S(1)}, f32[4096]{0:T(1024)S(1)}, u32[]{:S(2)}, u32[]{:S(2)}) collective-permute-start(f32[4096]{0:T(1024)S(1)} %bitcast.6), channel_id=1, source_target_pairs={{0,3},{1,2},{2,1},{3,0},{4,7},{5,6},{6,5},{7,4},{8,11},{9,10},{10,... | collective-permute-start | bytes 49160 | tf_op jit(solution)/shard_map/ppermute | solution.py:359
  9.5 2.3 %particle_side.4.rest_0_ = f32[32,8,128]{2,1,0:T(8,128)S(1)} custom-call(f32[34,8,128]{2,1,0:T(8,128)S(1)} %get-tuple-element.32.pan, s32[8,128]{1,0:T(8,128)S(1)} %get-tuple-element.47.items, bf16[32,48,128]{2,1,0:T(8,128)(2,1)S(1)} %get-tuple-element.26.un, bf16[34,48,128]{2,1,0:T(8,128)(2,1)S(1)} %get-tuple-element.34.v, ...), custom_call_target="tpu_custom_call" | custom-call | flops 1000000000 | bytes 100000 | tf_op jit(solution)/shard_map/particle_side/pallas_call | solution.py:317
  11.9 0.0 collective-permute-done.2
  11.9 2.2 %collective-permute-start.3 = (f32[4096]{0:T(1024)S(1)}, f32[4096]{0:T(1024)S(1)}, u32[]{:S(2)}, u32[]{:S(2)}) collective-permute-start(f32[4096]{0:T(1024)S(1)} %add.12), channel_id=1, source_target_pairs={{0,5},{1,4},{2,7},{3,6},{4,1},{5,0},{6,3},{7,2},{8,13},{9,12},{10,... | collective-permute-start | bytes 49160 | tf_op jit(solution)/shard_map/ppermute | solution.py:359
  14.1 2.3 %particle_side.5.rest_1_ = f32[32,8,128]{2,1,0:T(8,128)S(1)} custom-call(f32[34,8,128]{2,1,0:T(8,128)S(1)} %get-tuple-element.32.pan, s32[8,128]{1,0:T(8,128)S(1)} %get-tuple-element.47.items, bf16[32,48,128]{2,1,0:T(8,128)(2,1)S(1)} %get-tuple-element.26.un, bf16[34,48,128]{2,1,0:T(8,128)(2,1)S(1)} %get-tuple-element.34.v, ...), custom_call_target="tpu_custom_call" | custom-call | flops 1000000000 | bytes 100000 | tf_op jit(solution)/shard_map/particle_side/pallas_call | solution.py:317
  16.4 0.0 collective-permute-done.3
  16.5 1.9 %collective-permute-start.4 = (f32[4096]{0:T(1024)S(1)}, f32[4096]{0:T(1024)S(1)}, u32[]{:S(2)}, u32[]{:S(2)}) collective-permute-start(f32[4096]{0:T(1024)S(1)} %add.13), channel_id=1, source_target_pairs={{0,9},{1,8},{2,11},{3,10},{4,13},{5,12},{6,15},{7,14},{8,1},{9,0},... | collective-permute-start | bytes 49160 | tf_op jit(solution)/shard_map/ppermute | solution.py:359
  18.3 1.6 %particle_side.6.rest_2_ = f32[32,8,128]{2,1,0:T(8,128)S(1)} custom-call(f32[34,8,128]{2,1,0:T(8,128)S(1)} %get-tuple-element.32.pan, s32[8,128]{1,0:T(8,128)S(1)} %get-tuple-element.47.items, bf16[32,48,128]{2,1,0:T(8,128)(2,1)S(1)} %get-tuple-element.26.un, bf16[34,48,128]{2,1,0:T(8,128)(2,1)S(1)} %get-tuple-element.34.v, ...), custom_call_target="tpu_custom_call" | custom-call | flops 1000000000 | bytes 100000 | tf_op jit(solution)/shard_map/particle_side/pallas_call | solution.py:317
  19.9 0.7 %collective-permute-done.4 = f32[4096]{0:T(1024)S(1)} collective-permute-done((f32[4096]{0:T(1024)S(1)}, f32[4096]{0:T(1024)S(1)}, u32[]{:S(2)}, u32[]{:S(2)}) %collective-permute-start.4) | collective-permute-done | bytes 16416 | tf_op jit(solution)/shard_map/ppermute | solution.py:359
  20.6 0.0 collective-permute-start.5
  20.6 0.8 %particle_side.7.rest_3_ = f32[32,8,128]{2,1,0:T(8,128)S(1)} custom-call(f32[34,8,128]{2,1,0:T(8,128)S(1)} %get-tuple-element.32.pan, s32[8,128]{1,0:T(8,128)S(1)} %get-tuple-element.47.items, bf16[32,48,128]{2,1,0:T(8,128)(2,1)S(1)} %get-tuple-element.26.un, bf16[34,48,128]{2,1,0:T(8,128)(2,1)S(1)} %get-tuple-element.34.v, ...), custom_call_target="tpu_custom_call" | custom-call | flops 1000000000 | bytes 100000 | tf_op jit(solution)/shard_map/particle_side/pallas_call | solution.py:317
  21.4 0.4 %collective-permute-done.5 = f32[2048]{0:T(1024)S(1)} collective-permute-done((f32[2048]{0:T(1024)S(1)}, f32[2048]{0:T(1024)S(1)}, u32[]{:S(2)}, u32[]{:S(2)}) %collective-permute-start.5) | collective-permute-done | bytes 8224 | tf_op jit(solution)/shard_map/ppermute | solution.py:367
  21.8 0.7 %close.1 = (f32[1,2048]{1,0:T(1,128)}, f32[3,4096]{1,0:T(4,128)}) custom-call(f32[1,4096]{1,0:T(1,128)S(1)} %bitcast.5, f32[1,2048]{1,0:T(1,128)S(1)} %bitcast.8, f32[32,8,128]{2,1,0:T(8,128)S(1)} %particle_side.4.rest_0_, f32[32,8,128]{2,1,0:T(8,128)S(1)} %particle_side.5.rest_1_, f32[32,8,128]{2,1,0:T(8,128)S(1)} %particle_side.6.rest_2_, ...), custom_call_target="tpu_custom_call" | custom-call | tf_op jit(solution)/shard_map/close/pallas_call | solution.py:330
  (4 shorter events, 0.0 us)
Async XLA Ops:
  0.6 2.3 %collective-permute-start = (f32[8,2048]{1,0:T(8,128)}, f32[8,2048]{1,0:T(8,128)S(1)}, u32[]{:S(2)}, u32[]{:S(2)}) collective-permute-start(f32[8,2048]{1,0:T(8,128)} %panels.1), channel_id=1, source_target_pairs={{0,1},{1,0},{2,3},{3,2},{4,5},{5,4},{6,7},{7,6},{8,9},{9,8},{10,11... | collective-permute-start | bytes 196616 | tf_op jit(solution)/shard_map/ppermute | solution.py:346
  1.1 1.7 %collective-permute-start.1 = (s32[16,64]{1,0:T(8,128)}, s32[16,64]{1,0:T(8,128)S(1)}, u32[]{:S(2)}, u32[]{:S(2)}) collective-permute-start(s32[16,64]{1,0:T(8,128)} %near.1), channel_id=1, source_target_pairs={{0,1},{1,0},{2,3},{3,2},{4,5},{5,4},{6,7},{7,6},{8,9},{9,8},{10,11... | collective-permute-start | bytes 12296 | tf_op jit(solution)/shard_map/ppermute | solution.py:347
  1.2 0.9 %copy-start.3 = (f32[6,4096]{1,0:T(8,128)S(1)}, f32[6,4096]{1,0:T(8,128)}, u32[]{:S(2)}) copy-start(f32[6,4096]{1,0:T(8,128)} %particles.1) | copy-start | bytes 294916
  2.1 0.8 %copy-start = (f32[8,2048]{1,0:T(8,128)S(1)}, f32[8,2048]{1,0:T(8,128)}, u32[]{:S(2)}) copy-start(f32[8,2048]{1,0:T(8,128)} %panels.1) | copy-start | bytes 196612
  2.9 0.7 %copy-start.1 = (s32[16,64]{1,0:T(8,128)S(1)}, s32[16,64]{1,0:T(8,128)}, u32[]{:S(2)}) copy-start(s32[16,64]{1,0:T(8,128)} %near.1) | copy-start | bytes 12292
  2.9 0.7 %copy-start.2 = (s32[32]{0:T(128)S(1)}, s32[32]{0:T(128)}, u32[]{:S(2)}) copy-start(s32[32]{0:T(128)} %param.6) | copy-start | bytes 388
  7.4 4.4 %collective-permute-start.2 = (f32[4096]{0:T(1024)S(1)}, f32[4096]{0:T(1024)S(1)}, u32[]{:S(2)}, u32[]{:S(2)}) collective-permute-start(f32[4096]{0:T(1024)S(1)} %bitcast.6), channel_id=1, source_target_pairs={{0,3},{1,2},{2,1},{3,0},{4,7},{5,6},{6,5},{7,4},{8,11},{9,10},{10,... | collective-permute-start | bytes 49160 | tf_op jit(solution)/shard_map/ppermute | solution.py:359
  11.9 4.6 %collective-permute-start.3 = (f32[4096]{0:T(1024)S(1)}, f32[4096]{0:T(1024)S(1)}, u32[]{:S(2)}, u32[]{:S(2)}) collective-permute-start(f32[4096]{0:T(1024)S(1)} %add.12), channel_id=1, source_target_pairs={{0,5},{1,4},{2,7},{3,6},{4,1},{5,0},{6,3},{7,2},{8,13},{9,12},{10,... | collective-permute-start | bytes 49160 | tf_op jit(solution)/shard_map/ppermute | solution.py:359
  16.5 4.1 %collective-permute-start.4 = (f32[4096]{0:T(1024)S(1)}, f32[4096]{0:T(1024)S(1)}, u32[]{:S(2)}, u32[]{:S(2)}) collective-permute-start(f32[4096]{0:T(1024)S(1)} %add.13), channel_id=1, source_target_pairs={{0,9},{1,8},{2,11},{3,10},{4,13},{5,12},{6,15},{7,14},{8,1},{9,0},... | collective-permute-start | bytes 49160 | tf_op jit(solution)/shard_map/ppermute | solution.py:359
  20.6 1.2 %collective-permute-start.5 = (f32[2048]{0:T(1024)S(1)}, f32[2048]{0:T(1024)S(1)}, u32[]{:S(2)}, u32[]{:S(2)}) collective-permute-start(f32[2048]{0:T(1024)S(1)} %dynamic_slice.3), channel_id=1, source_target_pairs={{0,1},{1,0},{2,3},{3,2},{4,5},{5,4},{6,7},{7,6},{8,9},{9,8},{10,11... | collective-permute-start | bytes 24584 | tf_op jit(solution)/shard_map/ppermute | solution.py:367

commit v5 on v4

--- a/solution.py
+++ b/solution.py
@@ -11,8 +11,8 @@
 inv_four_pi = 0.07957747154594767
 BLK = 128
 WIN = 3
-EACH1 = 16
-EACH = 8
+EACH1 = 20
+EACH = 10
 bf16 = jnp.bfloat16
 f32 = jnp.float32
 
@@ -200,7 +200,7 @@
 
 
 def share(rounds, part, parts):
-    return jnp.minimum(rounds, (2 * part * rounds + 2 * parts - 2) // (2 * parts - 1))
+    return jnp.minimum(rounds, (part * rounds + parts - 1) // parts)
 
 
 def particle_sums(part, parts, pan, items, un, v, vn, org, *rest):

time: 22.7 us -> 21.2 us (0.934)
  Pallas kernels: 12.2 us -> 10.7 us
  starting transfers between devices: 6.82 us -> 7.84 us
  waiting for transfers between devices: 1.09 us -> 0.1 us
    pallas_call x4, Pallas kernels: 6.96 us -> 5.77 us  [particle_side(): pl.pallas_call(functools.partial(particle_sums, part, parts), out_shape=j...]
    ppermute x3, waiting for transfers between devices: 0.74 us -> 0.01 us  [on_device(): lax.ppermute(total, ('dom', 'panel'), pairs)]
    ppermute x3, starting transfers between devices: 6.23 us -> 6.95 us  [on_device(): lax.ppermute(total, ('dom', 'panel'), pairs)]
    pallas_call x1, Pallas kernels: 3.82 us -> 3.52 us  [panel_side(): pl.pallas_call(panel_sums, out_shape=(jax.ShapeDtypeStruct((1, npan), f32...]
    ppermute x1, starting transfers between devices: 0.01 us -> 0.3 us  [on_device(): return close(total, lax.ppermute(give, 'panel', swap), chunks)]
    ppermute x1, waiting for transfers between devices: 0.35 us -> 0.08 us  [on_device(): return close(total, lax.ppermute(give, 'panel', swap), chunks)]
  transfers between devices with their start and end apart: 6 -> 6, of which waited for: 2 -> 1; matrix products, arithmetic and copies ran while one was open for 0% -> 0% of each run, Pallas kernels for 34% -> 31%
where the time goes in v5:
time: 21.2 us; the launch traced here: 21 us
  Pallas kernels  10.7 us (50%)
  starting transfers between devices  7.84 us (37%)
  local copies, waits for them, and re-layouts  1.59 us (8%)
  between operations  0.77 us (4%)
    ppermute x3, starting transfers between devices, on_device(): lax.ppermute(total, ('dom', 'panel'), pairs)  6.95 us
    pallas_call x4, Pallas kernels, particle_side(): pl.pallas_call(functools.partial(particle_sums, part, parts), out_shape=j...  5.77 us
    pallas_call x1, Pallas kernels, panel_side(): pl.pallas_call(panel_sums, out_shape=(jax.ShapeDtypeStruct((1, npan), f32...  3.52 us
    unnamed x8, local copies, waits for them, and re-layouts  1.58 us
    pallas_call x1, Pallas kernels, prepare(): pl.pallas_call(particle_features, out_shape=(jax.ShapeDtypeStruct((nblk,...  0.74 us
    pallas_call x1, Pallas kernels, close(): pl.pallas_call(last_sums, out_shape=(jax.ShapeDtypeStruct((1, half), f32)...  0.66 us
    ppermute x1, starting transfers between devices, on_device(): others = lax.ppermute(panels, 'panel', swap)  0.52 us
  transfers between devices with their start and end apart: 6, of which 1 were waited for; matrix products, arithmetic and copies ran while one was open for 0% of the time, Pallas kernels for 31%

profile of v5, /device:TPU:0, one launch (start us, length us, event | category | flops | bytes accessed | tf_op | source)
XLA Modules:
  0.0 21.0 jit_solution(5465267431050269167)
XLA Ops:
  0.6 0.5 %collective-permute-start = (f32[8,2048]{1,0:T(8,128)}, f32[8,2048]{1,0:T(8,128)S(1)}, u32[]{:S(2)}, u32[]{:S(2)}) collective-permute-start(f32[8,2048]{1,0:T(8,128)} %panels.1), channel_id=1, source_target_pairs={{0,1},{1,0},{2,3},{3,2},{4,5},{5,4},{6,7},{7,6},{8,9},{9,8},{10,11... | collective-permute-start | bytes 196616 | tf_op jit(solution)/shard_map/ppermute | solution.py:346
  1.1 0.1 collective-permute-start.1
  1.2 0.0 copy-start.3
  1.2 0.9 %copy-done.3 = f32[6,4096]{1,0:T(8,128)S(1)} copy-done((f32[6,4096]{1,0:T(8,128)S(1)}, f32[6,4096]{1,0:T(8,128)}, u32[]{:S(2)}) %copy-start.3) | copy-done | bytes 98328
  2.1 0.0 copy-start
  2.1 0.7 %prepare.1 = (bf16[32,48,128]{2,1,0:T(8,128)(2,1)S(1)}, bf16[32,16,256]{2,1,0:T(8,128)(2,1)S(1)}, f32[32,32,128]{2,1,0:T(8,128)S(1)}) custom-call(f32[6,4096]{1,0:T(8,128)S(1)} %copy-done.3), custom_call_target="tpu_custom_call" | custom-call | flops 2000000000 | bytes 1000000 | tf_op jit(solution)/shard_map/prepare/pallas_call | solution.py:273
  2.9 0.0 copy-start.1
  2.9 0.0 collective-permute-done.1.near_o
  2.9 0.0 collective-permute-done.others
  2.9 0.0 copy-start.2
  2.9 0.0 copy-done
  3.0 0.6 %copy-done.1 = s32[16,64]{1,0:T(8,128)S(1)} copy-done((s32[16,64]{1,0:T(8,128)S(1)}, s32[16,64]{1,0:T(8,128)}, u32[]{:S(2)}) %copy-start.1) | copy-done | bytes 4120
  3.6 0.0 copy-done.2
  3.6 3.5 %panel_side.1 = (f32[1,4096]{1,0:T(1,128)S(1)}, f32[34,8,128]{2,1,0:T(8,128)S(1)}, s32[8,128]{1,0:T(8,128)S(1)}, bf16[34,48,128]{2,1,0:T(8,128)(2,1)S(1)}, bf16[34,48,128]{2,1,0:T(8,128)(2,1)S(1)}) custom-call(s32[1,32]{1,0:T(1,128)S(1)} %bitcast.9, f32[8,2048]{1,0:T(8,128)S(1)} %copy-done, f32[8,2048]{1,0:T(8,128)S(1)} %collective-permute-done.others, ...), custom_call_target="tpu_custom_call" | custom-call | tf_op jit(solution)/shard_map/panel_side/pallas_call | solution.py:293
  7.1 2.1 %collective-permute-start.2 = (f32[4096]{0:T(1024)S(1)}, f32[4096]{0:T(1024)S(1)}, u32[]{:S(2)}, u32[]{:S(2)}) collective-permute-start(f32[4096]{0:T(1024)S(1)} %bitcast.6), channel_id=1, source_target_pairs={{0,3},{1,2},{2,1},{3,0},{4,7},{5,6},{6,5},{7,4},{8,11},{9,10},{10,... | collective-permute-start | bytes 49160 | tf_op jit(solution)/shard_map/ppermute | solution.py:359
  9.2 1.6 %particle_side.4.rest_0_ = f32[32,8,128]{2,1,0:T(8,128)S(1)} custom-call(f32[34,8,128]{2,1,0:T(8,128)S(1)} %get-tuple-element.32.pan, s32[8,128]{1,0:T(8,128)S(1)} %get-tuple-element.47.items, bf16[32,48,128]{2,1,0:T(8,128)(2,1)S(1)} %get-tuple-element.26.un, bf16[34,48,128]{2,1,0:T(8,128)(2,1)S(1)} %get-tuple-element.34.v, ...), custom_call_target="tpu_custom_call" | custom-call | flops 1000000000 | bytes 100000 | tf_op jit(solution)/shard_map/particle_side/pallas_call | solution.py:317
  10.8 0.0 collective-permute-done.2
  10.9 1.7 %collective-permute-start.3 = (f32[4096]{0:T(1024)S(1)}, f32[4096]{0:T(1024)S(1)}, u32[]{:S(2)}, u32[]{:S(2)}) collective-permute-start(f32[4096]{0:T(1024)S(1)} %add.12), channel_id=1, source_target_pairs={{0,5},{1,4},{2,7},{3,6},{4,1},{5,0},{6,3},{7,2},{8,13},{9,12},{10,... | collective-permute-start | bytes 49160 | tf_op jit(solution)/shard_map/ppermute | solution.py:359
  12.6 1.6 %particle_side.5.rest_1_ = f32[32,8,128]{2,1,0:T(8,128)S(1)} custom-call(f32[34,8,128]{2,1,0:T(8,128)S(1)} %get-tuple-element.32.pan, s32[8,128]{1,0:T(8,128)S(1)} %get-tuple-element.47.items, bf16[32,48,128]{2,1,0:T(8,128)(2,1)S(1)} %get-tuple-element.26.un, bf16[34,48,128]{2,1,0:T(8,128)(2,1)S(1)} %get-tuple-element.34.v, ...), custom_call_target="tpu_custom_call" | custom-call | flops 1000000000 | bytes 100000 | tf_op jit(solution)/shard_map/particle_side/pallas_call | solution.py:317
  14.2 0.0 collective-permute-done.3
  14.3 3.1 %collective-permute-start.4 = (f32[4096]{0:T(1024)S(1)}, f32[4096]{0:T(1024)S(1)}, u32[]{:S(2)}, u32[]{:S(2)}) collective-permute-start(f32[4096]{0:T(1024)S(1)} %add.13), channel_id=1, source_target_pairs={{0,9},{1,8},{2,11},{3,10},{4,13},{5,12},{6,15},{7,14},{8,1},{9,0},... | collective-permute-start | bytes 49160 | tf_op jit(solution)/shard_map/ppermute | solution.py:359
  17.4 1.6 %particle_side.6.rest_2_ = f32[32,8,128]{2,1,0:T(8,128)S(1)} custom-call(f32[34,8,128]{2,1,0:T(8,128)S(1)} %get-tuple-element.32.pan, s32[8,128]{1,0:T(8,128)S(1)} %get-tuple-element.47.items, bf16[32,48,128]{2,1,0:T(8,128)(2,1)S(1)} %get-tuple-element.26.un, bf16[34,48,128]{2,1,0:T(8,128)(2,1)S(1)} %get-tuple-element.34.v, ...), custom_call_target="tpu_custom_call" | custom-call | flops 1000000000 | bytes 100000 | tf_op jit(solution)/shard_map/particle_side/pallas_call | solution.py:317
  19.1 0.0 collective-permute-done.4
  19.1 0.3 %collective-permute-start.5 = (f32[2048]{0:T(1024)S(1)}, f32[2048]{0:T(1024)S(1)}, u32[]{:S(2)}, u32[]{:S(2)}) collective-permute-start(f32[2048]{0:T(1024)S(1)} %dynamic_slice.3), channel_id=1, source_target_pairs={{0,1},{1,0},{2,3},{3,2},{4,5},{5,4},{6,7},{7,6},{8,9},{9,8},{10,11... | collective-permute-start | bytes 24584 | tf_op jit(solution)/shard_map/ppermute | solution.py:367
  19.4 0.9 %particle_side.7.rest_3_ = f32[32,8,128]{2,1,0:T(8,128)S(1)} custom-call(f32[34,8,128]{2,1,0:T(8,128)S(1)} %get-tuple-element.32.pan, s32[8,128]{1,0:T(8,128)S(1)} %get-tuple-element.47.items, bf16[32,48,128]{2,1,0:T(8,128)(2,1)S(1)} %get-tuple-element.26.un, bf16[34,48,128]{2,1,0:T(8,128)(2,1)S(1)} %get-tuple-element.34.v, ...), custom_call_target="tpu_custom_call" | custom-call | flops 1000000000 | bytes 100000 | tf_op jit(solution)/shard_map/particle_side/pallas_call | solution.py:317
  20.3 0.1 collective-permute-done.5
  20.3 0.7 %close.1 = (f32[1,2048]{1,0:T(1,128)}, f32[3,4096]{1,0:T(4,128)}) custom-call(f32[1,4096]{1,0:T(1,128)S(1)} %bitcast.5, f32[1,2048]{1,0:T(1,128)S(1)} %bitcast.8, f32[32,8,128]{2,1,0:T(8,128)S(1)} %particle_side.4.rest_0_, f32[32,8,128]{2,1,0:T(8,128)S(1)} %particle_side.5.rest_1_, f32[32,8,128]{2,1,0:T(8,128)S(1)} %particle_side.6.rest_2_, ...), custom_call_target="tpu_custom_call" | custom-call | tf_op jit(solution)/shard_map/close/pallas_call | solution.py:330
  (4 shorter events, 0.0 us)
Async XLA Ops:
  0.6 2.3 %collective-permute-start = (f32[8,2048]{1,0:T(8,128)}, f32[8,2048]{1,0:T(8,128)S(1)}, u32[]{:S(2)}, u32[]{:S(2)}) collective-permute-start(f32[8,2048]{1,0:T(8,128)} %panels.1), channel_id=1, source_target_pairs={{0,1},{1,0},{2,3},{3,2},{4,5},{5,4},{6,7},{7,6},{8,9},{9,8},{10,11... | collective-permute-start | bytes 196616 | tf_op jit(solution)/shard_map/ppermute | solution.py:346
  1.1 1.7 %collective-permute-start.1 = (s32[16,64]{1,0:T(8,128)}, s32[16,64]{1,0:T(8,128)S(1)}, u32[]{:S(2)}, u32[]{:S(2)}) collective-permute-start(s32[16,64]{1,0:T(8,128)} %near.1), channel_id=1, source_target_pairs={{0,1},{1,0},{2,3},{3,2},{4,5},{5,4},{6,7},{7,6},{8,9},{9,8},{10,11... | collective-permute-start | bytes 12296 | tf_op jit(solution)/shard_map/ppermute | solution.py:347
  1.2 0.9 %copy-start.3 = (f32[6,4096]{1,0:T(8,128)S(1)}, f32[6,4096]{1,0:T(8,128)}, u32[]{:S(2)}) copy-start(f32[6,4096]{1,0:T(8,128)} %particles.1) | copy-start | bytes 294916
  2.1 0.8 %copy-start = (f32[8,2048]{1,0:T(8,128)S(1)}, f32[8,2048]{1,0:T(8,128)}, u32[]{:S(2)}) copy-start(f32[8,2048]{1,0:T(8,128)} %panels.1) | copy-start | bytes 196612
  2.9 0.7 %copy-start.1 = (s32[16,64]{1,0:T(8,128)S(1)}, s32[16,64]{1,0:T(8,128)}, u32[]{:S(2)}) copy-start(s32[16,64]{1,0:T(8,128)} %near.1) | copy-start | bytes 12292
  2.9 0.7 %copy-start.2 = (s32[32]{0:T(128)S(1)}, s32[32]{0:T(128)}, u32[]{:S(2)}) copy-start(s32[32]{0:T(128)} %param.6) | copy-start | bytes 388
  7.1 3.7 %collective-permute-start.2 = (f32[4096]{0:T(1024)S(1)}, f32[4096]{0:T(1024)S(1)}, u32[]{:S(2)}, u32[]{:S(2)}) collective-permute-start(f32[4096]{0:T(1024)S(1)} %bitcast.6), channel_id=1, source_target_pairs={{0,3},{1,2},{2,1},{3,0},{4,7},{5,6},{6,5},{7,4},{8,11},{9,10},{10,... | collective-permute-start | bytes 49160 | tf_op jit(solution)/shard_map/ppermute | solution.py:359
  10.9 3.4 %collective-permute-start.3 = (f32[4096]{0:T(1024)S(1)}, f32[4096]{0:T(1024)S(1)}, u32[]{:S(2)}, u32[]{:S(2)}) collective-permute-start(f32[4096]{0:T(1024)S(1)} %add.12), channel_id=1, source_target_pairs={{0,5},{1,4},{2,7},{3,6},{4,1},{5,0},{6,3},{7,2},{8,13},{9,12},{10,... | collective-permute-start | bytes 49160 | tf_op jit(solution)/shard_map/ppermute | solution.py:359
  14.3 4.8 %collective-permute-start.4 = (f32[4096]{0:T(1024)S(1)}, f32[4096]{0:T(1024)S(1)}, u32[]{:S(2)}, u32[]{:S(2)}) collective-permute-start(f32[4096]{0:T(1024)S(1)} %add.13), channel_id=1, source_target_pairs={{0,9},{1,8},{2,11},{3,10},{4,13},{5,12},{6,15},{7,14},{8,1},{9,0},... | collective-permute-start | bytes 49160 | tf_op jit(solution)/shard_map/ppermute | solution.py:359
  19.1 1.2 %collective-permute-start.5 = (f32[2048]{0:T(1024)S(1)}, f32[2048]{0:T(1024)S(1)}, u32[]{:S(2)}, u32[]{:S(2)}) collective-permute-start(f32[2048]{0:T(1024)S(1)} %dynamic_slice.3), channel_id=1, source_target_pairs={{0,1},{1,0},{2,3},{3,2},{4,5},{5,4},{6,7},{7,6},{8,9},{9,8},{10,11... | collective-permute-start | bytes 24584 | tf_op jit(solution)/shard_map/ppermute | solution.py:367

commit v6 on v5

--- a/solution.py
+++ b/solution.py
@@ -11,7 +11,7 @@
 inv_four_pi = 0.07957747154594767
 BLK = 128
 WIN = 3
-EACH1 = 20
+EACH1 = 26
 EACH = 10
 bf16 = jnp.bfloat16
 f32 = jnp.float32
@@ -79,7 +79,7 @@
             org[q, 8 * i : 8 * i + 8, :] = v
         return carry
 
-    lax.fori_loop(0, nblk, one, 0, unroll=4)
+    lax.fori_loop(0, nblk, one, 0, unroll=16)
 
 
 def list_pairs(mine, other, counts, me, nblk, column, box):
@@ -124,7 +124,7 @@
             body(ref[:, block(k, BLK)], start + k)
             return carry
 
-        lax.fori_loop(0, many, one, 0, unroll=4)
+        lax.fori_loop(0, many, one, 0, unroll=8)
 
     run(panels, me * many)
     run(others, (1 - me) * many)

time: 21.2 us -> 20.5 us (0.967)
  Pallas kernels: 10.7 us -> 9.96 us
    pallas_call x1, Pallas kernels: 0.74 us -> 0.28 us  [prepare(): pl.pallas_call(particle_features, out_shape=(jax.ShapeDtypeStruct((nblk,...]
    pallas_call x1, Pallas kernels: 3.52 us -> 3.25 us  [panel_side(): pl.pallas_call(panel_sums, out_shape=(jax.ShapeDtypeStruct((1, npan), f32...]
  transfers between devices with their start and end apart: 6 -> 6, of which waited for: 1 -> 2; matrix products, arithmetic and copies ran while one was open for 0% -> 0% of each run, Pallas kernels for 31% -> 30%
where the time goes in v6:
time: 20.5 us; the launch traced here: 20.3 us
  Pallas kernels  9.96 us (49%)
  starting transfers between devices  7.8 us (38%)
  local copies, waits for them, and re-layouts  1.58 us (8%)
  between operations  0.75 us (4%)
    ppermute x3, starting transfers between devices, on_device(): lax.ppermute(total, ('dom', 'panel'), pairs)  6.88 us
    pallas_call x4, Pallas kernels, particle_side(): pl.pallas_call(functools.partial(particle_sums, part, parts), out_shape=j...  5.76 us
    pallas_call x1, Pallas kernels, panel_side(): pl.pallas_call(panel_sums, out_shape=(jax.ShapeDtypeStruct((1, npan), f32...  3.25 us
    unnamed x8, local copies, waits for them, and re-layouts  1.57 us
    pallas_call x1, Pallas kernels, close(): pl.pallas_call(last_sums, out_shape=(jax.ShapeDtypeStruct((1, half), f32)...  0.66 us
    ppermute x1, starting transfers between devices, on_device(): others = lax.ppermute(panels, 'panel', swap)  0.52 us
  transfers between devices with their start and end apart: 6, of which 2 were waited for; matrix products, arithmetic and copies ran while one was open for 0% of the time, Pallas kernels for 30%

profile of v6, /device:TPU:0, one launch (start us, length us, event | category | flops | bytes accessed | tf_op | source)
XLA Modules:
  0.0 20.3 jit_solution(989586249314409669)
XLA Ops:
  0.6 0.5 %collective-permute-start = (f32[8,2048]{1,0:T(8,128)}, f32[8,2048]{1,0:T(8,128)S(1)}, u32[]{:S(2)}, u32[]{:S(2)}) collective-permute-start(f32[8,2048]{1,0:T(8,128)} %panels.1), channel_id=1, source_target_pairs={{0,1},{1,0},{2,3},{3,2},{4,5},{5,4},{6,7},{7,6},{8,9},{9,8},{10,11... | collective-permute-start | bytes 196616 | tf_op jit(solution)/shard_map/ppermute | solution.py:346
  1.1 0.1 collective-permute-start.1
  1.2 0.0 copy-start.3
  1.2 0.9 %copy-done.3 = f32[6,4096]{1,0:T(8,128)S(1)} copy-done((f32[6,4096]{1,0:T(8,128)S(1)}, f32[6,4096]{1,0:T(8,128)}, u32[]{:S(2)}) %copy-start.3) | copy-done | bytes 98328
  2.1 0.0 copy-start
  2.1 0.3 %prepare.1 = (bf16[32,48,128]{2,1,0:T(8,128)(2,1)S(1)}, bf16[32,16,256]{2,1,0:T(8,128)(2,1)S(1)}, f32[32,32,128]{2,1,0:T(8,128)S(1)}) custom-call(f32[6,4096]{1,0:T(8,128)S(1)} %copy-done.3), custom_call_target="tpu_custom_call" | custom-call | flops 2000000000 | bytes 1000000 | tf_op jit(solution)/shard_map/prepare/pallas_call | solution.py:273
  2.4 0.0 copy-start.1
  2.4 0.1 collective-permute-done.1.near_o
  2.5 0.0 collective-permute-done.others
  2.5 0.0 copy-start.2
  2.5 0.4 %copy-done = f32[8,2048]{1,0:T(8,128)S(1)} copy-done((f32[8,2048]{1,0:T(8,128)S(1)}, f32[8,2048]{1,0:T(8,128)}, u32[]{:S(2)}) %copy-start) | copy-done | bytes 65560
  3.0 0.2 copy-done.1
  3.1 0.1 copy-done.2
  3.2 3.3 %panel_side.1 = (f32[1,4096]{1,0:T(1,128)S(1)}, f32[34,8,128]{2,1,0:T(8,128)S(1)}, s32[8,128]{1,0:T(8,128)S(1)}, bf16[34,48,128]{2,1,0:T(8,128)(2,1)S(1)}, bf16[34,48,128]{2,1,0:T(8,128)(2,1)S(1)}) custom-call(s32[1,32]{1,0:T(1,128)S(1)} %bitcast.9, f32[8,2048]{1,0:T(8,128)S(1)} %copy-done, f32[8,2048]{1,0:T(8,128)S(1)} %collective-permute-done.others, ...), custom_call_target="tpu_custom_call" | custom-call | tf_op jit(solution)/shard_map/panel_side/pallas_call | solution.py:293
  6.5 2.7 %collective-permute-start.2 = (f32[4096]{0:T(1024)S(1)}, f32[4096]{0:T(1024)S(1)}, u32[]{:S(2)}, u32[]{:S(2)}) collective-permute-start(f32[4096]{0:T(1024)S(1)} %bitcast.6), channel_id=1, source_target_pairs={{0,3},{1,2},{2,1},{3,0},{4,7},{5,6},{6,5},{7,4},{8,11},{9,10},{10,... | collective-permute-start | bytes 49160 | tf_op jit(solution)/shard_map/ppermute | solution.py:359
  9.2 1.6 %particle_side.4.rest_0_ = f32[32,8,128]{2,1,0:T(8,128)S(1)} custom-call(f32[34,8,128]{2,1,0:T(8,128)S(1)} %get-tuple-element.32.pan, s32[8,128]{1,0:T(8,128)S(1)} %get-tuple-element.47.items, bf16[32,48,128]{2,1,0:T(8,128)(2,1)S(1)} %get-tuple-element.26.un, bf16[34,48,128]{2,1,0:T(8,128)(2,1)S(1)} %get-tuple-element.34.v, ...), custom_call_target="tpu_custom_call" | custom-call | flops 1000000000 | bytes 100000 | tf_op jit(solution)/shard_map/particle_side/pallas_call | solution.py:317
  10.8 0.0 collective-permute-done.2
  10.8 1.6 %collective-permute-start.3 = (f32[4096]{0:T(1024)S(1)}, f32[4096]{0:T(1024)S(1)}, u32[]{:S(2)}, u32[]{:S(2)}) collective-permute-start(f32[4096]{0:T(1024)S(1)} %add.12), channel_id=1, source_target_pairs={{0,5},{1,4},{2,7},{3,6},{4,1},{5,0},{6,3},{7,2},{8,13},{9,12},{10,... | collective-permute-start | bytes 49160 | tf_op jit(solution)/shard_map/ppermute | solution.py:359
  12.4 1.6 %particle_side.5.rest_1_ = f32[32,8,128]{2,1,0:T(8,128)S(1)} custom-call(f32[34,8,128]{2,1,0:T(8,128)S(1)} %get-tuple-element.32.pan, s32[8,128]{1,0:T(8,128)S(1)} %get-tuple-element.47.items, bf16[32,48,128]{2,1,0:T(8,128)(2,1)S(1)} %get-tuple-element.26.un, bf16[34,48,128]{2,1,0:T(8,128)(2,1)S(1)} %get-tuple-element.34.v, ...), custom_call_target="tpu_custom_call" | custom-call | flops 1000000000 | bytes 100000 | tf_op jit(solution)/shard_map/particle_side/pallas_call | solution.py:317
  14.1 0.0 collective-permute-done.3
  14.1 2.6 %collective-permute-start.4 = (f32[4096]{0:T(1024)S(1)}, f32[4096]{0:T(1024)S(1)}, u32[]{:S(2)}, u32[]{:S(2)}) collective-permute-start(f32[4096]{0:T(1024)S(1)} %add.13), channel_id=1, source_target_pairs={{0,9},{1,8},{2,11},{3,10},{4,13},{5,12},{6,15},{7,14},{8,1},{9,0},... | collective-permute-start | bytes 49160 | tf_op jit(solution)/shard_map/ppermute | solution.py:359
  16.7 1.6 %particle_side.6.rest_2_ = f32[32,8,128]{2,1,0:T(8,128)S(1)} custom-call(f32[34,8,128]{2,1,0:T(8,128)S(1)} %get-tuple-element.32.pan, s32[8,128]{1,0:T(8,128)S(1)} %get-tuple-element.47.items, bf16[32,48,128]{2,1,0:T(8,128)(2,1)S(1)} %get-tuple-element.26.un, bf16[34,48,128]{2,1,0:T(8,128)(2,1)S(1)} %get-tuple-element.34.v, ...), custom_call_target="tpu_custom_call" | custom-call | flops 1000000000 | bytes 100000 | tf_op jit(solution)/shard_map/particle_side/pallas_call | solution.py:317
  18.3 0.0 collective-permute-done.4
  18.4 0.3 %collective-permute-start.5 = (f32[2048]{0:T(1024)S(1)}, f32[2048]{0:T(1024)S(1)}, u32[]{:S(2)}, u32[]{:S(2)}) collective-permute-start(f32[2048]{0:T(1024)S(1)} %dynamic_slice.3), channel_id=1, source_target_pairs={{0,1},{1,0},{2,3},{3,2},{4,5},{5,4},{6,7},{7,6},{8,9},{9,8},{10,11... | collective-permute-start | bytes 24584 | tf_op jit(solution)/shard_map/ppermute | solution.py:367
  18.7 0.8 %particle_side.7.rest_3_ = f32[32,8,128]{2,1,0:T(8,128)S(1)} custom-call(f32[34,8,128]{2,1,0:T(8,128)S(1)} %get-tuple-element.32.pan, s32[8,128]{1,0:T(8,128)S(1)} %get-tuple-element.47.items, bf16[32,48,128]{2,1,0:T(8,128)(2,1)S(1)} %get-tuple-element.26.un, bf16[34,48,128]{2,1,0:T(8,128)(2,1)S(1)} %get-tuple-element.34.v, ...), custom_call_target="tpu_custom_call" | custom-call | flops 1000000000 | bytes 100000 | tf_op jit(solution)/shard_map/particle_side/pallas_call | solution.py:317
  19.6 0.1 collective-permute-done.5
  19.6 0.7 %close.1 = (f32[1,2048]{1,0:T(1,128)}, f32[3,4096]{1,0:T(4,128)}) custom-call(f32[1,4096]{1,0:T(1,128)S(1)} %bitcast.5, f32[1,2048]{1,0:T(1,128)S(1)} %bitcast.8, f32[32,8,128]{2,1,0:T(8,128)S(1)} %particle_side.4.rest_0_, f32[32,8,128]{2,1,0:T(8,128)S(1)} %particle_side.5.rest_1_, f32[32,8,128]{2,1,0:T(8,128)S(1)} %particle_side.6.rest_2_, ...), custom_call_target="tpu_custom_call" | custom-call | tf_op jit(solution)/shard_map/close/pallas_call | solution.py:330
  (4 shorter events, 0.0 us)
Async XLA Ops:
  0.6 1.9 %collective-permute-start = (f32[8,2048]{1,0:T(8,128)}, f32[8,2048]{1,0:T(8,128)S(1)}, u32[]{:S(2)}, u32[]{:S(2)}) collective-permute-start(f32[8,2048]{1,0:T(8,128)} %panels.1), channel_id=1, source_target_pairs={{0,1},{1,0},{2,3},{3,2},{4,5},{5,4},{6,7},{7,6},{8,9},{9,8},{10,11... | collective-permute-start | bytes 196616 | tf_op jit(solution)/shard_map/ppermute | solution.py:346
  1.1 1.4 %collective-permute-start.1 = (s32[16,64]{1,0:T(8,128)}, s32[16,64]{1,0:T(8,128)S(1)}, u32[]{:S(2)}, u32[]{:S(2)}) collective-permute-start(s32[16,64]{1,0:T(8,128)} %near.1), channel_id=1, source_target_pairs={{0,1},{1,0},{2,3},{3,2},{4,5},{5,4},{6,7},{7,6},{8,9},{9,8},{10,11... | collective-permute-start | bytes 12296 | tf_op jit(solution)/shard_map/ppermute | solution.py:347
  1.2 0.9 %copy-start.3 = (f32[6,4096]{1,0:T(8,128)S(1)}, f32[6,4096]{1,0:T(8,128)}, u32[]{:S(2)}) copy-start(f32[6,4096]{1,0:T(8,128)} %particles.1) | copy-start | bytes 294916
  2.1 0.8 %copy-start = (f32[8,2048]{1,0:T(8,128)S(1)}, f32[8,2048]{1,0:T(8,128)}, u32[]{:S(2)}) copy-start(f32[8,2048]{1,0:T(8,128)} %panels.1) | copy-start | bytes 196612
  2.4 0.7 %copy-start.1 = (s32[16,64]{1,0:T(8,128)S(1)}, s32[16,64]{1,0:T(8,128)}, u32[]{:S(2)}) copy-start(s32[16,64]{1,0:T(8,128)} %near.1) | copy-start | bytes 12292
  2.5 0.7 %copy-start.2 = (s32[32]{0:T(128)S(1)}, s32[32]{0:T(128)}, u32[]{:S(2)}) copy-start(s32[32]{0:T(128)} %param.6) | copy-start | bytes 388
  6.5 4.3 %collective-permute-start.2 = (f32[4096]{0:T(1024)S(1)}, f32[4096]{0:T(1024)S(1)}, u32[]{:S(2)}, u32[]{:S(2)}) collective-permute-start(f32[4096]{0:T(1024)S(1)} %bitcast.6), channel_id=1, source_target_pairs={{0,3},{1,2},{2,1},{3,0},{4,7},{5,6},{6,5},{7,4},{8,11},{9,10},{10,... | collective-permute-start | bytes 49160 | tf_op jit(solution)/shard_map/ppermute | solution.py:359
  10.8 3.3 %collective-permute-start.3 = (f32[4096]{0:T(1024)S(1)}, f32[4096]{0:T(1024)S(1)}, u32[]{:S(2)}, u32[]{:S(2)}) collective-permute-start(f32[4096]{0:T(1024)S(1)} %add.12), channel_id=1, source_target_pairs={{0,5},{1,4},{2,7},{3,6},{4,1},{5,0},{6,3},{7,2},{8,13},{9,12},{10,... | collective-permute-start | bytes 49160 | tf_op jit(solution)/shard_map/ppermute | solution.py:359
  14.1 4.2 %collective-permute-start.4 = (f32[4096]{0:T(1024)S(1)}, f32[4096]{0:T(1024)S(1)}, u32[]{:S(2)}, u32[]{:S(2)}) collective-permute-start(f32[4096]{0:T(1024)S(1)} %add.13), channel_id=1, source_target_pairs={{0,9},{1,8},{2,11},{3,10},{4,13},{5,12},{6,15},{7,14},{8,1},{9,0},... | collective-permute-start | bytes 49160 | tf_op jit(solution)/shard_map/ppermute | solution.py:359
  18.4 1.2 %collective-permute-start.5 = (f32[2048]{0:T(1024)S(1)}, f32[2048]{0:T(1024)S(1)}, u32[]{:S(2)}, u32[]{:S(2)}) collective-permute-start(f32[2048]{0:T(1024)S(1)} %dynamic_slice.3), channel_id=1, source_target_pairs={{0,1},{1,0},{2,3},{3,2},{4,5},{5,4},{6,7},{7,6},{8,9},{9,8},{10,11... | collective-permute-start | bytes 24584 | tf_op jit(solution)/shard_map/ppermute | solution.py:367

commit v7 on v6

--- a/solution.py
+++ b/solution.py
@@ -47,9 +47,8 @@
     return pl.ds(pl.multiple_of(q * size, size), size)
 
 
-def particle_features(particles, un, fe, org, parts):
-    nblk = particles.shape[1] // BLK
-    parts[0:6, :] = particles[...]
+def particle_features(parts, un, fe, org):
+    nblk = parts.shape[1] // BLK
     row = rows8(BLK)
 
     def one(q, carry):
@@ -145,12 +144,15 @@
 TURN = (((0,), (0,)), ((), ()))
 
 
-def panel_sums(counts, panels, others, near, near_o, un, fe, org, out, pan, box, v, vn, geo, tot, column, items, sem):
+def panel_sums(
+    counts, particles, panels, others, near, near_o, out, pan, box, v, vn, un, org, fe, geo, tot, column, items, sem
+):
     me = lax.axis_index("panel")
     nblk = un.shape[0]
     list_pairs(near, near_o, counts, me, nblk, column, box)
     copy = pltpu.make_async_copy(box, items, sem)
     copy.start()
+    particle_features(particles, un, fe, org)
     row = rows8(BLK)
 
     def build(p, at):
@@ -267,29 +269,27 @@
     return pltpu.CompilerParams(vmem_limit_bytes=mib * 1024 * 1024)
 
 
-def prepare(particles):
-    width = particles.shape[1]
+def fetch(source, out):
+    out[0:6, :] = source[...]
+    out[6:8, :] = jnp.zeros((2, out.shape[1]), f32)
+
+
+def fetched(particles):
+    return pl.pallas_call(
+        fetch,
+        out_shape=jax.ShapeDtypeStruct((8, particles.shape[1]), f32),
+        in_specs=[vmem()],
+        out_specs=vmem(),
+        compiler_params=params(),
+        name="fetch",
+    )(particles)
+
+
+def panel_side(counts, particles, panels, others, near, near_o):
+    npan, width = 2 * panels.shape[1], particles.shape[1]
     nblk = width // BLK
-    return pl.pallas_call(
-        particle_features,
-        out_shape=(
-            jax.ShapeDtypeStruct((nblk, 48, BLK), bf16),
-            jax.ShapeDtypeStruct((nblk, 16, 2 * BLK), bf16),
-            jax.ShapeDtypeStruct((nblk, 32, BLK), f32),
-        ),
-        in_specs=[vmem()],
-        out_specs=(vmem(),) * 3,
-        scratch_shapes=[pltpu.VMEM((8, width), f32)],
-        compiler_params=params(),
-        cost_estimate=pl.CostEstimate(flops=2 * 10**9, bytes_accessed=10**6, transcendentals=0),
-        name="prepare",
-    )(particles)
-
-
-def panel_side(counts, panels, others, near, near_o, un, fe, org):
-    npan = 2 * panels.shape[1]
     full = npan // BLK + WIN - 1
-    wide = pl.cdiv(WIN * counts.shape[1] + EACH1, BLK) * BLK
+    wide = pl.cdiv(WIN * nblk + max(EACH1, EACH), BLK) * BLK
     return pl.pallas_call(
         panel_sums,
         out_shape=(
@@ -298,10 +298,13 @@
             jax.ShapeDtypeStruct((8, wide), jnp.int32),
             jax.ShapeDtypeStruct((full, 48, BLK), bf16),
             jax.ShapeDtypeStruct((full, 48, BLK), bf16),
+            jax.ShapeDtypeStruct((nblk, 48, BLK), bf16),
+            jax.ShapeDtypeStruct((nblk, 32, BLK), f32),
         ),
-        in_specs=[vmem()] * 8,
-        out_specs=(vmem(),) * 5,
+        in_specs=[vmem()] * 6,
+        out_specs=(vmem(),) * 7,
         scratch_shapes=[
+            pltpu.VMEM((nblk, 16, 2 * BLK), bf16),
             pltpu.VMEM((full, 32, BLK), f32),
             pltpu.VMEM((full, 8, BLK), f32),
             pltpu.VMEM((near.shape[1], 8), f32),
@@ -310,7 +313,7 @@
         ],
         compiler_params=params(),
         name="panel_side",
-    )(counts, panels, others, near, near_o, un, fe, org)
+    )(counts, particles, panels, others, near, near_o)
 
 
 def particle_side(part, parts, pan, box, un, v, vn, org):
@@ -345,8 +348,7 @@
     swap = [(0, 1), (1, 0)]
     others = lax.ppermute(panels, "panel", swap)
     near_o = lax.ppermute(near, "panel", swap)
-    un, fe, org = prepare(particles)
-    total, pan, box, v, vn = panel_side(counts.reshape(1, -1), panels, others, near, near_o, un, fe, org)
+    total, pan, box, v, vn, un, org = panel_side(counts.reshape(1, -1), fetched(particles), panels, others, near, near_o)
     total = total.reshape(total.shape[1])
     steps = [1 << b for b in range((dom - 1).bit_length())]
     parts = len(steps) + 1

time: 20.5 us -> 20.7 us (level); the launches traced: 20.3 us -> 20.9 us
  Pallas kernels: 9.96 us -> 10.5 us
  local copies, waits for them, and re-layouts: 1.58 us -> 1.37 us
    pallas_call x4, Pallas kernels: 5.76 us -> 6.55 us  [particle_side(): pl.pallas_call(functools.partial(particle_sums, part, parts), out_shape=j...]
    pallas_call x1, Pallas kernels: 0.28 us -> 0.02 us  [fetched(): pl.pallas_call(fetch, out_shape=jax.ShapeDtypeStruct((8, particles.shape[...]
    ppermute x1, waiting for transfers between devices: 0.09 us -> 0.35 us  [on_device(): near_o = lax.ppermute(near, 'panel', swap)]
    unnamed x8, local copies, waits for them, and re-layouts: 1.57 us -> 1.35 us
  transfers between devices with their start and end apart: 6 -> 6, of which waited for: 2 -> 1; matrix products, arithmetic and copies ran while one was open for 0% -> 0% of each run, Pallas kernels for 30% -> 31%
where the time goes in v7:
time: 20.7 us; the launch traced here: 20.9 us
  Pallas kernels  10.5 us (51%)
  starting transfers between devices  7.87 us (38%)
  local copies, waits for them, and re-layouts  1.37 us (7%)
  between operations  0.77 us (4%)
  waiting for transfers between devices  0.36 us (2%)
    ppermute x3, starting transfers between devices, on_device(): lax.ppermute(total, ('dom', 'panel'), pairs)  6.88 us
    pallas_call x4, Pallas kernels, particle_side(): pl.pallas_call(functools.partial(particle_sums, part, parts), out_shape=j...  6.55 us
    pallas_call x1, Pallas kernels, panel_side(): pl.pallas_call(panel_sums, out_shape=(jax.ShapeDtypeStruct((1, npan), f32...  3.28 us
    unnamed x8, local copies, waits for them, and re-layouts  1.35 us
    pallas_call x1, Pallas kernels, close(): pl.pallas_call(last_sums, out_shape=(jax.ShapeDtypeStruct((1, half), f32)...  0.66 us
    ppermute x1, starting transfers between devices, on_device(): others = lax.ppermute(panels, 'panel', swap)  0.52 us
  transfers between devices with their start and end apart: 6, of which 1 were waited for; matrix products, arithmetic and copies ran while one was open for 0% of the time, Pallas kernels for 31%

profile of v7, /device:TPU:0, one launch (start us, length us, event | category | flops | bytes accessed | tf_op | source)
XLA Modules:
  0.0 20.9 jit_solution(9399704289683392058)
XLA Ops:
  0.6 0.5 %collective-permute-start = (f32[8,2048]{1,0:T(8,128)}, f32[8,2048]{1,0:T(8,128)S(1)}, u32[]{:S(2)}, u32[]{:S(2)}) collective-permute-start(f32[8,2048]{1,0:T(8,128)} %panels.1), channel_id=1, source_target_pairs={{0,1},{1,0},{2,3},{3,2},{4,5},{5,4},{6,7},{7,6},{8,9},{9,8},{10,11... | collective-permute-start | bytes 196616 | tf_op jit(solution)/shard_map/ppermute | solution.py:349
  1.1 0.1 collective-permute-start.1
  1.2 0.0 copy-start
  1.2 0.9 %copy-done = f32[6,4096]{1,0:T(8,128)S(1)} copy-done((f32[6,4096]{1,0:T(8,128)S(1)}, f32[6,4096]{1,0:T(8,128)}, u32[]{:S(2)}) %copy-start) | copy-done | bytes 98328
  2.1 0.0 copy-start.1
  2.2 0.0 copy-start.2
  2.2 0.0 copy-start.3
  2.2 0.3 %collective-permute-done.1.near_o = s32[16,64]{1,0:T(8,128)S(1)} collective-permute-done((s32[16,64]{1,0:T(8,128)}, s32[16,64]{1,0:T(8,128)S(1)}, u32[]{:S(2)}, u32[]{:S(2)}) %collective-permute-start.1) | collective-permute-done | bytes 4128 | tf_op jit(solution)/shard_map/ppermute | solution.py:350
  2.5 0.0 collective-permute-done.others
  2.5 0.4 %copy-done.1 = f32[8,2048]{1,0:T(8,128)S(1)} copy-done((f32[8,2048]{1,0:T(8,128)S(1)}, f32[8,2048]{1,0:T(8,128)}, u32[]{:S(2)}) %copy-start.1) | copy-done | bytes 65560
  3.0 0.0 copy-done.2
  3.0 0.0 copy-done.3
  3.0 3.3 %panel_side.1 = (f32[1,4096]{1,0:T(1,128)S(1)}, f32[34,8,128]{2,1,0:T(8,128)S(1)}, s32[8,128]{1,0:T(8,128)S(1)}, bf16[34,48,128]{2,1,0:T(8,128)(2,1)S(1)}, bf16[...) custom-call(s32[1,32]{1,0:T(1,128)S(1)} %bitcast.9, ...), custom_call_target="tpu_custom_call" | custom-call | tf_op jit(solution)/shard_map/panel_side/pallas_call | solution.py:293
  6.3 1.9 %collective-permute-start.2 = (f32[4096]{0:T(1024)S(1)}, f32[4096]{0:T(1024)S(1)}, u32[]{:S(2)}, u32[]{:S(2)}) collective-permute-start(f32[4096]{0:T(1024)S(1)} %bitcast.6), channel_id=1, source_target_pairs={{0,3},{1,2},{2,1},{3,0},{4,7},{5,6},{6,5},{7,4},{8,11},{9,10},{10,... | collective-permute-start | bytes 49160 | tf_op jit(solution)/shard_map/ppermute | solution.py:361
  8.2 1.6 %particle_side.4.rest_0_ = f32[32,8,128]{2,1,0:T(8,128)S(1)} custom-call(f32[34,8,128]{2,1,0:T(8,128)S(1)} %get-tuple-element.28.pan, s32[8,128]{1,0:T(8,128)S(1)} %get-tuple-element.45.items, bf16[32,48,128]{2,1,0:T(8,128)(2,1)S(1)} %get-tuple-element.30.un, bf16[34,48,128]{2,1,0:T(8,128)(2,1)S(1)} %get-tuple-element.31.v, ...), custom_call_target="tpu_custom_call" | custom-call | flops 1000000000 | bytes 100000 | tf_op jit(solution)/shard_map/particle_side/pallas_call | solution.py:320
  9.8 0.0 collective-permute-done.2
  9.9 2.4 %collective-permute-start.3 = (f32[4096]{0:T(1024)S(1)}, f32[4096]{0:T(1024)S(1)}, u32[]{:S(2)}, u32[]{:S(2)}) collective-permute-start(f32[4096]{0:T(1024)S(1)} %add.12), channel_id=1, source_target_pairs={{0,5},{1,4},{2,7},{3,6},{4,1},{5,0},{6,3},{7,2},{8,13},{9,12},{10,... | collective-permute-start | bytes 49160 | tf_op jit(solution)/shard_map/ppermute | solution.py:361
  12.3 1.6 %particle_side.5.rest_1_ = f32[32,8,128]{2,1,0:T(8,128)S(1)} custom-call(f32[34,8,128]{2,1,0:T(8,128)S(1)} %get-tuple-element.28.pan, s32[8,128]{1,0:T(8,128)S(1)} %get-tuple-element.45.items, bf16[32,48,128]{2,1,0:T(8,128)(2,1)S(1)} %get-tuple-element.30.un, bf16[34,48,128]{2,1,0:T(8,128)(2,1)S(1)} %get-tuple-element.31.v, ...), custom_call_target="tpu_custom_call" | custom-call | flops 1000000000 | bytes 100000 | tf_op jit(solution)/shard_map/particle_side/pallas_call | solution.py:320
  14.0 0.0 collective-permute-done.3
  14.0 2.5 %collective-permute-start.4 = (f32[4096]{0:T(1024)S(1)}, f32[4096]{0:T(1024)S(1)}, u32[]{:S(2)}, u32[]{:S(2)}) collective-permute-start(f32[4096]{0:T(1024)S(1)} %add.13), channel_id=1, source_target_pairs={{0,9},{1,8},{2,11},{3,10},{4,13},{5,12},{6,15},{7,14},{8,1},{9,0},... | collective-permute-start | bytes 49160 | tf_op jit(solution)/shard_map/ppermute | solution.py:361
  16.5 1.6 %particle_side.6.rest_2_ = f32[32,8,128]{2,1,0:T(8,128)S(1)} custom-call(f32[34,8,128]{2,1,0:T(8,128)S(1)} %get-tuple-element.28.pan, s32[8,128]{1,0:T(8,128)S(1)} %get-tuple-element.45.items, bf16[32,48,128]{2,1,0:T(8,128)(2,1)S(1)} %get-tuple-element.30.un, bf16[34,48,128]{2,1,0:T(8,128)(2,1)S(1)} %get-tuple-element.31.v, ...), custom_call_target="tpu_custom_call" | custom-call | flops 1000000000 | bytes 100000 | tf_op jit(solution)/shard_map/particle_side/pallas_call | solution.py:320
  18.1 0.0 collective-permute-done.4
  18.2 0.4 %collective-permute-start.5 = (f32[2048]{0:T(1024)S(1)}, f32[2048]{0:T(1024)S(1)}, u32[]{:S(2)}, u32[]{:S(2)}) collective-permute-start(f32[2048]{0:T(1024)S(1)} %dynamic_slice.3), channel_id=1, source_target_pairs={{0,1},{1,0},{2,3},{3,2},{4,5},{5,4},{6,7},{7,6},{8,9},{9,8},{10,11... | collective-permute-start | bytes 24584 | tf_op jit(solution)/shard_map/ppermute | solution.py:369
  18.6 1.6 %particle_side.7.rest_3_ = f32[32,8,128]{2,1,0:T(8,128)S(1)} custom-call(f32[34,8,128]{2,1,0:T(8,128)S(1)} %get-tuple-element.28.pan, s32[8,128]{1,0:T(8,128)S(1)} %get-tuple-element.45.items, bf16[32,48,128]{2,1,0:T(8,128)(2,1)S(1)} %get-tuple-element.30.un, bf16[34,48,128]{2,1,0:T(8,128)(2,1)S(1)} %get-tuple-element.31.v, ...), custom_call_target="tpu_custom_call" | custom-call | flops 1000000000 | bytes 100000 | tf_op jit(solution)/shard_map/particle_side/pallas_call | solution.py:320
  20.2 0.0 collective-permute-done.5
  20.2 0.7 %close.1 = (f32[1,2048]{1,0:T(1,128)}, f32[3,4096]{1,0:T(4,128)}) custom-call(f32[1,4096]{1,0:T(1,128)S(1)} %bitcast.5, f32[1,2048]{1,0:T(1,128)S(1)} %bitcast.8, f32[32,8,128]{2,1,0:T(8,128)S(1)} %particle_side.4.rest_0_, f32[32,8,128]{2,1,0:T(8,128)S(1)} %particle_side.5.rest_1_, f32[32,8,128]{2,1,0:T(8,128)S(1)} %particle_side.6.rest_2_, ...), custom_call_target="tpu_custom_call" | custom-call | tf_op jit(solution)/shard_map/close/pallas_call | solution.py:333
  (5 shorter events, 0.0 us)
Async XLA Ops:
  0.6 1.9 %collective-permute-start = (f32[8,2048]{1,0:T(8,128)}, f32[8,2048]{1,0:T(8,128)S(1)}, u32[]{:S(2)}, u32[]{:S(2)}) collective-permute-start(f32[8,2048]{1,0:T(8,128)} %panels.1), channel_id=1, source_target_pairs={{0,1},{1,0},{2,3},{3,2},{4,5},{5,4},{6,7},{7,6},{8,9},{9,8},{10,11... | collective-permute-start | bytes 196616 | tf_op jit(solution)/shard_map/ppermute | solution.py:349
  1.1 1.4 %collective-permute-start.1 = (s32[16,64]{1,0:T(8,128)}, s32[16,64]{1,0:T(8,128)S(1)}, u32[]{:S(2)}, u32[]{:S(2)}) collective-permute-start(s32[16,64]{1,0:T(8,128)} %near.1), channel_id=1, source_target_pairs={{0,1},{1,0},{2,3},{3,2},{4,5},{5,4},{6,7},{7,6},{8,9},{9,8},{10,11... | collective-permute-start | bytes 12296 | tf_op jit(solution)/shard_map/ppermute | solution.py:350
  1.2 0.9 %copy-start = (f32[6,4096]{1,0:T(8,128)S(1)}, f32[6,4096]{1,0:T(8,128)}, u32[]{:S(2)}) copy-start(f32[6,4096]{1,0:T(8,128)} %source.1) | copy-start | bytes 294916
  2.1 0.8 %copy-start.1 = (f32[8,2048]{1,0:T(8,128)S(1)}, f32[8,2048]{1,0:T(8,128)}, u32[]{:S(2)}) copy-start(f32[8,2048]{1,0:T(8,128)} %panels.1) | copy-start | bytes 196612
  2.2 0.8 %copy-start.2 = (s32[16,64]{1,0:T(8,128)S(1)}, s32[16,64]{1,0:T(8,128)}, u32[]{:S(2)}) copy-start(s32[16,64]{1,0:T(8,128)} %near.1) | copy-start | bytes 12292
  2.2 0.8 %copy-start.3 = (s32[32]{0:T(128)S(1)}, s32[32]{0:T(128)}, u32[]{:S(2)}) copy-start(s32[32]{0:T(128)} %param.6) | copy-start | bytes 388
  6.3 3.6 %collective-permute-start.2 = (f32[4096]{0:T(1024)S(1)}, f32[4096]{0:T(1024)S(1)}, u32[]{:S(2)}, u32[]{:S(2)}) collective-permute-start(f32[4096]{0:T(1024)S(1)} %bitcast.6), channel_id=1, source_target_pairs={{0,3},{1,2},{2,1},{3,0},{4,7},{5,6},{6,5},{7,4},{8,11},{9,10},{10,... | collective-permute-start | bytes 49160 | tf_op jit(solution)/shard_map/ppermute | solution.py:361
  9.9 4.1 %collective-permute-start.3 = (f32[4096]{0:T(1024)S(1)}, f32[4096]{0:T(1024)S(1)}, u32[]{:S(2)}, u32[]{:S(2)}) collective-permute-start(f32[4096]{0:T(1024)S(1)} %add.12), channel_id=1, source_target_pairs={{0,5},{1,4},{2,7},{3,6},{4,1},{5,0},{6,3},{7,2},{8,13},{9,12},{10,... | collective-permute-start | bytes 49160 | tf_op jit(solution)/shard_map/ppermute | solution.py:361
  14.0 4.1 %collective-permute-start.4 = (f32[4096]{0:T(1024)S(1)}, f32[4096]{0:T(1024)S(1)}, u32[]{:S(2)}, u32[]{:S(2)}) collective-permute-start(f32[4096]{0:T(1024)S(1)} %add.13), channel_id=1, source_target_pairs={{0,9},{1,8},{2,11},{3,10},{4,13},{5,12},{6,15},{7,14},{8,1},{9,0},... | collective-permute-start | bytes 49160 | tf_op jit(solution)/shard_map/ppermute | solution.py:361
  18.2 2.0 %collective-permute-start.5 = (f32[2048]{0:T(1024)S(1)}, f32[2048]{0:T(1024)S(1)}, u32[]{:S(2)}, u32[]{:S(2)}) collective-permute-start(f32[2048]{0:T(1024)S(1)} %dynamic_slice.3), channel_id=1, source_target_pairs={{0,1},{1,0},{2,3},{3,2},{4,5},{5,4},{6,7},{7,6},{8,9},{9,8},{10,11... | collective-permute-start | bytes 24584 | tf_op jit(solution)/shard_map/ppermute | solution.py:369
